TPU v7x, 32 devices: a whole 2x2x4 slice. The times are simulated.
32 devices in a mesh: seq: 8 (over z, x), trow: 2 (over core), tcol: 2 (over y).
Axes of the slice: x: 2, y: 2, z: 4, core: 2. Of those that a mesh axis runs over, the one named last changes fastest.
Arguments:
- tokens: bfloat16 [4096, 4096], P('seq', ('trow', 'tcol')), may hold values from -24 to 24
- norm_gain: float32 [4096], replicated, may hold values from 0.1 to 1.9
- in_weight: bfloat16 [3, 4096, 8192], P(None, None, ('trow', 'tcol')), may hold values from -0.09375 to 0.09375
- filter_taps: float32 [128, 8192], P(None, ('trow', 'tcol')), may hold values from -0.5 to 0.5
- conv_skip: float32 [8192], P(('trow', 'tcol')), may hold values from -1 to 1
- out_weight: bfloat16 [8192, 4096], P(('trow', 'tcol')), may hold values from -0.09375 to 0.09375
Outputs:
- mixer_out: bfloat16 [4096, 4096], P('seq', ('trow', 'tcol'))
All inputs are finite; a program needn't handle non-finite values.
Results may differ from a plain program's by a relative error of at most 0.03.
Values may be sent and summed in bfloat16 or wider, within the bound.
No kernel may reach another device: no remote copies, remote signals or barrier semaphores. Data moves between devices by JAX's collectives and lax.ppermute only.
A program may use at most 128 MiB of HBM per device.

v0:
```python
import jax
import jax.numpy as jnp
from jax import lax
from jax.sharding import PartitionSpec as P


def passed_along(block, axis, distance):
    devices = range(lax.axis_size(axis))
    route = [(i - distance, i) for i in devices if i - distance in devices]
    return lax.ppermute(block, axis, route)


def on_device(tokens, norm_gain, in_weight, filter_taps, conv_skip, out_weight):
    whole = lax.all_gather(tokens, ("trow", "tcol"), axis=1, tiled=True)
    wide = whole.astype(jnp.float32)
    mean_square = jnp.mean(wide * wide, axis=1, keepdims=True)
    normed = (wide * lax.rsqrt(mean_square + 1e-06) * norm_gain).astype(jnp.bfloat16)
    query = jnp.dot(normed, in_weight[0], preferred_element_type=jnp.float32).astype(jnp.bfloat16)
    keys = jnp.dot(normed, in_weight[1], preferred_element_type=jnp.float32).astype(jnp.bfloat16)
    values = jnp.dot(normed, in_weight[2], preferred_element_type=jnp.float32).astype(jnp.bfloat16)
    mixed = (keys.astype(jnp.float32) * values.astype(jnp.float32)).astype(jnp.bfloat16)
    taps = filter_taps.shape[0]
    rows = mixed.shape[0]
    channels = mixed.shape[1]
    tail_rows = mixed[rows - (taps - 1) :]
    previous = passed_along(tail_rows, "seq", 1)
    extended = jnp.concatenate([previous, mixed], axis=0)

    def tap_group(group, total):
        for inner in range(8):
            index = group * 8 + inner
            window = lax.dynamic_slice_in_dim(extended, taps - 1 - index, rows, 0)
            weight = lax.dynamic_slice_in_dim(filter_taps, index, 1, 0)
            total = total + window.astype(jnp.float32) * weight
        return total

    filtered = lax.fori_loop(0, taps // 8, tap_group, jnp.zeros((rows, channels), jnp.float32))
    filtered = filtered + conv_skip * mixed.astype(jnp.float32)
    gated = (query.astype(jnp.float32) * filtered).astype(jnp.bfloat16)
    partial_sum = jnp.dot(gated, out_weight, preferred_element_type=jnp.float32)
    summed = lax.psum_scatter(
        partial_sum.astype(jnp.bfloat16), ("trow", "tcol"), scatter_dimension=1, tiled=True
    )
    return summed


def solution(mesh):
    placed = (
        P("seq", ("trow", "tcol")),
        P(),
        P(None, None, ("trow", "tcol")),
        P(None, ("trow", "tcol")),
        P(("trow", "tcol")),
        P(("trow", "tcol"), None),
    )
    return jax.shard_map(
        on_device, mesh=mesh, in_specs=placed, out_specs=P("seq", ("trow", "tcol")), check_vma=False
    )
```

profile of v0, /device:TPU:0, one launch (start us, length us, event | category | flops | bytes accessed | tf_op | source)
XLA Modules:
  0.0 324.0 jit_solution(5225030279427792783)
XLA Ops:
  7.3 38.8 %all-gather.2.cloned.1.call-done = bf16[512,4096]{1,0:T(8,128)(2,1)} async-done(((bf16[512,1024]{1,0:T(8,128)(2,1)}), bf16[512,4096]{1,0:T(8,128)(2,1)}) %all-gather.2.cloned.1.call-update) | async-done | bytes 4194320 | tf_op jit(solution)/shard_map/all_gather | solution.py:14
  49.6 12.6 %fusion.22 = bf16[512,2048]{1,0:T(8,128)(2,1)S(1)} fusion(bf16[3,4096,2048]{2,1,0:T(8,128)(2,1)} %param.10, bf16[512,4096]{1,0:T(8,128)(2,1)S(1)} %copy-done, f32[4096]{0:T(1024)S(1)} %copy-done.2, f32[512]{0:T(512)S(1)} %add_rsqrt_fusion), kind=kOutput, calls=%fused_computation.34 | convolution fusion | flops 8599371776 | bytes 23087104 | tf_op jit(solution)/shard_map/dot_general | solution.py:19
  62.2 12.6 %multiply_convert_fusion.1 = bf16[512,2048]{1,0:T(8,128)(2,1)S(1)} fusion(bf16[512,2048]{1,0:T(8,128)(2,1)S(1)} %fusion.22, bf16[3,4096,2048]{2,1,0:T(8,128)(2,1)} %param.10, bf16[512,4096]{1,0:T(8,128)(2,1)S(1)} %copy-done, f32[4096]{0:T(1024)S(1)} %copy-done.2, f32[512]{0:T(512)S(1)} %add_rsqrt_fusion), kind=kOutput, calls=%fused_computation.32 | convolution fusion | flops 8603566080 | bytes 25184256 | tf_op jit(solution)/shard_map/dot_general | solution.py:20
  75.0 3.6 %collective-permute-start = (bf16[127,2048]{1,0:T(8,128)(2,1)S(1)}, bf16[127,2048]{1,0:T(8,128)(2,1)S(1)}, u32[]{:S(2)}, u32[]{:S(2)}) collective-permute-start(bf16[127,2048]{1,0:T(8,128)(2,1)S(1)} %slice.16), channel_id=1, source_target_pairs={{0,4},{4,8},{8,12},{12,16},{16,20},{20,24},{24,28},{1,5},{5,9},{9,... | collective-permute-start | bytes 1560584 | tf_op jit(solution)/shard_map/ppermute | solution.py:10
  78.6 11.3 %collective-permute-done = bf16[127,2048]{1,0:T(8,128)(2,1)S(1)} collective-permute-done((bf16[127,2048]{1,0:T(8,128)(2,1)S(1)}, bf16[127,2048]{1,0:T(8,128)(2,1)S(1)}, u32[]{:S(2)}, u32[]{:S(2)}) %collective-permute-start) | collective-permute-done | bytes 520224 | tf_op jit(solution)/shard_map/ppermute | solution.py:10
  92.2 152.7 %while.17 = (s32[]{:T(128)}, f32[512,2048]{1,0:T(8,128)}, bf16[639,2048]{1,0:T(8,128)(2,1)S(1)}, f32[128,2048]{1,0:T(8,128)}, s32[]{:T(128)}, /*index=5*/s32[]{:...) while((s32[]{:T(128)}, f32[512,2048]{1,0:T(8,128)}, ...), condition=%wide.region_2.0_spmd.clone, body=%wide.region_1.0_spmd.clone.sunk | while | flops 26214468 | bytes 25363452 | solution.py:37
  93.6 6.8 %fusion.41 = f32[512,2048]{1,0:T(8,128)} fusion(f32[512,2048]{1,0:T(8,128)} %get-tuple-element.253, f32[2048]{0:T(1024)S(1)} %bitcast.47, bf16[639,2048]{1,0:T(8,128)(2,1)S(1)} %get-tuple-element.277, s32[]{:T(128)S(6)} %select_n.216, f32[2048]{0:T(1024)S(1)} %bitcast.48, s32[]{:T(128)S(6)} %select_n.217, f32[2048]{0:T(1024)S(1)} %bitcast.49, ...), kind=kLoop, calls=%fused_computation.7.clone.1 | loop fusion | flops 26214400 | bytes 25231392 | tf_op jit(solution)/shard_map/while/body/eval_jaxpr/add | solution.py:34
  101.6 8.4 %fusion.41 = f32[512,2048]{1,0:T(8,128)} fusion(f32[512,2048]{1,0:T(8,128)} %get-tuple-element.253, f32[2048]{0:T(1024)S(1)} %bitcast.47, bf16[639,2048]{1,0:T(8,128)(2,1)S(1)} %get-tuple-element.277, s32[]{:T(128)S(6)} %select_n.216, f32[2048]{0:T(1024)S(1)} %bitcast.48, s32[]{:T(128)S(6)} %select_n.217, f32[2048]{0:T(1024)S(1)} %bitcast.49, ...), kind=kLoop, calls=%fused_computation.7.clone.1 | loop fusion | flops 26214400 | bytes 25231392 | tf_op jit(solution)/shard_map/while/body/eval_jaxpr/add | solution.py:34
  111.3 8.4 %fusion.41 = f32[512,2048]{1,0:T(8,128)} fusion(f32[512,2048]{1,0:T(8,128)} %get-tuple-element.253, f32[2048]{0:T(1024)S(1)} %bitcast.47, bf16[639,2048]{1,0:T(8,128)(2,1)S(1)} %get-tuple-element.277, s32[]{:T(128)S(6)} %select_n.216, f32[2048]{0:T(1024)S(1)} %bitcast.48, s32[]{:T(128)S(6)} %select_n.217, f32[2048]{0:T(1024)S(1)} %bitcast.49, ...), kind=kLoop, calls=%fused_computation.7.clone.1 | loop fusion | flops 26214400 | bytes 25231392 | tf_op jit(solution)/shard_map/while/body/eval_jaxpr/add | solution.py:34
  120.9 8.4 %fusion.41 = f32[512,2048]{1,0:T(8,128)} fusion(f32[512,2048]{1,0:T(8,128)} %get-tuple-element.253, f32[2048]{0:T(1024)S(1)} %bitcast.47, bf16[639,2048]{1,0:T(8,128)(2,1)S(1)} %get-tuple-element.277, s32[]{:T(128)S(6)} %select_n.216, f32[2048]{0:T(1024)S(1)} %bitcast.48, s32[]{:T(128)S(6)} %select_n.217, f32[2048]{0:T(1024)S(1)} %bitcast.49, ...), kind=kLoop, calls=%fused_computation.7.clone.1 | loop fusion | flops 26214400 | bytes 25231392 | tf_op jit(solution)/shard_map/while/body/eval_jaxpr/add | solution.py:34
  130.5 8.4 %fusion.41 = f32[512,2048]{1,0:T(8,128)} fusion(f32[512,2048]{1,0:T(8,128)} %get-tuple-element.253, f32[2048]{0:T(1024)S(1)} %bitcast.47, bf16[639,2048]{1,0:T(8,128)(2,1)S(1)} %get-tuple-element.277, s32[]{:T(128)S(6)} %select_n.216, f32[2048]{0:T(1024)S(1)} %bitcast.48, s32[]{:T(128)S(6)} %select_n.217, f32[2048]{0:T(1024)S(1)} %bitcast.49, ...), kind=kLoop, calls=%fused_computation.7.clone.1 | loop fusion | flops 26214400 | bytes 25231392 | tf_op jit(solution)/shard_map/while/body/eval_jaxpr/add | solution.py:34
  140.2 8.4 %fusion.41 = f32[512,2048]{1,0:T(8,128)} fusion(f32[512,2048]{1,0:T(8,128)} %get-tuple-element.253, f32[2048]{0:T(1024)S(1)} %bitcast.47, bf16[639,2048]{1,0:T(8,128)(2,1)S(1)} %get-tuple-element.277, s32[]{:T(128)S(6)} %select_n.216, f32[2048]{0:T(1024)S(1)} %bitcast.48, s32[]{:T(128)S(6)} %select_n.217, f32[2048]{0:T(1024)S(1)} %bitcast.49, ...), kind=kLoop, calls=%fused_computation.7.clone.1 | loop fusion | flops 26214400 | bytes 25231392 | tf_op jit(solution)/shard_map/while/body/eval_jaxpr/add | solution.py:34
  149.8 8.4 %fusion.41 = f32[512,2048]{1,0:T(8,128)} fusion(f32[512,2048]{1,0:T(8,128)} %get-tuple-element.253, f32[2048]{0:T(1024)S(1)} %bitcast.47, bf16[639,2048]{1,0:T(8,128)(2,1)S(1)} %get-tuple-element.277, s32[]{:T(128)S(6)} %select_n.216, f32[2048]{0:T(1024)S(1)} %bitcast.48, s32[]{:T(128)S(6)} %select_n.217, f32[2048]{0:T(1024)S(1)} %bitcast.49, ...), kind=kLoop, calls=%fused_computation.7.clone.1 | loop fusion | flops 26214400 | bytes 25231392 | tf_op jit(solution)/shard_map/while/body/eval_jaxpr/add | solution.py:34
  159.5 8.4 %fusion.41 = f32[512,2048]{1,0:T(8,128)} fusion(f32[512,2048]{1,0:T(8,128)} %get-tuple-element.253, f32[2048]{0:T(1024)S(1)} %bitcast.47, bf16[639,2048]{1,0:T(8,128)(2,1)S(1)} %get-tuple-element.277, s32[]{:T(128)S(6)} %select_n.216, f32[2048]{0:T(1024)S(1)} %bitcast.48, s32[]{:T(128)S(6)} %select_n.217, f32[2048]{0:T(1024)S(1)} %bitcast.49, ...), kind=kLoop, calls=%fused_computation.7.clone.1 | loop fusion | flops 26214400 | bytes 25231392 | tf_op jit(solution)/shard_map/while/body/eval_jaxpr/add | solution.py:34
  169.1 8.4 %fusion.41 = f32[512,2048]{1,0:T(8,128)} fusion(f32[512,2048]{1,0:T(8,128)} %get-tuple-element.253, f32[2048]{0:T(1024)S(1)} %bitcast.47, bf16[639,2048]{1,0:T(8,128)(2,1)S(1)} %get-tuple-element.277, s32[]{:T(128)S(6)} %select_n.216, f32[2048]{0:T(1024)S(1)} %bitcast.48, s32[]{:T(128)S(6)} %select_n.217, f32[2048]{0:T(1024)S(1)} %bitcast.49, ...), kind=kLoop, calls=%fused_computation.7.clone.1 | loop fusion | flops 26214400 | bytes 25231392 | tf_op jit(solution)/shard_map/while/body/eval_jaxpr/add | solution.py:34
  178.7 8.4 %fusion.41 = f32[512,2048]{1,0:T(8,128)} fusion(f32[512,2048]{1,0:T(8,128)} %get-tuple-element.253, f32[2048]{0:T(1024)S(1)} %bitcast.47, bf16[639,2048]{1,0:T(8,128)(2,1)S(1)} %get-tuple-element.277, s32[]{:T(128)S(6)} %select_n.216, f32[2048]{0:T(1024)S(1)} %bitcast.48, s32[]{:T(128)S(6)} %select_n.217, f32[2048]{0:T(1024)S(1)} %bitcast.49, ...), kind=kLoop, calls=%fused_computation.7.clone.1 | loop fusion | flops 26214400 | bytes 25231392 | tf_op jit(solution)/shard_map/while/body/eval_jaxpr/add | solution.py:34
  188.4 8.4 %fusion.41 = f32[512,2048]{1,0:T(8,128)} fusion(f32[512,2048]{1,0:T(8,128)} %get-tuple-element.253, f32[2048]{0:T(1024)S(1)} %bitcast.47, bf16[639,2048]{1,0:T(8,128)(2,1)S(1)} %get-tuple-element.277, s32[]{:T(128)S(6)} %select_n.216, f32[2048]{0:T(1024)S(1)} %bitcast.48, s32[]{:T(128)S(6)} %select_n.217, f32[2048]{0:T(1024)S(1)} %bitcast.49, ...), kind=kLoop, calls=%fused_computation.7.clone.1 | loop fusion | flops 26214400 | bytes 25231392 | tf_op jit(solution)/shard_map/while/body/eval_jaxpr/add | solution.py:34
  198.0 8.4 %fusion.41 = f32[512,2048]{1,0:T(8,128)} fusion(f32[512,2048]{1,0:T(8,128)} %get-tuple-element.253, f32[2048]{0:T(1024)S(1)} %bitcast.47, bf16[639,2048]{1,0:T(8,128)(2,1)S(1)} %get-tuple-element.277, s32[]{:T(128)S(6)} %select_n.216, f32[2048]{0:T(1024)S(1)} %bitcast.48, s32[]{:T(128)S(6)} %select_n.217, f32[2048]{0:T(1024)S(1)} %bitcast.49, ...), kind=kLoop, calls=%fused_computation.7.clone.1 | loop fusion | flops 26214400 | bytes 25231392 | tf_op jit(solution)/shard_map/while/body/eval_jaxpr/add | solution.py:34
  207.6 8.4 %fusion.41 = f32[512,2048]{1,0:T(8,128)} fusion(f32[512,2048]{1,0:T(8,128)} %get-tuple-element.253, f32[2048]{0:T(1024)S(1)} %bitcast.47, bf16[639,2048]{1,0:T(8,128)(2,1)S(1)} %get-tuple-element.277, s32[]{:T(128)S(6)} %select_n.216, f32[2048]{0:T(1024)S(1)} %bitcast.48, s32[]{:T(128)S(6)} %select_n.217, f32[2048]{0:T(1024)S(1)} %bitcast.49, ...), kind=kLoop, calls=%fused_computation.7.clone.1 | loop fusion | flops 26214400 | bytes 25231392 | tf_op jit(solution)/shard_map/while/body/eval_jaxpr/add | solution.py:34
  217.3 8.4 %fusion.41 = f32[512,2048]{1,0:T(8,128)} fusion(f32[512,2048]{1,0:T(8,128)} %get-tuple-element.253, f32[2048]{0:T(1024)S(1)} %bitcast.47, bf16[639,2048]{1,0:T(8,128)(2,1)S(1)} %get-tuple-element.277, s32[]{:T(128)S(6)} %select_n.216, f32[2048]{0:T(1024)S(1)} %bitcast.48, s32[]{:T(128)S(6)} %select_n.217, f32[2048]{0:T(1024)S(1)} %bitcast.49, ...), kind=kLoop, calls=%fused_computation.7.clone.1 | loop fusion | flops 26214400 | bytes 25231392 | tf_op jit(solution)/shard_map/while/body/eval_jaxpr/add | solution.py:34
  226.9 8.4 %fusion.41 = f32[512,2048]{1,0:T(8,128)} fusion(f32[512,2048]{1,0:T(8,128)} %get-tuple-element.253, f32[2048]{0:T(1024)S(1)} %bitcast.47, bf16[639,2048]{1,0:T(8,128)(2,1)S(1)} %get-tuple-element.277, s32[]{:T(128)S(6)} %select_n.216, f32[2048]{0:T(1024)S(1)} %bitcast.48, s32[]{:T(128)S(6)} %select_n.217, f32[2048]{0:T(1024)S(1)} %bitcast.49, ...), kind=kLoop, calls=%fused_computation.7.clone.1 | loop fusion | flops 26214400 | bytes 25231392 | tf_op jit(solution)/shard_map/while/body/eval_jaxpr/add | solution.py:34
  236.5 8.4 %fusion.41 = f32[512,2048]{1,0:T(8,128)} fusion(f32[512,2048]{1,0:T(8,128)} %get-tuple-element.253, f32[2048]{0:T(1024)S(1)} %bitcast.47, bf16[639,2048]{1,0:T(8,128)(2,1)S(1)} %get-tuple-element.277, s32[]{:T(128)S(6)} %select_n.216, f32[2048]{0:T(1024)S(1)} %bitcast.48, s32[]{:T(128)S(6)} %select_n.217, f32[2048]{0:T(1024)S(1)} %bitcast.49, ...), kind=kLoop, calls=%fused_computation.7.clone.1 | loop fusion | flops 26214400 | bytes 25231392 | tf_op jit(solution)/shard_map/while/body/eval_jaxpr/add | solution.py:34
  244.9 26.5 %convolution_convert_fusion = bf16[512,4096]{1,0:T(8,128)(2,1)} fusion(bf16[2048,4096]{1,0:T(8,128)(2,1)} %param.13, f32[512,2048]{1,0:T(8,128)} %get-tuple-element.156, bf16[512,2048]{1,0:T(8,128)(2,1)} %copy-done.1, bf16[3,4096,2048]{2,1,0:T(8,128)(2,1)} %param.10, f32[2048]{0:T(1024)S(1)} %copy-done.3, ...), kind=kOutput, calls=%fused_computation.30 | convolution fusion | flops 17197694976 | bytes 48261120 | tf_op jit(solution)/shard_map/dot_general | solution.py:40
  271.4 45.7 %reduce-scatter.2.cloned.1.call-done = bf16[512,1024]{1,0:T(8,128)(2,1)} async-done(((bf16[512,4096]{1,0:T(8,128)(2,1)}), bf16[512,1024]{1,0:T(8,128)(2,1)}) %reduce-scatter.2.cloned.1.call-update) | async-done | bytes 1048592 | tf_op jit(solution)/shard_map/reduce_scatter | solution.py:41
  (33 shorter events, 27.0 us)
Async XLA Ops:
  6.5 42.8 %copy-start.2 = (f32[4096]{0:T(1024)S(1)}, f32[4096]{0:T(1024)}, u32[]{:S(2)}) copy-start(f32[4096]{0:T(1024)} %param.9) | copy-start | bytes 49156
  6.5 39.6 %all-gather.2.cloned.1.call-start = ((), (), s32[]{:S(2)}) async-start(), calls=%async_computation.1 | async-start | bytes 5242880 | tf_op jit(solution)/shard_map/all_gather | solution.py:14
  7.3 309.9 %reduce-scatter.2.cloned.1.call-start = ((), (), s32[]{:S(2)}) async-start(), calls=%async_computation.2 | async-start | bytes 5242880 | tf_op jit(solution)/shard_map/reduce_scatter | solution.py:41
  46.1 3.4 %copy-start = (bf16[512,4096]{1,0:T(8,128)(2,1)S(1)}, bf16[512,4096]{1,0:T(8,128)(2,1)}, u32[]{:S(2)}) copy-start(bf16[512,4096]{1,0:T(8,128)(2,1)} %all-gather.2.cloned.1.call-done) | copy-start | bytes 12582916
  74.8 3.8 %copy-start.1 = (bf16[512,2048]{1,0:T(8,128)(2,1)}, bf16[512,2048]{1,0:T(8,128)(2,1)S(1)}, u32[]{:S(2)}) copy-start(bf16[512,2048]{1,0:T(8,128)(2,1)S(1)} %multiply_convert_fusion.1) | copy-start | bytes 6291460
  75.0 15.0 %collective-permute-start = (bf16[127,2048]{1,0:T(8,128)(2,1)S(1)}, bf16[127,2048]{1,0:T(8,128)(2,1)S(1)}, u32[]{:S(2)}, u32[]{:S(2)}) collective-permute-start(bf16[127,2048]{1,0:T(8,128)(2,1)S(1)} %slice.16), channel_id=1, source_target_pairs={{0,4},{4,8},{8,12},{12,16},{16,20},{20,24},{24,28},{1,5},{5,9},{9,... | collective-permute-start | bytes 1560584 | tf_op jit(solution)/shard_map/ppermute | solution.py:10
  92.2 152.7 %copy-start.3 = (f32[2048]{0:T(1024)S(1)}, f32[2048]{0:T(1024)}, u32[]{:S(2)}) copy-start(f32[2048]{0:T(1024)} %param.12) | copy-start | bytes 24580
Sparse Core Ops, SparseCore 0:
  8.9 37.1 all-gather.1
  271.6 45.5 reduce-scatter.1
where the time goes:
time: 325 us; the launch traced here: 324 us
  other arithmetic  138 us (42%)
  waiting for transfers between devices  96.6 us (30%)
  matrix products  51.7 us (16%)
  local copies, waits for them, and re-layouts  20.7 us (6%)
  between operations  13.5 us (4%)
  starting transfers between devices  3.64 us (1%)
    add x16, other arithmetic, tap_group(): total = total + window.astype(jnp.float32) * weight  132 us
    reduce_scatter x1, waiting for transfers between devices, on_device(): lax.psum_scatter(partial_sum.astype(jnp.bfloat16), ('trow', 'tcol'), scat...  45.7 us
    all_gather x1, waiting for transfers between devices, on_device(): whole = lax.all_gather(tokens, ('trow', 'tcol'), axis=1, tiled=True)  38.8 us
    dot_general x1, matrix products, on_device(): partial_sum = jnp.dot(gated, out_weight, preferred_element_type=jnp.float32)  26.5 us
    dynamic_slice x16, local copies, waits for them, and re-layouts, tap_group(): weight = lax.dynamic_slice_in_dim(filter_taps, index, 1, 0)  20.4 us
    dot_general x1, matrix products, on_device(): jnp.dot(normed, in_weight[2], preferred_element_type=jnp.float32)  12.6 us
    dot_general x1, matrix products, on_device(): jnp.dot(normed, in_weight[1], preferred_element_type=jnp.float32)  12.6 us
    ppermute x1, waiting for transfers between devices, passed_along(): return lax.ppermute(block, axis, route)  11.3 us
  transfers between devices with their start and end apart: 3, of which 3 were waited for; matrix products, arithmetic and copies ran while one was open for 0% of the time, Pallas kernels for 0%

commit v1 on v0

v1 whole, which is shorter than its diff:
```python
import functools

import jax
import jax.numpy as jnp
import numpy as np
from jax import lax
from jax.experimental import pallas as pl
from jax.experimental.pallas import tpu as pltpu
from jax.sharding import PartitionSpec as P

BF16 = jnp.bfloat16
F32 = jnp.float32
MIB = 1024 * 1024


def dft_matrices(taps):
    size = 2 * taps
    t = np.arange(size)[None, :]
    k = np.arange(taps)[:, None]
    angle = 2.0 * np.pi * ((k * t) % size) / size
    cos, sin = np.cos(angle), np.sin(angle)
    alternating = (-1.0) ** t
    forward = np.concatenate([cos, alternating, -sin[1:]], axis=0)
    inverse = np.concatenate([cos[:1], 2.0 * cos[1:], alternating, -2.0 * sin[1:]], axis=0).T / size
    short = slice(0, taps)
    of_filter = np.concatenate(
        [cos[:, short], 0.0 * sin[:1, short], -sin[1:, short], alternating[:, short], cos[1:, short]], axis=0
    )
    of_filter = np.concatenate([of_filter, of_filter], axis=1)
    return forward.astype(BF16), inverse[taps:].astype(BF16), of_filter.astype(BF16)


def dot(a, b):
    return jnp.dot(a, b, preferred_element_type=F32)


def spectrum_kernel(taps_ref, skip_ref, of_filter_ref, spec_ref):
    h = taps_ref[...]
    first = lax.broadcasted_iota(jnp.int32, h.shape, 0) == 0
    h = h + jnp.where(first, skip_ref[...], 0.0)
    high = h.astype(BF16)
    low = (h - high.astype(F32)).astype(BF16)
    spec_ref[...] = dot(of_filter_ref[...], jnp.concatenate([high, low], axis=0))


def convolved(window, spectrum, forward, inverse):
    half = window.shape[0] // 2
    x = dot(forward, window)
    xa, xb = x[:half], x[half:]
    ha, hb, hc = spectrum[:half], spectrum[half : 2 * half], spectrum[2 * half :]
    y = jnp.concatenate([xa * ha - xb * hb, xa * hb + xb * hc], axis=0)
    return dot(inverse, y.astype(BF16))


def scaled_inputs(lhs_refs, gain_refs, xg_ref):
    total = jnp.zeros((xg_ref.shape[1], 1), F32)
    for i, (x_ref, g_ref) in enumerate(zip(lhs_refs, gain_refs)):
        x = x_ref[...].astype(F32)
        total = total + jnp.sum(x * x, axis=1, keepdims=True)
        xg_ref[i] = (x * g_ref[0]).astype(BF16)
    return jnp.broadcast_to(total, (xg_ref.shape[1], 128))


def columns(step, ct):
    return pl.ds(pl.multiple_of(step * ct, ct), ct)


def local_kernel(n_lhs, blocks_ref, *refs):
    lhs, gains, weights = refs[:n_lhs], refs[n_lhs : 2 * n_lhs], refs[2 * n_lhs : 3 * n_lhs]
    acc_ref, ssq_ref, xg_ref = refs[-3:]
    step = pl.program_id(0)

    @pl.when(step == 0)
    def _():
        ssq_ref[...] = scaled_inputs(lhs, gains, xg_ref)

    at = columns(step, weights[0].shape[2])
    for j in range(3):
        acc = dot(xg_ref[0], weights[0][j])
        for i in range(1, n_lhs):
            acc = acc + dot(xg_ref[i], weights[i][j])
        acc_ref[j, :, at] = acc


def streams(n_lhs, d_model, rows, at, lhs, gains, weights, acc_ref, ssq_ref, xg_ref, own_ssq_ref):
    @pl.when(pl.program_id(0) == 0)
    def _():
        own_ssq_ref[...] = scaled_inputs(lhs, gains, xg_ref)

    scale = lax.rsqrt((ssq_ref[rows, :1] + own_ssq_ref[:, :1]) / d_model + 1e-06)
    out = []
    for j in range(3):
        acc = acc_ref[j, rows, at]
        for i in range(n_lhs):
            acc = acc + dot(xg_ref[i], weights[i][j])
        out.append((acc * scale).astype(BF16))
    query, keys, values = out
    mixed = (keys.astype(F32) * values.astype(F32)).astype(BF16)
    return query, mixed


def gate(query, mixed, b, at, spec_ref, fwd_ref, inv_ref, taps):
    filtered = convolved(mixed[(b - 1) * taps : (b + 1) * taps], spec_ref[:, at], fwd_ref[...], inv_ref[...])
    return (query[b * taps : (b + 1) * taps].astype(F32) * filtered).astype(BF16)


def upper_kernel(n_lhs, d_model, taps, blocks_ref, *refs):
    lhs, gains, weights = refs[:n_lhs], refs[n_lhs : 2 * n_lhs], refs[2 * n_lhs : 3 * n_lhs]
    acc_ref, ssq_ref, spec_ref, fwd_ref, inv_ref = refs[3 * n_lhs : 3 * n_lhs + 5]
    tail_ref, q_ref, mixed_ref, gated_ref, xg_ref, own_ssq_ref = refs[-6:]
    at = columns(pl.program_id(0), weights[0].shape[2])
    rows = slice(2 * taps, 4 * taps)
    query, mixed = streams(n_lhs, d_model, rows, at, lhs, gains, weights, acc_ref, ssq_ref, xg_ref, own_ssq_ref)
    tail_ref[...] = mixed[taps:]
    q_ref[:, at] = query[:taps]
    mixed_ref[:, at] = mixed[:taps]
    gated_ref[:, at] = gate(query, mixed, 1, at, spec_ref, fwd_ref, inv_ref, taps)


def lower_kernel(n_lhs, d_model, taps, blocks_ref, *refs):
    lhs, gains, weights = refs[:n_lhs], refs[n_lhs : 2 * n_lhs], refs[2 * n_lhs : 3 * n_lhs]
    acc_ref, ssq_ref, spec_ref, fwd_ref, inv_ref, q_up_ref, mixed_up_ref = refs[3 * n_lhs : 3 * n_lhs + 7]
    q_ref, mixed_ref, one_ref, two_ref, xg_ref, own_ssq_ref = refs[-6:]
    at = columns(pl.program_id(0), weights[0].shape[2])
    rows = slice(0, 2 * taps)
    query, mixed = streams(n_lhs, d_model, rows, at, lhs, gains, weights, acc_ref, ssq_ref, xg_ref, own_ssq_ref)
    q_ref[:, at] = query[:taps]
    mixed_ref[:, at] = mixed[:taps]
    mixed = jnp.concatenate([mixed, mixed_up_ref[:, at]], axis=0)
    query = jnp.concatenate([query, q_up_ref[:, at]], axis=0)
    one_ref[:, at] = gate(query, mixed, 1, at, spec_ref, fwd_ref, inv_ref, taps)
    two_ref[:, at] = gate(query, mixed, 2, at, spec_ref, fwd_ref, inv_ref, taps)


def first_kernel(halo_ref, mixed_ref, q_ref, spec_ref, fwd_ref, inv_ref, gated_ref):
    ct = column_tile(q_ref.shape[1])
    for at in range(0, q_ref.shape[1], ct):
        at = slice(at, at + ct)
        window = jnp.concatenate([halo_ref[:, at], mixed_ref[:, at]], axis=0)
        filtered = convolved(window, spec_ref[:, at], fwd_ref[...], inv_ref[...])
        gated_ref[:, at] = (q_ref[:, at].astype(F32) * filtered).astype(BF16)


def params(mib, steps=1):
    return pltpu.CompilerParams(dimension_semantics=("arbitrary",) * steps, vmem_limit_bytes=mib * MIB)


def in_hbm(x):
    return pltpu.with_memory_space_constraint(x, pltpu.HBM)


def in_vmem(x):
    return pltpu.with_memory_space_constraint(x, pltpu.VMEM)


RESIDENT = pl.BlockSpec(memory_space=pltpu.VMEM)


def whole(shape):
    return pl.BlockSpec(shape, lambda ch, *_: (0,) * len(shape))


def lhs_specs(lhs, first, norm_gain, in_weight, ct):
    rows, depth = lhs[0].shape
    n = len(lhs)
    gain = norm_gain.reshape(-1, 1, depth)
    specs = [whole((rows, depth))] * n
    specs += [pl.BlockSpec((1, 1, depth), lambda ch, b, i=i: (b[first + i], 0, 0)) for i in range(n)]
    specs += [pl.BlockSpec((3, depth, ct), lambda ch, b, i=i: (0, b[first + i], ch)) for i in range(n)]
    scratch = [pltpu.VMEM((n, rows, depth), BF16)]
    return specs, scratch, [in_hbm(x) for x in lhs] + [gain] * n + [in_hbm(in_weight)] * n


def cost(rows, depth, width, extra=0):
    return pl.CostEstimate(
        flops=2 * rows * depth * width, bytes_accessed=2 * (rows * depth + depth * width) + extra, transcendentals=0
    )


def column_tile(channels, most=256):
    return most if channels % most == 0 else channels


def nothing_kernel(*refs):
    pass


def held_until(x, *others):
    return pl.pallas_call(
        nothing_kernel,
        in_specs=[pl.BlockSpec(memory_space=pl.ANY)] * (1 + len(others)),
        out_specs=pl.BlockSpec(memory_space=pl.ANY),
        out_shape=jax.ShapeDtypeStruct(x.shape, x.dtype),
        input_output_aliases={0: 0},
        compiler_params=pltpu.CompilerParams(vmem_limit_bytes=MIB),
        name="held_until",
    )(x, *others)


def filter_transform(filter_taps, conv_skip, of_filter):
    taps, channels = filter_taps.shape
    ct = column_tile(channels, 1024)
    tile = lambda r: pl.BlockSpec((r, ct), lambda ch: (0, ch))
    return pl.pallas_call(
        spectrum_kernel,
        grid=(channels // ct,),
        in_specs=[tile(taps), tile(1), whole(of_filter.shape)],
        out_specs=tile(3 * taps),
        out_shape=pltpu.VMEM((3 * taps, channels), F32),
        compiler_params=params(10),
        cost_estimate=cost(3 * taps, 2 * taps, channels),
        name="filter_transform",
    )(in_hbm(filter_taps), conv_skip.reshape(1, -1), of_filter)


def project_local(lhs, places, first, norm_gain, in_weight, waits):
    rows, depth = lhs[0].shape
    channels = in_weight.shape[2]
    ct = column_tile(channels)
    specs, scratch, operands = lhs_specs(lhs, first, norm_gain, in_weight, ct)
    return pl.pallas_call(
        functools.partial(local_kernel, len(lhs)),
        grid_spec=pltpu.PrefetchScalarGridSpec(
            num_scalar_prefetch=1,
            grid=(channels // ct,),
            in_specs=specs + [pl.BlockSpec(memory_space=pl.ANY)] * len(waits),
            out_specs=[RESIDENT, RESIDENT],
            scratch_shapes=scratch,
        ),
        out_shape=[pltpu.VMEM((3, rows, channels), F32), pltpu.VMEM((rows, 128), F32)],
        compiler_params=params(18),
        cost_estimate=cost(rows, depth * len(lhs), 3 * channels),
        name="project_local",
    )(places, *operands, *waits)


def project_rest(kernel, name, lhs, places, first, norm_gain, in_weight, resident, waits, outs, tiled, d_model, taps):
    rows, depth = lhs[0].shape
    channels = in_weight.shape[2]
    ct = column_tile(channels)
    specs, scratch, operands = lhs_specs(lhs, first, norm_gain, in_weight, ct)
    return pl.pallas_call(
        functools.partial(kernel, len(lhs), d_model, taps),
        grid_spec=pltpu.PrefetchScalarGridSpec(
            num_scalar_prefetch=1,
            grid=(channels // ct,),
            in_specs=specs + [RESIDENT] * len(resident) + [pl.BlockSpec(memory_space=pl.ANY)] * len(waits),
            out_specs=[pl.BlockSpec((taps, ct), lambda ch, b: (0, ch))] * tiled + [RESIDENT] * outs,
            scratch_shapes=scratch + [pltpu.VMEM((rows, 128), F32)],
        ),
        out_shape=[jax.ShapeDtypeStruct((taps, channels), BF16)] * tiled + [pltpu.VMEM((taps, channels), BF16)] * outs,
        compiler_params=params(18),
        cost_estimate=cost(rows, depth * len(lhs), 3 * channels),
        name=name,
    )(places, *operands, *[in_vmem(x) for x in resident], *waits)


def gate_first(halo, mixed, query, spectrum, forward, inverse):
    taps, channels = mixed.shape
    return pl.pallas_call(
        first_kernel,
        in_specs=[RESIDENT] * 6,
        out_specs=RESIDENT,
        out_shape=pltpu.VMEM((taps, channels), BF16),
        compiler_params=pltpu.CompilerParams(vmem_limit_bytes=8 * MIB),
        cost_estimate=cost(3 * taps, 2 * taps, channels),
        name="gate_first",
    )(in_hbm(halo), *[in_vmem(x) for x in (mixed, query, spectrum, forward, inverse)])


def out_kernel(n_parts, first, n_groups, has_add, groups_ref, *refs):
    parts, w_ref = refs[:n_parts], refs[n_parts]
    o_ref = refs[-1]
    width = o_ref.shape[2]
    lhs = jnp.concatenate([p[...] for p in parts], axis=0)
    for g in range(n_groups):
        at = pl.ds(pl.multiple_of(groups_ref[first + g] * width, width), width)
        product = dot(lhs, w_ref[:, at])
        if has_add:
            product = product + refs[n_parts + 1][g].astype(F32)
        o_ref[g] = product.astype(o_ref.dtype)


def project_out(parts, out_weight, places, first, n_groups, width, add, dtype, name):
    rows = sum(p.shape[0] for p in parts)
    channels = out_weight.shape[0]
    return pl.pallas_call(
        functools.partial(out_kernel, len(parts), first, n_groups, add is not None),
        in_specs=[pl.BlockSpec(memory_space=pltpu.SMEM)] + [RESIDENT] * (len(parts) + 1 + (add is not None)),
        out_specs=RESIDENT,
        out_shape=jax.ShapeDtypeStruct((n_groups, rows, width), dtype),
        compiler_params=pltpu.CompilerParams(vmem_limit_bytes=10 * MIB),
        cost_estimate=cost(rows, channels, n_groups * width),
        name=name,
    )(places, *[in_vmem(p) for p in parts], in_vmem(out_weight), *([add] if add is not None else []))


def finish_kernel(n_come, *refs):
    total = refs[0][0]
    for x in refs[1 : 1 + n_come]:
        total = total + x[...].astype(F32)
    refs[-1][...] = total.astype(refs[-1].dtype)


def finish(near, come, into, part, parts):
    rows, width = near.shape[1:]
    operands = [near, *come] + ([into] if into is not None else [])
    return pl.pallas_call(
        functools.partial(finish_kernel, len(come)),
        grid=(1,),
        in_specs=[pl.BlockSpec((1, rows, width), lambda i: (0, 0, 0))]
        + [pl.BlockSpec((rows, width), lambda i: (0, 0))] * len(come)
        + ([pl.BlockSpec(memory_space=pl.ANY)] if into is not None else []),
        out_specs=pl.BlockSpec((rows, width), lambda i: (part, 0)),
        out_shape=jax.ShapeDtypeStruct((rows * parts, width), BF16),
        input_output_aliases={len(operands) - 1: 0} if into is not None else {},
        compiler_params=params(8),
        name="finish",
    )(*operands)


def on_device(tokens, norm_gain, in_weight, filter_taps, conv_skip, out_weight):
    n_row, n_col, n_seq = lax.axis_size("trow"), lax.axis_size("tcol"), lax.axis_size("seq")
    r, c = lax.axis_index("trow"), lax.axis_index("tcol")
    rows, depth = tokens.shape
    taps = filter_taps.shape[0]
    half = 2 * taps
    d_model = depth * n_row * n_col
    assert n_row == 2 and rows == 2 * half
    forward, inverse, of_filter = (jnp.asarray(m) for m in dft_matrices(taps))

    def other_core(x):
        return lax.ppermute(x, "trow", [(0, 1), (1, 0)])

    def chips_along(x, s):
        return lax.ppermute(x, "tcol", [(i, (i + s) % n_col) for i in range(n_col)])

    def block_of(row, s):
        return row * n_col + lax.rem(c + s + n_col, n_col)

    beside = other_core(tokens)
    upper_far = [chips_along(tokens[half:], s) for s in range(1, n_col)]
    lower_far = [chips_along(tokens[:half], s) for s in range(1, n_col)]
    shifts = range(1, n_col)
    places = jnp.stack(
        [block_of(r, 0), block_of(1 - r, 0)]
        + [block_of(row, -s) for row in (r, 1 - r) for s in shifts]
        + [block_of(row, s) for row in (1 - r, r) for s in shifts]
        + [block_of(1 - r, 0), block_of(r, 0)]
    )
    far_features, theirs_far = 2, 2 * n_col
    mine_far = theirs_far + n_col - 1
    theirs_near, mine_near = mine_far + n_col - 1, mine_far + n_col
    spectrum = filter_transform(filter_taps, conv_skip, of_filter)
    acc, ssq = project_local([tokens, beside], places, 0, norm_gain, in_weight, [spectrum])
    rest = functools.partial(project_rest, places=places, first=far_features, norm_gain=norm_gain, in_weight=in_weight, d_model=d_model, taps=taps)
    upper_far = [held_until(x, ssq) for x in upper_far]
    lower_far = [held_until(x, ssq) for x in lower_far]
    resident = [acc, ssq, spectrum, forward, inverse]
    upper = upper_far + [other_core(x) for x in upper_far]
    tail, q_up, mixed_up, gated_up = rest(
        upper_kernel, "project_upper", upper, resident=resident, waits=lower_far, outs=3, tiled=1
    )
    halo = lax.ppermute(tail, "seq", [(i, i + 1) for i in range(n_seq - 1)])
    lower = lower_far + [other_core(x) for x in lower_far]
    q_low, mixed_low, gated_one, gated_two = rest(
        lower_kernel, "project_lower", lower, resident=resident + [q_up, mixed_up], waits=[], outs=4, tiled=0
    )

    def out_rows(parts, name):
        project = functools.partial(project_out, parts, out_weight, places)
        far = other_core(project(theirs_far, n_col - 1, depth, None, BF16, name + "_theirs_far"))
        near = other_core(project(theirs_near, 1, depth, None, BF16, name + "_theirs_near"))
        sent = project(mine_far, n_col - 1, depth, far, BF16, name + "_mine_far")
        come = [chips_along(sent[s - 1], s) for s in range(1, n_col)]
        return project(mine_near, 1, depth, near, F32, name + "_mine_near"), come, sent

    near_up, come_up, sent_up = out_rows([gated_two, gated_up], "out_up")
    gated_first = gate_first(halo, mixed_low, q_low, spectrum, forward, inverse)
    near_low, come_low, _ = out_rows([gated_first, gated_one], "out_low")
    out = finish(near_up, come_up, None, 1, 2)
    return finish(near_low, come_low, out, 0, 2)


def solution(mesh):
    placed = (
        P("seq", ("trow", "tcol")),
        P(),
        P(None, None, ("trow", "tcol")),
        P(None, ("trow", "tcol")),
        P(("trow", "tcol")),
        P(("trow", "tcol"), None),
    )
    return jax.shard_map(
        on_device, mesh=mesh, in_specs=placed, out_specs=P("seq", ("trow", "tcol")), check_vma=False
    )
```

time: 325 us -> 110 us (0.34)
  other arithmetic: 138 us -> 0.01 us
  waiting for transfers between devices: 96.6 us -> 16.5 us
  Pallas kernels: 0 us -> 74.8 us
  matrix products: 51.7 us -> 0 us
  local copies, waits for them, and re-layouts: 20.7 us -> 7.06 us
  between operations: 13.5 us -> 0.27 us
  starting transfers between devices: 3.64 us -> 10.9 us
    add x16 -> x0, other arithmetic: 132 us -> none  [tap_group(): total = total + window.astype(jnp.float32) * weight]
    pallas_call x0 -> x17, Pallas kernels: none -> 74.8 us  [the longest x2 34.8 us: project_rest(): pl.pallas_call(functools.partial(kernel, len(lhs), d_model, taps), grid_s...]
    dot_general x3 -> x0, matrix products: 51.7 us -> none  [the longest x1 26.5 us: on_device(): partial_sum = jnp.dot(gated, out_weight, preferred_element_type=jnp.float32)]
    reduce_scatter x1 -> x0, waiting for transfers between devices: 45.7 us -> none  [on_device(): lax.psum_scatter(partial_sum.astype(jnp.bfloat16), ('trow', 'tcol'), scat...]
    all_gather x1 -> x0, waiting for transfers between devices: 38.8 us -> none  [on_device(): whole = lax.all_gather(tokens, ('trow', 'tcol'), axis=1, tiled=True)]
    dynamic_slice x16 -> x0, local copies, waits for them, and re-layouts: 20.4 us -> none  [tap_group(): weight = lax.dynamic_slice_in_dim(filter_taps, index, 1, 0)]
    ppermute x1 -> x12, starting transfers between devices: 3.6 us -> 10.9 us  [the longest x4 4.82 us: chips_along(): return lax.ppermute(x, 'tcol', [(i, (i + s) % n_col) for i in range(n_col)])]
    unnamed x8 -> x30, local copies, waits for them, and re-layouts: 0.21 us -> 5.71 us
  transfers between devices with their start and end apart: 3 -> 12, of which waited for: 3 -> 3; matrix products, arithmetic and copies ran while one was open for 0% -> 1% of each run, Pallas kernels for 0% -> 68%
where the time goes in v1:
time: 110 us; the launch traced here: 109 us
  Pallas kernels  74.8 us (68%)
  waiting for transfers between devices  16.5 us (15%)
  starting transfers between devices  10.9 us (10%)
  local copies, waits for them, and re-layouts  7.06 us (6%)
    pallas_call x2, Pallas kernels, project_rest(): pl.pallas_call(functools.partial(kernel, len(lhs), d_model, taps), grid_s...  34.8 us
    pallas_call x1, Pallas kernels, project_local(): pl.pallas_call(functools.partial(local_kernel, len(lhs)), grid_spec=pltpu...  18.7 us
    ppermute x4, waiting for transfers between devices, chips_along(): return lax.ppermute(x, 'tcol', [(i, (i + s) % n_col) for i in range(n_col)])  15 us
    pallas_call x8, Pallas kernels, project_out(): pl.pallas_call(functools.partial(out_kernel, len(parts), first, n_groups,...  14.5 us
    unnamed x30, local copies, waits for them, and re-layouts  5.71 us
    ppermute x4, starting transfers between devices, chips_along(): return lax.ppermute(x, 'tcol', [(i, (i + s) % n_col) for i in range(n_col)])  4.82 us
    ppermute x1, starting transfers between devices, on_device(): halo = lax.ppermute(tail, 'seq', [(i, i + 1) for i in range(n_seq - 1)])  4.04 us
    pallas_call x1, Pallas kernels, gate_first(): pl.pallas_call(first_kernel, in_specs=[RESIDENT] * 6, out_specs=RESIDENT,...  3.1 us
  transfers between devices with their start and end apart: 12, of which 3 were waited for; matrix products, arithmetic and copies ran while one was open for 1% of the time, Pallas kernels for 68%

profile of v1, /device:TPU:0, one launch (start us, length us, event | category | flops | bytes accessed | tf_op | source)
XLA Modules:
  0.0 109.4 jit_solution(15425246719489255524)
XLA Ops:
  0.5 1.3 %fusion = (bf16[256,1024]{1,0:T(8,128)(2,1)S(1)}, bf16[256,1024]{1,0:T(8,128)(2,1)S(1)}) fusion(bf16[512,1024]{1,0:T(8,128)(2,1)} %refs_0_.1), kind=kLoop, calls=%fused_computation | loop fusion | bytes 2097152 | tf_op jit(solution)/shard_map/slice | solution.py:343
  1.7 2.6 %collective-permute-start.3 = (bf16[256,1024]{1,0:T(8,128)(2,1)S(1)}, bf16[256,1024]{1,0:T(8,128)(2,1)S(1)}, u32[]{:S(2)}, u32[]{:S(2)}) collective-permute-start(bf16[256,1024]{1,0:T(8,128)(2,1)S(1)} %get-tuple-element.25), channel_id=1, source_target_pairs={{0,1},{1,0},{2,3},{3,2},{4,5},{5,4},{6,7},{7,6},{8,9},{9,8},{10,11... | collective-permute-start | bytes 1572872 | tf_op jit(solution)/shard_map/ppermute | solution.py:336
  4.5 0.9 copy-done.5
  6.1 2.0 %filter_transform.1.refs_6_.refs_8_.spec_ref = f32[384,2048]{1,0:T(8,128)S(1)} custom-call(f32[128,2048]{1,0:T(8,128)} %taps_ref.1, f32[1,2048]{1,0:T(1,128)S(1)} %bitcast.20, bf16[384,256]{1,0:T(8,128)(2,1)S(1)} %copy-done.5), custom_call_target="tpu_custom_call" | custom-call | flops 402653184 | bytes 1245184 | tf_op jit(solution)/shard_map/filter_transform/pallas_call | solution.py:204
  8.1 1.0 copy-done.7
  9.8 18.7 %project_local.1 = (f32[3,512,2048]{2,1,0:T(8,128)S(1)}, f32[512,128]{1,0:T(8,128)S(1)}) custom-call(s32[8]{0:T(128)S(1)} %stack.29.blocks_ref.groups_ref, bf16[512,1024]{1,0:T(8,128)(2,1)} %refs_0_.1, bf16[512,1024]{1,0:T(8,128)(2,1)} %copy-done.7, f32[4,1,1024]{2,1,0:T(1,128)S(1)} %bitcast.12, f32[4,1,1024]{2,1,0:T(1,128)S(1)} %bitcast.13, ...), custom_call_target="tpu_custom_call" | custom-call | flops 12884901888 | bytes 27262976 | tf_op jit(solution)/shard_map/project_local/pallas_call | solution.py:221
  29.1 1.4 %collective-permute-done.2.refs_1_ = bf16[256,1024]{1,0:T(8,128)(2,1)S(1)} collective-permute-done((bf16[256,1024]{1,0:T(8,128)(2,1)S(1)}, bf16[256,1024]{1,0:T(8,128)(2,1)S(1)}, u32[]{:S(2)}, u32[]{:S(2)}) %collective-permute-start.2) | collective-permute-done | bytes 524320 | tf_op jit(solution)/shard_map/ppermute | solution.py:333
  31.3 16.8 %project_upper.1 = (bf16[128,2048]{1,0:T(8,128)(2,1)S(1)}, bf16[128,2048]{1,0:T(8,128)(2,1)S(1)}, bf16[128,2048]{1,0:T(8,128)(2,1)S(1)}, bf16[128,2048]{1,0:T(8,128)(2,1)S(1)}) custom-call(s32[8]{0:T(128)S(1)} %stack.29.blocks_ref.groups_ref, bf16[256,1024]{1,0:T(8,128)(2,1)} %copy-done.1, bf16[256,1024]{1,0:T(8,128)(2,1)} %copy-done.9, ...), custom_call_target="tpu_custom_call" | custom-call | flops 6442450944 | bytes 26214400 | tf_op jit(solution)/shard_map/project_upper/pallas_call | solution.py:242
  48.2 4.0 %collective-permute-start.4 = (bf16[128,2048]{1,0:T(8,128)(2,1)S(1)}, bf16[128,2048]{1,0:T(8,128)(2,1)S(1)}, u32[]{:S(2)}, u32[]{:S(2)}) collective-permute-start(bf16[128,2048]{1,0:T(8,128)(2,1)S(1)} %get-tuple-element.17), channel_id=1, source_target_pairs={{0,4},{4,8},{8,12},{12,16},{16,20},{20,24},{24,28},{1,5},{5,9},{9,... | collective-permute-start | bytes 1572872 | tf_op jit(solution)/shard_map/ppermute | solution.py:364
  53.0 18.0 %project_lower.1 = (bf16[128,2048]{1,0:T(8,128)(2,1)S(1)}, bf16[128,2048]{1,0:T(8,128)(2,1)S(1)}, bf16[128,2048]{1,0:T(8,128)(2,1)S(1)}, bf16[128,2048]{1,0:T(8,128)(2,1)S(1)}) custom-call(s32[8]{0:T(128)S(1)} %stack.29.blocks_ref.groups_ref, bf16[256,1024]{1,0:T(8,128)(2,1)} %copy-done, bf16[256,1024]{1,0:T(8,128)(2,1)} %copy-done.8, ...), custom_call_target="tpu_custom_call" | custom-call | flops 6442450944 | bytes 26214400 | tf_op jit(solution)/shard_map/project_lower/pallas_call | solution.py:242
  71.0 1.8 %out_up_theirs_far.1 = bf16[1,256,1024]{2,1,0:T(8,128)(2,1)S(1)} custom-call(s32[8]{0:T(128)S(1)} %stack.29.blocks_ref.groups_ref, bf16[128,2048]{1,0:T(8,128)(2,1)S(1)} %get-tuple-element.23.refs_0_, bf16[128,2048]{1,0:T(8,128)(2,1)S(1)} %get-tuple-element.24.refs_1_, bf16[2048,4096]{1,0:T(8,128)(2,1)S(1)} %bitcast.11), custom_call_target="tpu_custom_call" | custom-call | flops 1073741824 | bytes 5242880 | tf_op jit(solution)/shard_map/out_up_theirs_far/pallas_call | solution.py:287
  73.7 3.1 %gate_first.1.refs_0_ = bf16[128,2048]{1,0:T(8,128)(2,1)S(1)} custom-call(bf16[128,2048]{1,0:T(8,128)(2,1)} %copy-done.10, bf16[128,2048]{1,0:T(8,128)(2,1)S(1)} %get-tuple-element.20.mixed_ref, bf16[128,2048]{1,0:T(8,128)(2,1)S(1)} %get-tuple-element.21.q_ref, f32[384,2048]{1,0:T(8,128)S(1)} %filter_transform.1.refs_6_.refs_8_.spec_ref, ...), custom_call_target="tpu_custom_call" | custom-call | flops 402653184 | bytes 1245184 | tf_op jit(solution)/shard_map/gate_first/pallas_call | solution.py:260
  76.8 1.8 %out_low_theirs_far.1 = bf16[1,256,1024]{2,1,0:T(8,128)(2,1)S(1)} custom-call(s32[8]{0:T(128)S(1)} %stack.29.blocks_ref.groups_ref, bf16[128,2048]{1,0:T(8,128)(2,1)S(1)} %gate_first.1.refs_0_, bf16[128,2048]{1,0:T(8,128)(2,1)S(1)} %get-tuple-element.22.refs_1_, bf16[2048,4096]{1,0:T(8,128)(2,1)S(1)} %bitcast.11), custom_call_target="tpu_custom_call" | custom-call | flops 1073741824 | bytes 5242880 | tf_op jit(solution)/shard_map/out_low_theirs_far/pallas_call | solution.py:287
  79.2 1.8 %out_up_theirs_near.1 = bf16[1,256,1024]{2,1,0:T(8,128)(2,1)S(1)} custom-call(s32[8]{0:T(128)S(1)} %stack.29.blocks_ref.groups_ref, bf16[128,2048]{1,0:T(8,128)(2,1)S(1)} %get-tuple-element.23.refs_0_, bf16[128,2048]{1,0:T(8,128)(2,1)S(1)} %get-tuple-element.24.refs_1_, bf16[2048,4096]{1,0:T(8,128)(2,1)S(1)} %bitcast.11), custom_call_target="tpu_custom_call" | custom-call | flops 1073741824 | bytes 5242880 | tf_op jit(solution)/shard_map/out_up_theirs_near/pallas_call | solution.py:287
  81.1 1.8 %out_up_mine_far.1 = bf16[1,256,1024]{2,1,0:T(8,128)(2,1)S(1)} custom-call(s32[8]{0:T(128)S(1)} %stack.29.blocks_ref.groups_ref, bf16[128,2048]{1,0:T(8,128)(2,1)S(1)} %get-tuple-element.23.refs_0_, bf16[128,2048]{1,0:T(8,128)(2,1)S(1)} %get-tuple-element.24.refs_1_, bf16[2048,4096]{1,0:T(8,128)(2,1)S(1)} %bitcast.11, ...), custom_call_target="tpu_custom_call" | custom-call | flops 1073741824 | bytes 5242880 | tf_op jit(solution)/shard_map/out_up_mine_far/pallas_call | solution.py:287
  82.9 1.6 %collective-permute-start.11 = (bf16[256,1024]{1,0:T(8,128)(2,1)S(1)}, bf16[256,1024]{1,0:T(8,128)(2,1)S(1)}, u32[]{:S(2)}, u32[]{:S(2)}) collective-permute-start(bf16[256,1024]{1,0:T(8,128)(2,1)S(1)} %bitcast.19), channel_id=1, source_target_pairs={{0,1},{1,0},{2,3},{3,2},{4,5},{5,4},{6,7},{7,6},{8,9},{9,8},{10,11... | collective-permute-start | bytes 1572872 | tf_op jit(solution)/shard_map/ppermute | solution.py:336
  84.5 1.8 %out_low_theirs_near.1 = bf16[1,256,1024]{2,1,0:T(8,128)(2,1)S(1)} custom-call(s32[8]{0:T(128)S(1)} %stack.29.blocks_ref.groups_ref, bf16[128,2048]{1,0:T(8,128)(2,1)S(1)} %gate_first.1.refs_0_, bf16[128,2048]{1,0:T(8,128)(2,1)S(1)} %get-tuple-element.22.refs_1_, bf16[2048,4096]{1,0:T(8,128)(2,1)S(1)} %bitcast.11), custom_call_target="tpu_custom_call" | custom-call | flops 1073741824 | bytes 5242880 | tf_op jit(solution)/shard_map/out_low_theirs_near/pallas_call | solution.py:287
  86.6 1.8 %out_low_mine_far.1 = bf16[1,256,1024]{2,1,0:T(8,128)(2,1)S(1)} custom-call(s32[8]{0:T(128)S(1)} %stack.29.blocks_ref.groups_ref, bf16[128,2048]{1,0:T(8,128)(2,1)S(1)} %gate_first.1.refs_0_, bf16[128,2048]{1,0:T(8,128)(2,1)S(1)} %get-tuple-element.22.refs_1_, bf16[2048,4096]{1,0:T(8,128)(2,1)S(1)} %bitcast.11, ...), custom_call_target="tpu_custom_call" | custom-call | flops 1073741824 | bytes 5242880 | tf_op jit(solution)/shard_map/out_low_mine_far/pallas_call | solution.py:287
  89.0 1.8 %out_up_mine_near.1.refs_0_ = f32[1,256,1024]{2,1,0:T(8,128)S(1)} custom-call(s32[8]{0:T(128)S(1)} %stack.29.blocks_ref.groups_ref, bf16[128,2048]{1,0:T(8,128)(2,1)S(1)} %get-tuple-element.23.refs_0_, bf16[128,2048]{1,0:T(8,128)(2,1)S(1)} %get-tuple-element.24.refs_1_, bf16[2048,4096]{1,0:T(8,128)(2,1)S(1)} %bitcast.11, ...), custom_call_target="tpu_custom_call" | custom-call | flops 1073741824 | bytes 5242880 | tf_op jit(solution)/shard_map/out_up_mine_near/pallas_call | solution.py:287
  90.8 6.9 %collective-permute-done.11.refs_1_ = bf16[256,1024]{1,0:T(8,128)(2,1)S(1)} collective-permute-done((bf16[256,1024]{1,0:T(8,128)(2,1)S(1)}, bf16[256,1024]{1,0:T(8,128)(2,1)S(1)}, u32[]{:S(2)}, u32[]{:S(2)}) %collective-permute-start.11) | collective-permute-done | bytes 524320 | tf_op jit(solution)/shard_map/ppermute | solution.py:336
  97.7 0.9 finish.2.refs_2_
  98.6 1.8 %out_low_mine_near.1.refs_0_ = f32[1,256,1024]{2,1,0:T(8,128)S(1)} custom-call(s32[8]{0:T(128)S(1)} %stack.29.blocks_ref.groups_ref, bf16[128,2048]{1,0:T(8,128)(2,1)S(1)} %gate_first.1.refs_0_, bf16[128,2048]{1,0:T(8,128)(2,1)S(1)} %get-tuple-element.22.refs_1_, bf16[2048,4096]{1,0:T(8,128)(2,1)S(1)} %bitcast.11, ...), custom_call_target="tpu_custom_call" | custom-call | flops 1073741824 | bytes 5242880 | tf_op jit(solution)/shard_map/out_low_mine_near/pallas_call | solution.py:287
  100.4 8.1 %collective-permute-done.8.refs_1_ = bf16[256,1024]{1,0:T(8,128)(2,1)S(1)} collective-permute-done((bf16[256,1024]{1,0:T(8,128)(2,1)S(1)}, bf16[256,1024]{1,0:T(8,128)(2,1)S(1)}, u32[]{:S(2)}, u32[]{:S(2)}) %collective-permute-start.8) | collective-permute-done | bytes 524320 | tf_op jit(solution)/shard_map/ppermute | solution.py:336
  108.6 0.9 finish.3
  (50 shorter events, 6.6 us)
Async XLA Ops:
  0.0 8.1 %collective-permute-start.1 = (bf16[512,1024]{1,0:T(8,128)(2,1)}, bf16[512,1024]{1,0:T(8,128)(2,1)S(1)}, u32[]{:S(2)}, u32[]{:S(2)}) collective-permute-start(bf16[512,1024]{1,0:T(8,128)(2,1)} %refs_0_.1), channel_id=1, source_target_pairs={{0,2},{2,0},{1,3},{3,1},{4,6},{6,4},{5,7},{7,5},{8,10},{10,8},{9,1... | collective-permute-start | bytes 3145736 | tf_op jit(solution)/shard_map/ppermute | solution.py:333
  1.7 27.1 %collective-permute-start.3 = (bf16[256,1024]{1,0:T(8,128)(2,1)S(1)}, bf16[256,1024]{1,0:T(8,128)(2,1)S(1)}, u32[]{:S(2)}, u32[]{:S(2)}) collective-permute-start(bf16[256,1024]{1,0:T(8,128)(2,1)S(1)} %get-tuple-element.25), channel_id=1, source_target_pairs={{0,1},{1,0},{2,3},{3,2},{4,5},{5,4},{6,7},{7,6},{8,9},{9,8},{10,11... | collective-permute-start | bytes 1572872 | tf_op jit(solution)/shard_map/ppermute | solution.py:336
  4.3 24.2 %collective-permute-start = (bf16[256,1024]{1,0:T(8,128)(2,1)S(1)}, bf16[256,1024]{1,0:T(8,128)(2,1)S(1)}, u32[]{:S(2)}, u32[]{:S(2)}) collective-permute-start(bf16[256,1024]{1,0:T(8,128)(2,1)S(1)} %get-tuple-element.26), channel_id=1, source_target_pairs={{0,1},{1,0},{2,3},{3,2},{4,5},{5,4},{6,7},{7,6},{8,9},{9,8},{10,11... | collective-permute-start | bytes 1572872 | tf_op jit(solution)/shard_map/ppermute | solution.py:336
  4.5 0.9 copy-start.5
  8.1 1.0 copy-start.7
  9.8 21.5 %copy-start.2 = (bf16[256,256]{1,0:T(8,128)(2,1)S(1)}, bf16[256,256]{1,0:T(8,128)(2,1)}, u32[]{:S(2)}) copy-start(bf16[256,256]{1,0:T(8,128)(2,1)} %constant.27.clone.refs_9_.fwd_ref) | copy-start | bytes 393220
  9.8 21.5 %copy-start.3 = (bf16[128,256]{1,0:T(8,128)(2,1)S(1)}, bf16[128,256]{1,0:T(8,128)(2,1)}, u32[]{:S(2)}) copy-start(bf16[128,256]{1,0:T(8,128)(2,1)} %constant.28.clone.refs_10_.inv_ref) | copy-start | bytes 196612
  28.5 2.0 %copy-start.1 = (bf16[256,1024]{1,0:T(8,128)(2,1)}, bf16[256,1024]{1,0:T(8,128)(2,1)S(1)}, u32[]{:S(2)}) copy-start(bf16[256,1024]{1,0:T(8,128)(2,1)S(1)} %held_until.2.refs_0_) | copy-start | bytes 1572868
  28.5 2.0 %collective-permute-start.2 = (bf16[256,1024]{1,0:T(8,128)(2,1)S(1)}, bf16[256,1024]{1,0:T(8,128)(2,1)S(1)}, u32[]{:S(2)}, u32[]{:S(2)}) collective-permute-start(bf16[256,1024]{1,0:T(8,128)(2,1)S(1)} %held_until.2.refs_0_), channel_id=1, source_target_pairs={{0,2},{2,0},{1,3},{3,1},{4,6},{6,4},{5,7},{7,5},{8,10},{10,8},{9,1... | collective-permute-start | bytes 1572872 | tf_op jit(solution)/shard_map/ppermute | solution.py:333
  28.8 19.3 %copy-start = (bf16[256,1024]{1,0:T(8,128)(2,1)}, bf16[256,1024]{1,0:T(8,128)(2,1)S(1)}, u32[]{:S(2)}) copy-start(bf16[256,1024]{1,0:T(8,128)(2,1)S(1)} %held_until.3.refs_11_.refs_0_) | copy-start | bytes 1572868
  28.8 23.4 %collective-permute-start.5 = (bf16[256,1024]{1,0:T(8,128)(2,1)S(1)}, bf16[256,1024]{1,0:T(8,128)(2,1)S(1)}, u32[]{:S(2)}, u32[]{:S(2)}) collective-permute-start(bf16[256,1024]{1,0:T(8,128)(2,1)S(1)} %held_until.3.refs_11_.refs_0_), channel_id=1, source_target_pairs={{0,2},{2,0},{1,3},{3,1},{4,6},{6,4},{5,7},{7,5},{8,10},{10,8},{9,1... | collective-permute-start | bytes 1572872 | tf_op jit(solution)/shard_map/ppermute | solution.py:333
  30.5 0.8 copy-start.9
  31.3 39.7 %slice-start = ((s8[16777216]{0:T(1024)(128)(4,1)}), s8[4194304]{0:T(1024)(128)(4,1)S(1)}, s32[]{:S(2)}) async-start(s8[16777216]{0:T(1024)(128)(4,1)} %bitcast.10), calls=%async_computation | async-start | bytes 8388608
  31.3 39.7 %slice-start.1 = ((s8[16777216]{0:T(1024)(128)(4,1)}), s8[4194304]{0:T(1024)(128)(4,1)S(1)}, s32[]{:S(2)}) async-start(s8[16777216]{0:T(1024)(128)(4,1)} %bitcast.10), calls=%async_computation.1 | async-start | bytes 8388608
  48.2 24.8 %collective-permute-start.4 = (bf16[128,2048]{1,0:T(8,128)(2,1)S(1)}, bf16[128,2048]{1,0:T(8,128)(2,1)S(1)}, u32[]{:S(2)}, u32[]{:S(2)}) collective-permute-start(bf16[128,2048]{1,0:T(8,128)(2,1)S(1)} %get-tuple-element.17), channel_id=1, source_target_pairs={{0,4},{4,8},{8,12},{12,16},{16,20},{20,24},{24,28},{1,5},{5,9},{9,... | collective-permute-start | bytes 1572872 | tf_op jit(solution)/shard_map/ppermute | solution.py:364
  52.2 0.8 copy-start.8
  53.0 18.0 %slice-start.2 = ((s8[16777216]{0:T(1024)(128)(4,1)}), s8[4194304]{0:T(1024)(128)(4,1)S(1)}, s32[]{:S(2)}) async-start(s8[16777216]{0:T(1024)(128)(4,1)} %bitcast.10), calls=%async_computation.2 | async-start | bytes 8388608
  53.0 18.0 %slice-start.3 = ((s8[16777216]{0:T(1024)(128)(4,1)}), s8[4194304]{0:T(1024)(128)(4,1)S(1)}, s32[]{:S(2)}) async-start(s8[16777216]{0:T(1024)(128)(4,1)} %bitcast.10), calls=%async_computation.3 | async-start | bytes 8388608
  72.9 8.3 %collective-permute-start.10 = (bf16[1,256,1024]{2,1,0:T(8,128)(2,1)S(1)}, bf16[1,256,1024]{2,1,0:T(8,128)(2,1)S(1)}, u32[]{:S(2)}, u32[]{:S(2)}) collective-permute-start(bf16[1,256,1024]{2,1,0:T(8,128)(2,1)S(1)} %out_up_theirs_far.1), channel_id=1, source_target_pairs={{0,2},{2,0},{1,3},{3,1},{4,6},{6,4},{5,7},{7,5},{8,10},{10,8},{9,1... | collective-permute-start | bytes 1572872 | tf_op jit(solution)/shard_map/ppermute | solution.py:333
  78.7 7.9 %collective-permute-start.7 = (bf16[1,256,1024]{2,1,0:T(8,128)(2,1)S(1)}, bf16[1,256,1024]{2,1,0:T(8,128)(2,1)S(1)}, u32[]{:S(2)}, u32[]{:S(2)}) collective-permute-start(bf16[1,256,1024]{2,1,0:T(8,128)(2,1)S(1)} %out_low_theirs_far.1), channel_id=1, source_target_pairs={{0,2},{2,0},{1,3},{3,1},{4,6},{6,4},{5,7},{7,5},{8,10},{10,8},{9,1... | collective-permute-start | bytes 1572872 | tf_op jit(solution)/shard_map/ppermute | solution.py:333
  81.0 8.0 %collective-permute-start.9 = (bf16[1,256,1024]{2,1,0:T(8,128)(2,1)S(1)}, bf16[1,256,1024]{2,1,0:T(8,128)(2,1)S(1)}, u32[]{:S(2)}, u32[]{:S(2)}) collective-permute-start(bf16[1,256,1024]{2,1,0:T(8,128)(2,1)S(1)} %out_up_theirs_near.1), channel_id=1, source_target_pairs={{0,2},{2,0},{1,3},{3,1},{4,6},{6,4},{5,7},{7,5},{8,10},{10,8},{9,1... | collective-permute-start | bytes 1572872 | tf_op jit(solution)/shard_map/ppermute | solution.py:333
  82.9 14.8 %collective-permute-start.11 = (bf16[256,1024]{1,0:T(8,128)(2,1)S(1)}, bf16[256,1024]{1,0:T(8,128)(2,1)S(1)}, u32[]{:S(2)}, u32[]{:S(2)}) collective-permute-start(bf16[256,1024]{1,0:T(8,128)(2,1)S(1)} %bitcast.19), channel_id=1, source_target_pairs={{0,1},{1,0},{2,3},{3,2},{4,5},{5,4},{6,7},{7,6},{8,9},{9,8},{10,11... | collective-permute-start | bytes 1572872 | tf_op jit(solution)/shard_map/ppermute | solution.py:336
  86.3 12.3 %collective-permute-start.6 = (bf16[1,256,1024]{2,1,0:T(8,128)(2,1)S(1)}, bf16[1,256,1024]{2,1,0:T(8,128)(2,1)S(1)}, u32[]{:S(2)}, u32[]{:S(2)}) collective-permute-start(bf16[1,256,1024]{2,1,0:T(8,128)(2,1)S(1)} %out_low_theirs_near.1), channel_id=1, source_target_pairs={{0,2},{2,0},{1,3},{3,1},{4,6},{6,4},{5,7},{7,5},{8,10},{10,8},{9,1... | collective-permute-start | bytes 1572872 | tf_op jit(solution)/shard_map/ppermute | solution.py:333
  88.4 20.2 %collective-permute-start.8 = (bf16[256,1024]{1,0:T(8,128)(2,1)S(1)}, bf16[256,1024]{1,0:T(8,128)(2,1)S(1)}, u32[]{:S(2)}, u32[]{:S(2)}) collective-permute-start(bf16[256,1024]{1,0:T(8,128)(2,1)S(1)} %bitcast.18), channel_id=1, source_target_pairs={{0,1},{1,0},{2,3},{3,2},{4,5},{5,4},{6,7},{7,6},{8,9},{9,8},{10,11... | collective-permute-start | bytes 1572872 | tf_op jit(solution)/shard_map/ppermute | solution.py:336
  (3 other events, 2.2 us)

commit v2 on v1

v2 whole, which is shorter than its diff:
```python
import functools

import jax
import jax.numpy as jnp
import numpy as np
from jax import lax
from jax.experimental import pallas as pl
from jax.experimental.pallas import tpu as pltpu
from jax.sharding import PartitionSpec as P

BF16 = jnp.bfloat16
F32 = jnp.float32
MIB = 1024 * 1024


def dft_matrices(taps):
    size = 2 * taps
    t = np.arange(size)[None, :]
    k = np.arange(taps)[:, None]
    angle = 2.0 * np.pi * ((k * t) % size) / size
    cos, sin = np.cos(angle), np.sin(angle)
    alternating = (-1.0) ** t
    forward = np.concatenate([cos, alternating, -sin[1:]], axis=0)
    inverse = np.concatenate([cos[:1], 2.0 * cos[1:], alternating, -2.0 * sin[1:]], axis=0).T / size
    short = slice(0, taps)
    of_filter = np.concatenate(
        [cos[:, short], 0.0 * sin[:1, short], -sin[1:, short], alternating[:, short], cos[1:, short]], axis=0
    )
    of_filter = np.concatenate([of_filter, of_filter], axis=1)
    return forward.astype(BF16), inverse[taps:].astype(BF16), of_filter.astype(BF16)


def dot(a, b):
    return jnp.dot(a, b, preferred_element_type=F32)


def spectrum_kernel(taps_ref, skip_ref, of_filter_ref, *refs):
    spec_ref = refs[-1]
    h = taps_ref[...]
    first = lax.broadcasted_iota(jnp.int32, h.shape, 0) == 0
    h = h + jnp.where(first, skip_ref[...], 0.0)
    high = h.astype(BF16)
    low = (h - high.astype(F32)).astype(BF16)
    spec_ref[...] = dot(of_filter_ref[...], jnp.concatenate([high, low], axis=0))


def convolved(window, spectrum, forward, inverse):
    half = window.shape[0] // 2
    x = dot(forward, window)
    xa, xb = x[:half], x[half:]
    ha, hb, hc = spectrum[:half], spectrum[half : 2 * half], spectrum[2 * half :]
    y = jnp.concatenate([xa * ha - xb * hb, xa * hb + xb * hc], axis=0)
    return dot(inverse, y.astype(BF16))


def columns(step, ct):
    return pl.ds(pl.multiple_of(step * ct, ct), ct)


def projection(first, places, tokens, gain_ref, weight_ref, xg_ref, buf, sem, use, before=None):
    slots, _, _, ct = buf.shape
    depth = tokens[0].shape[1]
    tiles = weight_ref.shape[2] // ct

    def copies(tile, slot):
        return [
            pltpu.make_async_copy(
                weight_ref.at[:, pl.ds(pl.multiple_of(places[first + i] * depth, depth), depth), columns(tile, ct)],
                buf.at[slot, :, pl.ds(i * depth, depth)],
                sem.at[slot, i],
            )
            for i in range(len(tokens))
        ]

    for tile in range(min(slots - 1, tiles)):
        for copy in copies(tile, tile):
            copy.start()
    total = jnp.zeros((xg_ref.shape[0], 1), F32)
    for i, x_ref in reversed(list(enumerate(tokens))):
        if i == 0 and before is not None:
            before.wait()
        x = x_ref[...].astype(F32)
        total = total + jnp.sum(x * x, axis=1, keepdims=True)
        xg_ref[:, i * depth : (i + 1) * depth] = (x * gain_ref[places[first + i]]).astype(BF16)

    def step(tile, _):
        slot = lax.rem(tile, slots)
        ahead = tile + slots - 1

        @pl.when(ahead < tiles)
        def _():
            for copy in copies(ahead, lax.rem(ahead, slots)):
                copy.start()

        for copy in copies(tile, slot):
            copy.wait()
        use(tile, [dot(xg_ref[...], buf[slot, j]) for j in range(3)], total)
        return 0

    lax.fori_loop(0, tiles, step, 0)
    return total


def local_kernel(first, places, own_ref, beside_ref, gain_ref, weight_ref, out_w_ref, acc_ref, ssq_ref, held_w_ref,
                 own_held, xg_ref, buf, sem, own_sem, out_sem):
    ct = buf.shape[3]
    load = pltpu.make_async_copy(own_ref, own_held, own_sem)
    load.start()
    tiles = weight_ref.shape[2] // ct
    piece = out_w_ref.shape[0] // tiles

    def piece_copy(tile):
        rows = pl.ds(pl.multiple_of(tile * piece, piece), piece)
        return pltpu.make_async_copy(out_w_ref.at[rows], held_w_ref.at[rows], out_sem.at[tile])

    def use(tile, products, total):
        piece_copy(tile).start()
        for j in range(3):
            acc_ref[j, :, columns(tile, ct)] = products[j].astype(BF16)

    total = projection(first, places, [own_held, beside_ref], gain_ref, weight_ref, xg_ref, buf, sem, use, load)
    ssq_ref[...] = jnp.broadcast_to(total, ssq_ref.shape)
    for tile in range(tiles):
        piece_copy(tile).wait()


def streams(acc_ref, rows, at, products, ssq, d_model):
    scale = lax.rsqrt(ssq / d_model + 1e-06)
    query, keys, values = [((acc_ref[j, rows, at].astype(F32) + products[j]) * scale).astype(BF16) for j in range(3)]
    mixed = (keys.astype(F32) * values.astype(F32)).astype(BF16)
    return query, mixed


def gate(before, now, query, at, spec_ref, fwd_ref, inv_ref):
    window = jnp.concatenate([before, now], axis=0)
    filtered = convolved(window, spec_ref[:, at], fwd_ref[...], inv_ref[...])
    return (query.astype(F32) * filtered).astype(BF16)


def upper_kernel(first, d_model, taps, n_lhs, places, *refs):
    tokens = refs[:n_lhs]
    gain_ref, weight_ref, acc_ref, ssq_ref, spec_ref, fwd_ref, inv_ref = refs[n_lhs : n_lhs + 7]
    tail_ref, q_ref, mixed_ref, gated_ref, q_tail, xg_ref, buf, sem = refs[-8:]
    ct = buf.shape[3]
    rows = slice(2 * taps, 4 * taps)

    def finish_tile(tile):
        at = columns(tile, ct)
        gated_ref[:, at] = gate(mixed_ref[:, at], tail_ref[:, at], q_tail[:, at], at, spec_ref, fwd_ref, inv_ref)

    def use(tile, products, total):
        at = columns(tile, ct)
        finish_tile(jnp.maximum(tile - 1, 0))
        query, mixed = streams(acc_ref, rows, at, products, ssq_ref[rows, :1] + total, d_model)
        q_ref[:, at] = query[:taps]
        q_tail[:, at] = query[taps:]
        mixed_ref[:, at] = mixed[:taps]
        tail_ref[:, at] = mixed[taps:]

    projection(first, places, tokens, gain_ref, weight_ref, xg_ref, buf, sem, use)
    finish_tile(weight_ref.shape[2] // ct - 1)


def lower_kernel(first, d_model, taps, n_lhs, places, *refs):
    tokens = refs[:n_lhs]
    gain_ref, weight_ref, acc_ref, ssq_ref, spec_ref, fwd_ref, inv_ref, q_up_ref, mixed_up_ref = refs[n_lhs : n_lhs + 9]
    q_ref, mixed_ref, one_ref, two_ref, q_one, mixed_one, xg_ref, buf, sem = refs[-9:]
    ct = buf.shape[3]
    rows = slice(0, 2 * taps)

    def finish_tile(tile):
        at = columns(tile, ct)
        one_ref[:, at] = gate(mixed_ref[:, at], mixed_one[:, at], q_one[:, at], at, spec_ref, fwd_ref, inv_ref)
        two_ref[:, at] = gate(mixed_one[:, at], mixed_up_ref[:, at], q_up_ref[:, at], at, spec_ref, fwd_ref, inv_ref)

    def use(tile, products, total):
        at = columns(tile, ct)
        finish_tile(jnp.maximum(tile - 1, 0))
        query, mixed = streams(acc_ref, rows, at, products, ssq_ref[rows, :1] + total, d_model)
        q_ref[:, at] = query[:taps]
        q_one[:, at] = query[taps:]
        mixed_ref[:, at] = mixed[:taps]
        mixed_one[:, at] = mixed[taps:]

    projection(first, places, tokens, gain_ref, weight_ref, xg_ref, buf, sem, use)
    finish_tile(weight_ref.shape[2] // ct - 1)


def first_kernel(halo_ref, mixed_ref, q_ref, spec_ref, fwd_ref, inv_ref, *refs):
    gated_ref = refs[-1]
    ct = column_tile(q_ref.shape[1], 1024)
    for at in range(0, q_ref.shape[1], ct):
        at = slice(at, at + ct)
        gated_ref[:, at] = gate(halo_ref[:, at], mixed_ref[:, at], q_ref[:, at], at, spec_ref, fwd_ref, inv_ref)


def halves_kernel(x_ref, low_ref, high_ref, sem):
    half = low_ref.shape[0]
    copies = [
        pltpu.make_async_copy(x_ref.at[pl.ds(half * i, half)], ref, sem.at[i]) for i, ref in enumerate((low_ref, high_ref))
    ]
    for copy in copies:
        copy.start()
    for copy in copies:
        copy.wait()


def params(mib, steps=1):
    return pltpu.CompilerParams(dimension_semantics=("arbitrary",) * steps, vmem_limit_bytes=mib * MIB)


def in_hbm(x):
    return pltpu.with_memory_space_constraint(x, pltpu.HBM)


def in_vmem(x):
    return pltpu.with_memory_space_constraint(x, pltpu.VMEM)


RESIDENT = pl.BlockSpec(memory_space=pltpu.VMEM)


def whole(shape):
    return pl.BlockSpec(shape, lambda ch, *_: (0,) * len(shape))


def cost(rows, depth, width, extra=0):
    return pl.CostEstimate(
        flops=2 * rows * depth * width, bytes_accessed=2 * (rows * depth + depth * width) + extra, transcendentals=0
    )


def column_tile(channels, most=256):
    return most if channels % most == 0 else channels


def nothing_kernel(*refs):
    pass


def held_until(x, *others):
    return pl.pallas_call(
        nothing_kernel,
        in_specs=[pl.BlockSpec(memory_space=pl.ANY)] * (1 + len(others)),
        out_specs=pl.BlockSpec(memory_space=pl.ANY),
        out_shape=jax.ShapeDtypeStruct(x.shape, x.dtype),
        input_output_aliases={0: 0},
        compiler_params=pltpu.CompilerParams(vmem_limit_bytes=2 * MIB),
        name="held_until",
    )(x, *others)


BRIEF = pl.CostEstimate(flops=1, bytes_accessed=1, transcendentals=0)
IN_PLACE = pl.BlockSpec(memory_space=pl.ANY)
SCALARS = pl.BlockSpec(memory_space=pltpu.SMEM)


def row_halves(x):
    rows, width = x.shape
    return pl.pallas_call(
        halves_kernel,
        in_specs=[IN_PLACE],
        out_specs=[RESIDENT] * 2,
        out_shape=[pltpu.VMEM((rows // 2, width), x.dtype)] * 2,
        scratch_shapes=[pltpu.SemaphoreType.DMA((2,))],
        compiler_params=pltpu.CompilerParams(vmem_limit_bytes=4 * MIB),
        name="row_halves",
    )(in_hbm(x))


def filter_transform(filter_taps, conv_skip, of_filter, waits):
    taps, channels = filter_taps.shape
    ct = column_tile(channels, 1024)
    tile = lambda r: pl.BlockSpec((r, ct), lambda ch: (0, ch))
    return pl.pallas_call(
        spectrum_kernel,
        grid=(channels // ct,),
        in_specs=[tile(taps), tile(1), whole(of_filter.shape)] + [IN_PLACE] * len(waits),
        out_specs=tile(3 * taps),
        out_shape=pltpu.VMEM((3 * taps, channels), F32),
        compiler_params=params(16),
        cost_estimate=cost(3 * taps, 2 * taps, channels),
        name="filter_transform",
    )(in_hbm(filter_taps), in_hbm(conv_skip.reshape(1, -1)), in_hbm(of_filter), *waits)


def weight_scratch(rows, depth, channels, n_lhs, slots=3):
    ct = column_tile(channels)
    return [
        pltpu.VMEM((rows, depth * n_lhs), BF16),
        pltpu.VMEM((slots, 3, depth * n_lhs, ct), BF16),
        pltpu.SemaphoreType.DMA((slots, n_lhs)),
    ]


def weight_limit(rows, depth, channels, n_lhs, more=0, slots=3):
    held = 2 * depth * n_lhs * (rows + slots * 3 * column_tile(channels)) + more
    return pltpu.CompilerParams(vmem_limit_bytes=held + 10 * MIB)


def gain_rows(norm_gain, depth):
    return in_hbm(norm_gain.reshape(-1, 1, depth))


def project_local(own, beside, places, first, norm_gain, in_weight, out_weight):
    rows, depth = own.shape
    channels = in_weight.shape[2]
    tiles = channels // column_tile(channels)
    return pl.pallas_call(
        functools.partial(local_kernel, first),
        in_specs=[SCALARS, IN_PLACE, RESIDENT, RESIDENT, IN_PLACE, IN_PLACE],
        out_specs=[RESIDENT] * 3,
        out_shape=[
            pltpu.VMEM((3, rows, channels), BF16),
            pltpu.VMEM((rows, 128), F32),
            pltpu.VMEM(out_weight.shape, BF16),
        ],
        scratch_shapes=[pltpu.VMEM((rows, depth), BF16)]
        + weight_scratch(rows, depth, channels, 2)
        + [pltpu.SemaphoreType.DMA, pltpu.SemaphoreType.DMA((tiles,))],
        compiler_params=weight_limit(rows, depth, channels, 2, 2 * rows * depth),
        cost_estimate=cost(rows, depth * 2, 3 * channels),
        name="project_local",
    )(places, in_hbm(own), in_vmem(beside), gain_rows(norm_gain, depth), in_hbm(in_weight), in_hbm(out_weight))


def project_rest(kernel, name, lhs, places, first, norm_gain, in_weight, resident, estimate, d_model, taps, more):
    rows, depth = lhs[0].shape
    channels = in_weight.shape[2]
    return pl.pallas_call(
        functools.partial(kernel, first, d_model, taps, len(lhs)),
        in_specs=[SCALARS]
        + [RESIDENT] * (len(lhs) + 1)
        + [IN_PLACE]
        + [RESIDENT] * len(resident),
        out_specs=[RESIDENT] * 4,
        out_shape=[pltpu.VMEM((taps, channels), BF16)] * 4,
        scratch_shapes=[pltpu.VMEM((taps, channels), BF16)] * more + weight_scratch(rows, depth, channels, len(lhs)),
        compiler_params=weight_limit(rows, depth, channels, len(lhs), more * 2 * taps * channels),
        cost_estimate=estimate,
        name=name,
    )(
        places,
        *[in_vmem(x) for x in lhs],
        gain_rows(norm_gain, depth),
        in_hbm(in_weight),
        *[in_vmem(x) for x in resident],
    )


def gate_first(halo, mixed, query, spectrum, forward, inverse, waits):
    taps, channels = mixed.shape
    return pl.pallas_call(
        first_kernel,
        in_specs=[RESIDENT] * 6 + [IN_PLACE] * len(waits),
        out_specs=RESIDENT,
        out_shape=pltpu.VMEM((taps, channels), BF16),
        compiler_params=pltpu.CompilerParams(vmem_limit_bytes=16 * MIB),
        cost_estimate=BRIEF,
        name="gate_first",
    )(*[in_vmem(x) for x in (halo, mixed, query, spectrum, forward, inverse)], *waits)


def out_kernel(n_parts, n_add, n_come, first, add_first, places, *refs):
    parts, w_ref = refs[:n_parts], refs[n_parts]
    add, come = refs[n_parts + 1 : n_parts + 1 + n_add], refs[n_parts + 1 + n_add : n_parts + 1 + n_add + n_come]
    o_ref = refs[-1]
    width = o_ref.shape[-1]
    lhs = jnp.concatenate([p[...] for p in parts], axis=0)
    for g in range(o_ref.shape[0] if len(o_ref.shape) == 3 else 1):
        at = pl.ds(pl.multiple_of(places[first + g] * width, width), width)
        product = dot(lhs, w_ref[:, at])
        for x in add:
            product = product + x[add_first + g].astype(F32)
        for x in come:
            product = product + x[...].astype(F32)
        if len(o_ref.shape) == 3:
            o_ref[g] = product.astype(o_ref.dtype)
        else:
            o_ref[...] = product.astype(o_ref.dtype)


def project_out(parts, out_weight, places, first, n_groups, width, name, add=(), add_first=0, dtype=BF16, waits=()):
    rows = sum(p.shape[0] for p in parts)
    return pl.pallas_call(
        functools.partial(out_kernel, len(parts), len(add), 0, first, add_first),
        in_specs=[SCALARS] + [RESIDENT] * (len(parts) + 1 + len(add)) + [IN_PLACE] * len(waits),
        out_specs=RESIDENT,
        out_shape=pltpu.VMEM((n_groups, rows, width), dtype),
        compiler_params=pltpu.CompilerParams(vmem_limit_bytes=16 * MIB),
        cost_estimate=BRIEF,
        name=name,
    )(places, *[in_vmem(x) for x in (*parts, out_weight, *add)], *waits)


def project_last(parts, out_weight, places, first, width, name, add, add_first, come, part, n_parts):
    rows = sum(p.shape[0] for p in parts)
    return pl.pallas_call(
        functools.partial(out_kernel, len(parts), len(add), len(come), first, add_first),
        grid=(1,),
        in_specs=[SCALARS] + [RESIDENT] * (len(parts) + 1 + len(add) + len(come)),
        out_specs=pl.BlockSpec((rows, width), lambda i: (part, 0)),
        out_shape=jax.ShapeDtypeStruct((rows * n_parts, width), BF16),
        compiler_params=params(16),
        cost_estimate=BRIEF,
        name=name,
    )(places, *[in_vmem(x) for x in (*parts, out_weight, *add, *come)])


def finish_kernel(n_come, *refs):
    total = refs[0][0]
    for x in refs[1 : 1 + n_come]:
        total = total + x[...].astype(F32)
    refs[-1][...] = total.astype(refs[-1].dtype)


def finish(near, come, into, part):
    rows, width = near.shape[1:]
    return pl.pallas_call(
        functools.partial(finish_kernel, len(come)),
        grid=(1,),
        in_specs=[RESIDENT] * (1 + len(come)) + [IN_PLACE],
        out_specs=pl.BlockSpec((rows, width), lambda i: (part, 0)),
        out_shape=jax.ShapeDtypeStruct(into.shape, BF16),
        input_output_aliases={1 + len(come): 0},
        compiler_params=params(16),
        cost_estimate=BRIEF,
        name="finish",
    )(in_vmem(near), *[in_vmem(x) for x in come], into)


def on_device(tokens, norm_gain, in_weight, filter_taps, conv_skip, out_weight):
    n_row, n_col, n_seq = lax.axis_size("trow"), lax.axis_size("tcol"), lax.axis_size("seq")
    r, c = lax.axis_index("trow"), lax.axis_index("tcol")
    rows, depth = tokens.shape
    taps = filter_taps.shape[0]
    half = 2 * taps
    d_model = depth * n_row * n_col
    assert n_row == 2 and rows == 2 * half
    forward, inverse, of_filter = (jnp.asarray(m) for m in dft_matrices(taps))

    def other_core(x):
        return lax.ppermute(x, "trow", [(0, 1), (1, 0)])

    def chips_along(x, s):
        return lax.ppermute(x, "tcol", [(i, (i + s) % n_col) for i in range(n_col)])

    def block_of(row, s):
        return row * n_col + lax.rem(c + s + n_col, n_col)

    beside = other_core(tokens)
    low_rows, high_rows = row_halves(tokens)
    upper_far = [chips_along(high_rows, s) for s in range(1, n_col)]
    lower_far = [chips_along(low_rows, s) for s in range(1, n_col)]
    shifts = range(1, n_col)
    places = jnp.stack(
        [block_of(r, 0), block_of(1 - r, 0)]
        + [block_of(row, -s) for row in (r, 1 - r) for s in shifts]
        + [block_of(row, s) for row in (1 - r, r) for s in (*shifts, 0)]
    )
    n_far = n_col - 1
    far_features, theirs_far = 2, 2 * n_col
    theirs_near, mine_far = theirs_far + n_far, theirs_far + n_col
    mine_near = mine_far + n_far
    acc, ssq, held_weight = project_local(tokens, beside, places, 0, norm_gain, in_weight, out_weight)
    spectrum = filter_transform(filter_taps, conv_skip, of_filter, [ssq])
    rest = functools.partial(
        project_rest, places=places, first=far_features, norm_gain=norm_gain, in_weight=in_weight, d_model=d_model, taps=taps
    )
    upper_far = [held_until(x, ssq) for x in upper_far]
    resident = [acc, ssq, spectrum, forward, inverse]
    upper = upper_far + [other_core(x) for x in upper_far]
    tail, q_up, mixed_up, gated_up = rest(
        upper_kernel, "project_upper", upper, resident=resident, estimate=BRIEF, more=1
    )
    halo = lax.ppermute(tail, "seq", [(i, i + 1) for i in range(n_seq - 1)])
    lower_far = [held_until(x, tail) for x in lower_far]
    lower = lower_far + [other_core(x) for x in lower_far]
    q_low, mixed_low, gated_one, gated_two = rest(
        lower_kernel, "project_lower", lower, resident=resident + [q_up, mixed_up], estimate=cost(2 * taps, d_model, 3 * in_weight.shape[2]), more=2
    )
    gated_first = gate_first(halo, mixed_low, q_low, spectrum, forward, inverse, [])

    project = functools.partial(project_out, [gated_two, gated_up], held_weight, places, width=depth)
    far = other_core(project(theirs_far, n_far, name="up_theirs_far", waits=[gated_first]))
    near = project(theirs_near, 1, name="up_theirs_near")
    sent_up = project(mine_far, n_far, name="up_mine_far", add=[far], waits=[near])
    near = other_core(near)
    come_up = [chips_along(sent_up[s - 1], s) for s in shifts]

    low = [gated_first, gated_one]
    project = functools.partial(project_out, low, held_weight, places, width=depth)
    theirs = other_core(project(theirs_far, n_col, name="low_theirs", waits=[sent_up]))
    sent_low = project(mine_far, n_far, name="low_mine_far", add=[theirs])
    come_low = [chips_along(sent_low[s - 1], s) for s in shifts]

    out = project_last(
        [gated_two, gated_up], held_weight, places, mine_near, depth, "up_mine_near", [near], 0, come_up, 1, 2
    )
    near_low = project(mine_near, 1, name="low_mine_near", add=[theirs], add_first=n_far, dtype=F32, waits=come_up)
    return finish(near_low, come_low, out, 0)


def solution(mesh):
    placed = (
        P("seq", ("trow", "tcol")),
        P(),
        P(None, None, ("trow", "tcol")),
        P(None, ("trow", "tcol")),
        P(("trow", "tcol")),
        P(("trow", "tcol"), None),
    )
    return jax.shard_map(
        on_device, mesh=mesh, in_specs=placed, out_specs=P("seq", ("trow", "tcol")), check_vma=False
    )
```

time: 110 us -> 94 us (0.85)
  Pallas kernels: 74.8 us -> 64.8 us
  local copies, waits for them, and re-layouts: 7.06 us -> 0.1 us
  waiting for transfers between devices: 16.5 us -> 17.9 us
    pallas_call x12, Pallas kernels: 71 us -> 61.9 us  [the longest x2 27.4 us: project_rest(): pl.pallas_call(functools.partial(kernel, first, d_model, taps, len(lhs)),...]
    unnamed x30 -> x4, local copies, waits for them, and re-layouts: 5.71 us -> 0.01 us
    ppermute x4, waiting for transfers between devices: 15 us -> 16.3 us  [chips_along(): return lax.ppermute(x, 'tcol', [(i, (i + s) % n_col) for i in range(n_col)])]
    slice x1 -> x0, local copies, waits for them, and re-layouts: 1.27 us -> none  [on_device(): lower_far = [chips_along(tokens[:half], s) for s in range(1, n_col)]]
  transfers between devices with their start and end apart: 12 -> 11, of which waited for: 3 -> 3; matrix products, arithmetic and copies ran while one was open for 1% -> 0% of each run, Pallas kernels for 68% -> 60%
where the time goes in v2:
time: 94 us; the launch traced here: 93.6 us
  Pallas kernels  64.8 us (69%)
  waiting for transfers between devices  17.9 us (19%)
  starting transfers between devices  10.6 us (11%)
    pallas_call x2, Pallas kernels, project_rest(): pl.pallas_call(functools.partial(kernel, first, d_model, taps, len(lhs)),...  27.4 us
    pallas_call x1, Pallas kernels, project_local(): pl.pallas_call(functools.partial(local_kernel, first), in_specs=[SCALARS,...  17.7 us
    ppermute x4, waiting for transfers between devices, chips_along(): return lax.ppermute(x, 'tcol', [(i, (i + s) % n_col) for i in range(n_col)])  16.3 us
    pallas_call x6, Pallas kernels, project_out(): pl.pallas_call(functools.partial(out_kernel, len(parts), len(add), 0, fir...  11.9 us
    ppermute x4, starting transfers between devices, chips_along(): return lax.ppermute(x, 'tcol', [(i, (i + s) % n_col) for i in range(n_col)])  5.29 us
    ppermute x1, starting transfers between devices, on_device(): halo = lax.ppermute(tail, 'seq', [(i, i + 1) for i in range(n_seq - 1)])  3.59 us
    pallas_call x1, Pallas kernels, project_last(): pl.pallas_call(functools.partial(out_kernel, len(parts), len(add), len(co...  2.63 us
    pallas_call x1, Pallas kernels, filter_transform(): pl.pallas_call(spectrum_kernel, grid=(channels // ct,), in_specs=[tile(ta...  2.08 us
  transfers between devices with their start and end apart: 11, of which 3 were waited for; matrix products, arithmetic and copies ran while one was open for 0% of the time, Pallas kernels for 60%

profile of v2, /device:TPU:0, one launch (start us, length us, event | category | flops | bytes accessed | tf_op | source)
XLA Modules:
  0.0 93.6 jit_solution(9004840945682007453)
XLA Ops:
  0.0 0.5 collective-permute-start.1
  0.5 1.2 %row_halves.1 = (bf16[256,1024]{1,0:T(8,128)(2,1)S(1)}, bf16[256,1024]{1,0:T(8,128)(2,1)S(1)}) custom-call(bf16[512,1024]{1,0:T(8,128)(2,1)} %own_ref.1), custom_call_target="tpu_custom_call" | custom-call | tf_op jit(solution)/shard_map/row_halves/pallas_call | solution.py:260
  1.7 2.6 %collective-permute-start = (bf16[256,1024]{1,0:T(8,128)(2,1)S(1)}, bf16[256,1024]{1,0:T(8,128)(2,1)S(1)}, u32[]{:S(2)}, u32[]{:S(2)}) collective-permute-start(bf16[256,1024]{1,0:T(8,128)(2,1)S(1)} %get-tuple-element.18), channel_id=1, source_target_pairs={{0,1},{1,0},{2,3},{3,2},{4,5},{5,4},{6,7},{7,6},{8,9},{9,8},{10,11... | collective-permute-start | bytes 1572872 | tf_op jit(solution)/shard_map/ppermute | solution.py:446
  4.4 17.7 %project_local.1 = (bf16[3,512,2048]{2,1,0:T(8,128)(2,1)S(1)}, f32[512,128]{1,0:T(8,128)S(1)}, bf16[2048,4096]{1,0:T(8,128)(2,1)S(1)}) custom-call(s32[8]{0:T(128)S(1)} %stack.29.places, bf16[512,1024]{1,0:T(8,128)(2,1)} %own_ref.1, bf16[512,1024]{1,0:T(8,128)(2,1)S(1)} %collective-permute-done.1.beside_ref, f32[4,1,1024]{2,1,0:T(1,128)} %bitcast.12, ...), custom_call_target="tpu_custom_call" | custom-call | flops 12884901888 | bytes 27262976 | tf_op jit(solution)/shard_map/project_local/pallas_call | solution.py:309
  22.4 1.4 %collective-permute-start.4 = (bf16[256,1024]{1,0:T(8,128)(2,1)S(1)}, bf16[256,1024]{1,0:T(8,128)(2,1)S(1)}, u32[]{:S(2)}, u32[]{:S(2)}) collective-permute-start(bf16[256,1024]{1,0:T(8,128)(2,1)S(1)} %get-tuple-element.22), channel_id=1, source_target_pairs={{0,1},{1,0},{2,3},{3,2},{4,5},{5,4},{6,7},{7,6},{8,9},{9,8},{10,11... | collective-permute-start | bytes 1572872 | tf_op jit(solution)/shard_map/ppermute | solution.py:446
  23.8 2.1 %filter_transform.1.refs_6_.spec_ref = f32[384,2048]{1,0:T(8,128)S(1)} custom-call(f32[128,2048]{1,0:T(8,128)} %taps_ref.1, f32[1,2048]{1,0:T(1,128)} %bitcast.15, bf16[384,256]{1,0:T(8,128)(2,1)} %constant.29.clone.of_filter_ref, f32[512,128]{1,0:T(8,128)S(1)} %get-tuple-element.19.refs_1_.refs_0_.refs_5_), custom_call_target="tpu_custom_call" | custom-call | flops 402653184 | bytes 1245184 | tf_op jit(solution)/shard_map/filter_transform/pallas_call | solution.py:275
  25.9 12.7 %project_upper.1 = (bf16[128,2048]{1,0:T(8,128)(2,1)S(1)}, bf16[128,2048]{1,0:T(8,128)(2,1)S(1)}, bf16[128,2048]{1,0:T(8,128)(2,1)S(1)}, bf16[128,2048]{1,0:T(8,128)(2,1)S(1)}) custom-call(s32[8]{0:T(128)S(1)} %stack.29.places, bf16[256,1024]{1,0:T(8,128)(2,1)S(1)} %held_until.2.refs_0_, bf16[256,1024]{1,0:T(8,128)(2,1)S(1)} %collective-permute-done.2.refs_1_, ...), custom_call_target="tpu_custom_call" | custom-call | flops 1 | bytes 1 | tf_op jit(solution)/shard_map/project_upper/pallas_call | solution.py:330
  38.8 3.6 %collective-permute-start.3 = (bf16[128,2048]{1,0:T(8,128)(2,1)S(1)}, bf16[128,2048]{1,0:T(8,128)(2,1)S(1)}, u32[]{:S(2)}, u32[]{:S(2)}) collective-permute-start(bf16[128,2048]{1,0:T(8,128)(2,1)S(1)} %get-tuple-element.21.refs_1_), channel_id=1, source_target_pairs={{0,4},{4,8},{8,12},{12,16},{16,20},{20,24},{24,28},{1,5},{5,9},{9,... | collective-permute-start | bytes 1572872 | tf_op jit(solution)/shard_map/ppermute | solution.py:476
  42.4 14.6 %project_lower.1 = (bf16[128,2048]{1,0:T(8,128)(2,1)S(1)}, bf16[128,2048]{1,0:T(8,128)(2,1)S(1)}, bf16[128,2048]{1,0:T(8,128)(2,1)S(1)}, bf16[128,2048]{1,0:T(8,128)(2,1)S(1)}) custom-call(s32[8]{0:T(128)S(1)} %stack.29.places, bf16[256,1024]{1,0:T(8,128)(2,1)S(1)} %held_until.3.refs_0_, bf16[256,1024]{1,0:T(8,128)(2,1)S(1)} %collective-permute-done.5.refs_1_, ...), custom_call_target="tpu_custom_call" | custom-call | flops 12884901888 | bytes 52428800 | tf_op jit(solution)/shard_map/project_lower/pallas_call | solution.py:330
  57.1 1.0 %gate_first.1.refs_3_.refs_0_ = bf16[128,2048]{1,0:T(8,128)(2,1)S(1)} custom-call(bf16[128,2048]{1,0:T(8,128)(2,1)S(1)} %collective-permute-done.3.halo_ref, bf16[128,2048]{1,0:T(8,128)(2,1)S(1)} %get-tuple-element.25.mixed_ref, bf16[128,2048]{1,0:T(8,128)(2,1)S(1)} %get-tuple-element.26.q_ref, f32[384,2048]{1,0:T(8,128)S(1)} %filter_transform.1.refs_6_.spec_ref, ...), custom_call_target="tpu_custom_call" | custom-call | flops 1 | bytes 1 | tf_op jit(solution)/shard_map/gate_first/pallas_call | solution.py:353
  58.1 1.8 %up_theirs_far.1 = bf16[1,256,1024]{2,1,0:T(8,128)(2,1)S(1)} custom-call(s32[8]{0:T(128)S(1)} %stack.29.places, bf16[128,2048]{1,0:T(8,128)(2,1)S(1)} %get-tuple-element.29.refs_0_, bf16[128,2048]{1,0:T(8,128)(2,1)S(1)} %get-tuple-element.30.refs_1_, bf16[2048,4096]{1,0:T(8,128)(2,1)S(1)} %get-tuple-element.28.refs_2_, ...), custom_call_target="tpu_custom_call" | custom-call | flops 1 | bytes 1 | tf_op jit(solution)/shard_map/up_theirs_far/pallas_call | solution.py:385
  60.1 1.8 %up_theirs_near.1.refs_4_ = bf16[1,256,1024]{2,1,0:T(8,128)(2,1)S(1)} custom-call(s32[8]{0:T(128)S(1)} %stack.29.places, bf16[128,2048]{1,0:T(8,128)(2,1)S(1)} %get-tuple-element.29.refs_0_, bf16[128,2048]{1,0:T(8,128)(2,1)S(1)} %get-tuple-element.30.refs_1_, bf16[2048,4096]{1,0:T(8,128)(2,1)S(1)} %get-tuple-element.28.refs_2_), custom_call_target="tpu_custom_call" | custom-call | flops 1 | bytes 1 | tf_op jit(solution)/shard_map/up_theirs_near/pallas_call | solution.py:385
  61.9 1.8 %up_mine_far.1.refs_3_ = bf16[1,256,1024]{2,1,0:T(8,128)(2,1)S(1)} custom-call(s32[8]{0:T(128)S(1)} %stack.29.places, bf16[128,2048]{1,0:T(8,128)(2,1)S(1)} %get-tuple-element.29.refs_0_, bf16[128,2048]{1,0:T(8,128)(2,1)S(1)} %get-tuple-element.30.refs_1_, bf16[2048,4096]{1,0:T(8,128)(2,1)S(1)} %get-tuple-element.28.refs_2_, ...), custom_call_target="tpu_custom_call" | custom-call | flops 1 | bytes 1 | tf_op jit(solution)/shard_map/up_mine_far/pallas_call | solution.py:385
  63.8 2.9 %low_theirs.1 = bf16[2,256,1024]{2,1,0:T(8,128)(2,1)S(1)} custom-call(s32[8]{0:T(128)S(1)} %stack.29.places, bf16[128,2048]{1,0:T(8,128)(2,1)S(1)} %gate_first.1.refs_3_.refs_0_, bf16[128,2048]{1,0:T(8,128)(2,1)S(1)} %get-tuple-element.27.refs_1_, bf16[2048,4096]{1,0:T(8,128)(2,1)S(1)} %get-tuple-element.28.refs_2_, bf16[1,256,1024]{2,1,0:T(8,128)(2,1)S(1)} %up_mine_far.1.refs_3_), custom_call_target="tpu_custom_call" | custom-call | flops 1 | bytes 1 | tf_op jit(solution)/shard_map/low_theirs/pallas_call | solution.py:385
  66.7 0.4 collective-permute-start.7
  67.3 0.6 collective-permute-start.8
  67.9 1.5 %collective-permute-done.7.refs_3_ = bf16[2,256,1024]{2,1,0:T(8,128)(2,1)S(1)} collective-permute-done((bf16[2,256,1024]{2,1,0:T(8,128)(2,1)S(1)}, bf16[2,256,1024]{2,1,0:T(8,128)(2,1)S(1)}, u32[]{:S(2)}, u32[]{:S(2)}) %collective-permute-start.7) | collective-permute-done | bytes 1048608 | tf_op jit(solution)/shard_map/ppermute | solution.py:443
  69.4 1.8 %low_mine_far.1 = bf16[1,256,1024]{2,1,0:T(8,128)(2,1)S(1)} custom-call(s32[8]{0:T(128)S(1)} %stack.29.places, bf16[128,2048]{1,0:T(8,128)(2,1)S(1)} %gate_first.1.refs_3_.refs_0_, bf16[128,2048]{1,0:T(8,128)(2,1)S(1)} %get-tuple-element.27.refs_1_, bf16[2048,4096]{1,0:T(8,128)(2,1)S(1)} %get-tuple-element.28.refs_2_, ...), custom_call_target="tpu_custom_call" | custom-call | flops 1 | bytes 1 | tf_op jit(solution)/shard_map/low_mine_far/pallas_call | solution.py:385
  71.2 0.7 collective-permute-start.9
  71.9 10.1 %collective-permute-done.8.refs_4_ = bf16[256,1024]{1,0:T(8,128)(2,1)S(1)} collective-permute-done((bf16[256,1024]{1,0:T(8,128)(2,1)S(1)}, bf16[256,1024]{1,0:T(8,128)(2,1)S(1)}, u32[]{:S(2)}, u32[]{:S(2)}) %collective-permute-start.8) | collective-permute-done | bytes 524320 | tf_op jit(solution)/shard_map/ppermute | solution.py:446
  82.0 2.6 %up_mine_near.1.refs_2_ = bf16[512,1024]{1,0:T(8,128)(2,1)} custom-call(s32[8]{0:T(128)S(1)} %stack.29.places, bf16[128,2048]{1,0:T(8,128)(2,1)S(1)} %get-tuple-element.29.refs_0_, bf16[128,2048]{1,0:T(8,128)(2,1)S(1)} %get-tuple-element.30.refs_1_, bf16[2048,4096]{1,0:T(8,128)(2,1)S(1)} %get-tuple-element.28.refs_2_, ...), custom_call_target="tpu_custom_call" | custom-call | flops 1 | bytes 1 | tf_op jit(solution)/shard_map/up_mine_near/pallas_call | solution.py:398
  84.6 1.8 %low_mine_near.1.refs_0_ = f32[1,256,1024]{2,1,0:T(8,128)S(1)} custom-call(s32[8]{0:T(128)S(1)} %stack.29.places, bf16[128,2048]{1,0:T(8,128)(2,1)S(1)} %gate_first.1.refs_3_.refs_0_, bf16[128,2048]{1,0:T(8,128)(2,1)S(1)} %get-tuple-element.27.refs_1_, bf16[2048,4096]{1,0:T(8,128)(2,1)S(1)} %get-tuple-element.28.refs_2_, ...), custom_call_target="tpu_custom_call" | custom-call | flops 1 | bytes 1 | tf_op jit(solution)/shard_map/low_mine_near/pallas_call | solution.py:385
  86.4 6.2 %collective-permute-done.9.refs_1_ = bf16[256,1024]{1,0:T(8,128)(2,1)S(1)} collective-permute-done((bf16[256,1024]{1,0:T(8,128)(2,1)S(1)}, bf16[256,1024]{1,0:T(8,128)(2,1)S(1)}, u32[]{:S(2)}, u32[]{:S(2)}) %collective-permute-start.9) | collective-permute-done | bytes 524320 | tf_op jit(solution)/shard_map/ppermute | solution.py:446
  92.7 0.9 finish.1
  (19 shorter events, 0.9 us)
Async XLA Ops:
  0.0 4.3 %collective-permute-start.1 = (bf16[512,1024]{1,0:T(8,128)(2,1)}, bf16[512,1024]{1,0:T(8,128)(2,1)S(1)}, u32[]{:S(2)}, u32[]{:S(2)}) collective-permute-start(bf16[512,1024]{1,0:T(8,128)(2,1)} %own_ref.1), channel_id=1, source_target_pairs={{0,2},{2,0},{1,3},{3,1},{4,6},{6,4},{5,7},{7,5},{8,10},{10,8},{9,1... | collective-permute-start | bytes 3145736 | tf_op jit(solution)/shard_map/ppermute | solution.py:443
  1.7 20.4 %collective-permute-start = (bf16[256,1024]{1,0:T(8,128)(2,1)S(1)}, bf16[256,1024]{1,0:T(8,128)(2,1)S(1)}, u32[]{:S(2)}, u32[]{:S(2)}) collective-permute-start(bf16[256,1024]{1,0:T(8,128)(2,1)S(1)} %get-tuple-element.18), channel_id=1, source_target_pairs={{0,1},{1,0},{2,3},{3,2},{4,5},{5,4},{6,7},{7,6},{8,9},{9,8},{10,11... | collective-permute-start | bytes 1572872 | tf_op jit(solution)/shard_map/ppermute | solution.py:446
  4.3 21.5 %copy-start = (bf16[256,256]{1,0:T(8,128)(2,1)S(1)}, bf16[256,256]{1,0:T(8,128)(2,1)}, u32[]{:S(2)}) copy-start(bf16[256,256]{1,0:T(8,128)(2,1)} %constant.27.clone.refs_7_.fwd_ref) | copy-start | bytes 393220
  4.4 21.5 %copy-start.1 = (bf16[128,256]{1,0:T(8,128)(2,1)S(1)}, bf16[128,256]{1,0:T(8,128)(2,1)}, u32[]{:S(2)}) copy-start(bf16[128,256]{1,0:T(8,128)(2,1)} %constant.28.clone.refs_8_.inv_ref) | copy-start | bytes 196612
  22.1 3.8 %collective-permute-start.2 = (bf16[256,1024]{1,0:T(8,128)(2,1)S(1)}, bf16[256,1024]{1,0:T(8,128)(2,1)S(1)}, u32[]{:S(2)}, u32[]{:S(2)}) collective-permute-start(bf16[256,1024]{1,0:T(8,128)(2,1)S(1)} %held_until.2.refs_0_), channel_id=1, source_target_pairs={{0,2},{2,0},{1,3},{3,1},{4,6},{6,4},{5,7},{7,5},{8,10},{10,8},{9,1... | collective-permute-start | bytes 1572872 | tf_op jit(solution)/shard_map/ppermute | solution.py:443
  22.4 16.3 %collective-permute-start.4 = (bf16[256,1024]{1,0:T(8,128)(2,1)S(1)}, bf16[256,1024]{1,0:T(8,128)(2,1)S(1)}, u32[]{:S(2)}, u32[]{:S(2)}) collective-permute-start(bf16[256,1024]{1,0:T(8,128)(2,1)S(1)} %get-tuple-element.22), channel_id=1, source_target_pairs={{0,1},{1,0},{2,3},{3,2},{4,5},{5,4},{6,7},{7,6},{8,9},{9,8},{10,11... | collective-permute-start | bytes 1572872 | tf_op jit(solution)/shard_map/ppermute | solution.py:446
  38.7 3.8 %collective-permute-start.5 = (bf16[256,1024]{1,0:T(8,128)(2,1)S(1)}, bf16[256,1024]{1,0:T(8,128)(2,1)S(1)}, u32[]{:S(2)}, u32[]{:S(2)}) collective-permute-start(bf16[256,1024]{1,0:T(8,128)(2,1)S(1)} %held_until.3.refs_0_), channel_id=1, source_target_pairs={{0,2},{2,0},{1,3},{3,1},{4,6},{6,4},{5,7},{7,5},{8,10},{10,8},{9,1... | collective-permute-start | bytes 1572872 | tf_op jit(solution)/shard_map/ppermute | solution.py:443
  38.8 18.2 %collective-permute-start.3 = (bf16[128,2048]{1,0:T(8,128)(2,1)S(1)}, bf16[128,2048]{1,0:T(8,128)(2,1)S(1)}, u32[]{:S(2)}, u32[]{:S(2)}) collective-permute-start(bf16[128,2048]{1,0:T(8,128)(2,1)S(1)} %get-tuple-element.21.refs_1_), channel_id=1, source_target_pairs={{0,4},{4,8},{8,12},{12,16},{16,20},{20,24},{24,28},{1,5},{5,9},{9,... | collective-permute-start | bytes 1572872 | tf_op jit(solution)/shard_map/ppermute | solution.py:476
  59.9 2.0 %collective-permute-start.6 = (bf16[1,256,1024]{2,1,0:T(8,128)(2,1)S(1)}, bf16[1,256,1024]{2,1,0:T(8,128)(2,1)S(1)}, u32[]{:S(2)}, u32[]{:S(2)}) collective-permute-start(bf16[1,256,1024]{2,1,0:T(8,128)(2,1)S(1)} %up_theirs_far.1), channel_id=1, source_target_pairs={{0,2},{2,0},{1,3},{3,1},{4,6},{6,4},{5,7},{7,5},{8,10},{10,8},{9,1... | collective-permute-start | bytes 1572872 | tf_op jit(solution)/shard_map/ppermute | solution.py:443
  66.7 2.7 %collective-permute-start.7 = (bf16[2,256,1024]{2,1,0:T(8,128)(2,1)S(1)}, bf16[2,256,1024]{2,1,0:T(8,128)(2,1)S(1)}, u32[]{:S(2)}, u32[]{:S(2)}) collective-permute-start(bf16[2,256,1024]{2,1,0:T(8,128)(2,1)S(1)} %low_theirs.1), channel_id=1, source_target_pairs={{0,2},{2,0},{1,3},{3,1},{4,6},{6,4},{5,7},{7,5},{8,10},{10,8},{9,1... | collective-permute-start | bytes 3145736 | tf_op jit(solution)/shard_map/ppermute | solution.py:443
  67.1 4.8 %collective-permute-start.10 = (bf16[1,256,1024]{2,1,0:T(8,128)(2,1)S(1)}, bf16[1,256,1024]{2,1,0:T(8,128)(2,1)S(1)}, u32[]{:S(2)}, u32[]{:S(2)}) collective-permute-start(bf16[1,256,1024]{2,1,0:T(8,128)(2,1)S(1)} %up_theirs_near.1.refs_4_), channel_id=1, source_target_pairs={{0,2},{2,0},{1,3},{3,1},{4,6},{6,4},{5,7},{7,5},{8,10},{10,8},{9,1... | collective-permute-start | bytes 1572872 | tf_op jit(solution)/shard_map/ppermute | solution.py:443
  67.3 14.7 %collective-permute-start.8 = (bf16[256,1024]{1,0:T(8,128)(2,1)S(1)}, bf16[256,1024]{1,0:T(8,128)(2,1)S(1)}, u32[]{:S(2)}, u32[]{:S(2)}) collective-permute-start(bf16[256,1024]{1,0:T(8,128)(2,1)S(1)} %bitcast.10), channel_id=1, source_target_pairs={{0,1},{1,0},{2,3},{3,2},{4,5},{5,4},{6,7},{7,6},{8,9},{9,8},{10,11... | collective-permute-start | bytes 1572872 | tf_op jit(solution)/shard_map/ppermute | solution.py:446
  71.2 21.5 %collective-permute-start.9 = (bf16[256,1024]{1,0:T(8,128)(2,1)S(1)}, bf16[256,1024]{1,0:T(8,128)(2,1)S(1)}, u32[]{:S(2)}, u32[]{:S(2)}) collective-permute-start(bf16[256,1024]{1,0:T(8,128)(2,1)S(1)} %bitcast.11), channel_id=1, source_target_pairs={{0,1},{1,0},{2,3},{3,2},{4,5},{5,4},{6,7},{7,6},{8,9},{9,8},{10,11... | collective-permute-start | bytes 1572872 | tf_op jit(solution)/shard_map/ppermute | solution.py:446

commit v3 on v2

--- a/solution.py
+++ b/solution.py
@@ -124,66 +124,39 @@
         piece_copy(tile).wait()
 
 
-def streams(acc_ref, rows, at, products, ssq, d_model):
-    scale = lax.rsqrt(ssq / d_model + 1e-06)
-    query, keys, values = [((acc_ref[j, rows, at].astype(F32) + products[j]) * scale).astype(BF16) for j in range(3)]
-    mixed = (keys.astype(F32) * values.astype(F32)).astype(BF16)
-    return query, mixed
-
-
 def gate(before, now, query, at, spec_ref, fwd_ref, inv_ref):
     window = jnp.concatenate([before, now], axis=0)
     filtered = convolved(window, spec_ref[:, at], fwd_ref[...], inv_ref[...])
     return (query.astype(F32) * filtered).astype(BF16)
 
 
-def upper_kernel(first, d_model, taps, n_lhs, places, *refs):
+def last_kernel(first, d_model, taps, n_lhs, places, *refs):
     tokens = refs[:n_lhs]
     gain_ref, weight_ref, acc_ref, ssq_ref, spec_ref, fwd_ref, inv_ref = refs[n_lhs : n_lhs + 7]
-    tail_ref, q_ref, mixed_ref, gated_ref, q_tail, xg_ref, buf, sem = refs[-8:]
-    ct = buf.shape[3]
-    rows = slice(2 * taps, 4 * taps)
-
-    def finish_tile(tile):
-        at = columns(tile, ct)
-        gated_ref[:, at] = gate(mixed_ref[:, at], tail_ref[:, at], q_tail[:, at], at, spec_ref, fwd_ref, inv_ref)
+    tail_ref, q_ref, mixed_ref, gated_ref, q_rest, mixed_rest, xg_ref, buf, sem = refs[-9:]
+    channels, ct = weight_ref.shape[2], buf.shape[3]
 
     def use(tile, products, total):
         at = columns(tile, ct)
-        finish_tile(jnp.maximum(tile - 1, 0))
-        query, mixed = streams(acc_ref, rows, at, products, ssq_ref[rows, :1] + total, d_model)
+        scale = lax.rsqrt((ssq_ref[:, :1] + total) / d_model + 1e-06)
+        query, keys, values = [((acc_ref[j, :, at].astype(F32) + products[j]) * scale).astype(BF16) for j in range(3)]
+        mixed = (keys.astype(F32) * values.astype(F32)).astype(BF16)
         q_ref[:, at] = query[:taps]
-        q_tail[:, at] = query[taps:]
+        q_rest[:, at] = query[taps:]
         mixed_ref[:, at] = mixed[:taps]
-        tail_ref[:, at] = mixed[taps:]
+        mixed_rest[:, at] = mixed[taps:]
+        tail_ref[:, at] = mixed[mixed.shape[0] - taps :]
 
     projection(first, places, tokens, gain_ref, weight_ref, xg_ref, buf, sem, use)
-    finish_tile(weight_ref.shape[2] // ct - 1)
-
-
-def lower_kernel(first, d_model, taps, n_lhs, places, *refs):
-    tokens = refs[:n_lhs]
-    gain_ref, weight_ref, acc_ref, ssq_ref, spec_ref, fwd_ref, inv_ref, q_up_ref, mixed_up_ref = refs[n_lhs : n_lhs + 9]
-    q_ref, mixed_ref, one_ref, two_ref, q_one, mixed_one, xg_ref, buf, sem = refs[-9:]
-    ct = buf.shape[3]
-    rows = slice(0, 2 * taps)
-
-    def finish_tile(tile):
-        at = columns(tile, ct)
-        one_ref[:, at] = gate(mixed_ref[:, at], mixed_one[:, at], q_one[:, at], at, spec_ref, fwd_ref, inv_ref)
-        two_ref[:, at] = gate(mixed_one[:, at], mixed_up_ref[:, at], q_up_ref[:, at], at, spec_ref, fwd_ref, inv_ref)
-
-    def use(tile, products, total):
-        at = columns(tile, ct)
-        finish_tile(jnp.maximum(tile - 1, 0))
-        query, mixed = streams(acc_ref, rows, at, products, ssq_ref[rows, :1] + total, d_model)
-        q_ref[:, at] = query[:taps]
-        q_one[:, at] = query[taps:]
-        mixed_ref[:, at] = mixed[:taps]
-        mixed_one[:, at] = mixed[taps:]
-
-    projection(first, places, tokens, gain_ref, weight_ref, xg_ref, buf, sem, use)
-    finish_tile(weight_ref.shape[2] // ct - 1)
+    wide = column_tile(channels, 1024)
+    for at in range(0, channels, wide):
+        at = slice(at, at + wide)
+        before = mixed_ref[:, at]
+        for row in range(0, mixed_rest.shape[0], taps):
+            rows = slice(row, row + taps)
+            now = mixed_rest[rows, at]
+            gated_ref[rows, at] = gate(before, now, q_rest[rows, at], at, spec_ref, fwd_ref, inv_ref)
+            before = now
 
 
 def first_kernel(halo_ref, mixed_ref, q_ref, spec_ref, fwd_ref, inv_ref, *refs):
@@ -192,17 +165,6 @@
     for at in range(0, q_ref.shape[1], ct):
         at = slice(at, at + ct)
         gated_ref[:, at] = gate(halo_ref[:, at], mixed_ref[:, at], q_ref[:, at], at, spec_ref, fwd_ref, inv_ref)
-
-
-def halves_kernel(x_ref, low_ref, high_ref, sem):
-    half = low_ref.shape[0]
-    copies = [
-        pltpu.make_async_copy(x_ref.at[pl.ds(half * i, half)], ref, sem.at[i]) for i, ref in enumerate((low_ref, high_ref))
-    ]
-    for copy in copies:
-        copy.start()
-    for copy in copies:
-        copy.wait()
 
 
 def params(mib, steps=1):
@@ -253,19 +215,6 @@
 BRIEF = pl.CostEstimate(flops=1, bytes_accessed=1, transcendentals=0)
 IN_PLACE = pl.BlockSpec(memory_space=pl.ANY)
 SCALARS = pl.BlockSpec(memory_space=pltpu.SMEM)
-
-
-def row_halves(x):
-    rows, width = x.shape
-    return pl.pallas_call(
-        halves_kernel,
-        in_specs=[IN_PLACE],
-        out_specs=[RESIDENT] * 2,
-        out_shape=[pltpu.VMEM((rows // 2, width), x.dtype)] * 2,
-        scratch_shapes=[pltpu.SemaphoreType.DMA((2,))],
-        compiler_params=pltpu.CompilerParams(vmem_limit_bytes=4 * MIB),
-        name="row_halves",
-    )(in_hbm(x))
 
 
 def filter_transform(filter_taps, conv_skip, of_filter, waits):
@@ -324,21 +273,20 @@
     )(places, in_hbm(own), in_vmem(beside), gain_rows(norm_gain, depth), in_hbm(in_weight), in_hbm(out_weight))
 
 
-def project_rest(kernel, name, lhs, places, first, norm_gain, in_weight, resident, estimate, d_model, taps, more):
+def project_last_part(lhs, places, first, norm_gain, in_weight, resident, d_model, taps):
     rows, depth = lhs[0].shape
     channels = in_weight.shape[2]
-    return pl.pallas_call(
-        functools.partial(kernel, first, d_model, taps, len(lhs)),
-        in_specs=[SCALARS]
-        + [RESIDENT] * (len(lhs) + 1)
-        + [IN_PLACE]
-        + [RESIDENT] * len(resident),
+    n = len(lhs)
+    rest = rows - taps
+    return pl.pallas_call(
+        functools.partial(last_kernel, first, d_model, taps, n),
+        in_specs=[SCALARS] + [RESIDENT] * (n + 1) + [IN_PLACE] + [RESIDENT] * len(resident),
         out_specs=[RESIDENT] * 4,
-        out_shape=[pltpu.VMEM((taps, channels), BF16)] * 4,
-        scratch_shapes=[pltpu.VMEM((taps, channels), BF16)] * more + weight_scratch(rows, depth, channels, len(lhs)),
-        compiler_params=weight_limit(rows, depth, channels, len(lhs), more * 2 * taps * channels),
-        cost_estimate=estimate,
-        name=name,
+        out_shape=[pltpu.VMEM((r, channels), BF16) for r in (taps, taps, taps, rest)],
+        scratch_shapes=[pltpu.VMEM((rest, channels), BF16)] * 2 + weight_scratch(rows, depth, channels, n),
+        compiler_params=weight_limit(rows, depth, channels, n, 4 * rest * channels),
+        cost_estimate=cost(rows, depth * n, 3 * channels),
+        name="project_last_part",
     )(
         places,
         *[in_vmem(x) for x in lhs],
@@ -361,72 +309,66 @@
     )(*[in_vmem(x) for x in (halo, mixed, query, spectrum, forward, inverse)], *waits)
 
 
-def out_kernel(n_parts, n_add, n_come, first, add_first, places, *refs):
-    parts, w_ref = refs[:n_parts], refs[n_parts]
-    add, come = refs[n_parts + 1 : n_parts + 1 + n_add], refs[n_parts + 1 + n_add : n_parts + 1 + n_add + n_come]
-    o_ref = refs[-1]
+def out_kernel(slices, n_add, first, add_first, places, *refs):
+    n = len(slices)
+    w_ref, add, o_ref = refs[n], refs[n + 1 : n + 1 + n_add], refs[-1]
     width = o_ref.shape[-1]
-    lhs = jnp.concatenate([p[...] for p in parts], axis=0)
-    for g in range(o_ref.shape[0] if len(o_ref.shape) == 3 else 1):
+    lhs = [ref[part] for ref, part in zip(refs[:n], slices)]
+    lhs = lhs[0] if n == 1 else jnp.concatenate(lhs, axis=0)
+    for g in range(o_ref.shape[0]):
         at = pl.ds(pl.multiple_of(places[first + g] * width, width), width)
         product = dot(lhs, w_ref[:, at])
         for x in add:
             product = product + x[add_first + g].astype(F32)
-        for x in come:
-            product = product + x[...].astype(F32)
-        if len(o_ref.shape) == 3:
-            o_ref[g] = product.astype(o_ref.dtype)
-        else:
-            o_ref[...] = product.astype(o_ref.dtype)
+        o_ref[g] = product.astype(o_ref.dtype)
 
 
 def project_out(parts, out_weight, places, first, n_groups, width, name, add=(), add_first=0, dtype=BF16, waits=()):
-    rows = sum(p.shape[0] for p in parts)
-    return pl.pallas_call(
-        functools.partial(out_kernel, len(parts), len(add), 0, first, add_first),
+    arrays, slices = zip(*parts)
+    rows = sum(part.stop - part.start for part in slices)
+    return pl.pallas_call(
+        functools.partial(out_kernel, slices, len(add), first, add_first),
         in_specs=[SCALARS] + [RESIDENT] * (len(parts) + 1 + len(add)) + [IN_PLACE] * len(waits),
         out_specs=RESIDENT,
         out_shape=pltpu.VMEM((n_groups, rows, width), dtype),
         compiler_params=pltpu.CompilerParams(vmem_limit_bytes=16 * MIB),
         cost_estimate=BRIEF,
         name=name,
-    )(places, *[in_vmem(x) for x in (*parts, out_weight, *add)], *waits)
-
-
-def project_last(parts, out_weight, places, first, width, name, add, add_first, come, part, n_parts):
-    rows = sum(p.shape[0] for p in parts)
-    return pl.pallas_call(
-        functools.partial(out_kernel, len(parts), len(add), len(come), first, add_first),
-        grid=(1,),
-        in_specs=[SCALARS] + [RESIDENT] * (len(parts) + 1 + len(add) + len(come)),
-        out_specs=pl.BlockSpec((rows, width), lambda i: (part, 0)),
-        out_shape=jax.ShapeDtypeStruct((rows * n_parts, width), BF16),
-        compiler_params=params(16),
+    )(places, *[in_vmem(x) for x in (*arrays, out_weight, *add)], *waits)
+
+
+def total_kernel(slices, n_come, first_row, *refs):
+    near, come = refs[: len(slices)], refs[len(slices) : len(slices) + n_come]
+    out_ref, held, sem = refs[-3:]
+    row = 0
+    for ref, part in zip(near, slices):
+        rows = slice(row, row + part.stop - part.start)
+        total = ref[0, part]
+        for x in come:
+            total = total + x[rows].astype(F32)
+        held[rows] = total.astype(BF16)
+        row = rows.stop
+    copy = pltpu.make_async_copy(held, out_ref.at[pl.ds(first_row, held.shape[0])], sem)
+    copy.start()
+    copy.wait()
+
+
+def total_rows(near, come, first_row, rows, into):
+    arrays, slices = zip(*near)
+    part, width = come[0].shape
+    given = [] if into is None else [into]
+    n = len(near) + len(come)
+    return pl.pallas_call(
+        functools.partial(total_kernel, slices, len(come), first_row),
+        in_specs=[RESIDENT] * n + [IN_PLACE] * len(given),
+        out_specs=IN_PLACE,
+        out_shape=jax.ShapeDtypeStruct((rows, width), BF16),
+        input_output_aliases={n: 0} if given else {},
+        scratch_shapes=[pltpu.VMEM((part, width), BF16), pltpu.SemaphoreType.DMA],
+        compiler_params=pltpu.CompilerParams(vmem_limit_bytes=8 * MIB),
         cost_estimate=BRIEF,
-        name=name,
-    )(places, *[in_vmem(x) for x in (*parts, out_weight, *add, *come)])
-
-
-def finish_kernel(n_come, *refs):
-    total = refs[0][0]
-    for x in refs[1 : 1 + n_come]:
-        total = total + x[...].astype(F32)
-    refs[-1][...] = total.astype(refs[-1].dtype)
-
-
-def finish(near, come, into, part):
-    rows, width = near.shape[1:]
-    return pl.pallas_call(
-        functools.partial(finish_kernel, len(come)),
-        grid=(1,),
-        in_specs=[RESIDENT] * (1 + len(come)) + [IN_PLACE],
-        out_specs=pl.BlockSpec((rows, width), lambda i: (part, 0)),
-        out_shape=jax.ShapeDtypeStruct(into.shape, BF16),
-        input_output_aliases={1 + len(come): 0},
-        compiler_params=params(16),
-        cost_estimate=BRIEF,
-        name="finish",
-    )(in_vmem(near), *[in_vmem(x) for x in come], into)
+        name="total_rows",
+    )(*[in_vmem(x) for x in (*arrays, *come)], *given)
 
 
 def on_device(tokens, norm_gain, in_weight, filter_taps, conv_skip, out_weight):
@@ -434,9 +376,8 @@
     r, c = lax.axis_index("trow"), lax.axis_index("tcol")
     rows, depth = tokens.shape
     taps = filter_taps.shape[0]
-    half = 2 * taps
     d_model = depth * n_row * n_col
-    assert n_row == 2 and rows == 2 * half
+    assert n_row == 2 and rows % taps == 0
     forward, inverse, of_filter = (jnp.asarray(m) for m in dft_matrices(taps))
 
     def other_core(x):
@@ -448,57 +389,50 @@
     def block_of(row, s):
         return row * n_col + lax.rem(c + s + n_col, n_col)
 
+    shifts = range(1, n_col)
+    n_far = n_col - 1
     beside = other_core(tokens)
-    low_rows, high_rows = row_halves(tokens)
-    upper_far = [chips_along(high_rows, s) for s in range(1, n_col)]
-    lower_far = [chips_along(low_rows, s) for s in range(1, n_col)]
-    shifts = range(1, n_col)
+    far = [chips_along(tokens, s) for s in shifts]
     places = jnp.stack(
         [block_of(r, 0), block_of(1 - r, 0)]
         + [block_of(row, -s) for row in (r, 1 - r) for s in shifts]
         + [block_of(row, s) for row in (1 - r, r) for s in (*shifts, 0)]
     )
-    n_far = n_col - 1
-    far_features, theirs_far = 2, 2 * n_col
+    theirs_far = 2 + 2 * n_far
     theirs_near, mine_far = theirs_far + n_far, theirs_far + n_col
     mine_near = mine_far + n_far
     acc, ssq, held_weight = project_local(tokens, beside, places, 0, norm_gain, in_weight, out_weight)
     spectrum = filter_transform(filter_taps, conv_skip, of_filter, [ssq])
-    rest = functools.partial(
-        project_rest, places=places, first=far_features, norm_gain=norm_gain, in_weight=in_weight, d_model=d_model, taps=taps
-    )
-    upper_far = [held_until(x, ssq) for x in upper_far]
-    resident = [acc, ssq, spectrum, forward, inverse]
-    upper = upper_far + [other_core(x) for x in upper_far]
-    tail, q_up, mixed_up, gated_up = rest(
-        upper_kernel, "project_upper", upper, resident=resident, estimate=BRIEF, more=1
+    far = [held_until(x, ssq) for x in far]
+    far = far + [other_core(x) for x in far]
+    tail, q_low, mixed_low, gated_rest = project_last_part(
+        far, places, 2, norm_gain, in_weight, [acc, ssq, spectrum, forward, inverse], d_model, taps
     )
     halo = lax.ppermute(tail, "seq", [(i, i + 1) for i in range(n_seq - 1)])
-    lower_far = [held_until(x, tail) for x in lower_far]
-    lower = lower_far + [other_core(x) for x in lower_far]
-    q_low, mixed_low, gated_one, gated_two = rest(
-        lower_kernel, "project_lower", lower, resident=resident + [q_up, mixed_up], estimate=cost(2 * taps, d_model, 3 * in_weight.shape[2]), more=2
-    )
-    gated_first = gate_first(halo, mixed_low, q_low, spectrum, forward, inverse, [])
-
-    project = functools.partial(project_out, [gated_two, gated_up], held_weight, places, width=depth)
-    far = other_core(project(theirs_far, n_far, name="up_theirs_far", waits=[gated_first]))
-    near = project(theirs_near, 1, name="up_theirs_near")
-    sent_up = project(mine_far, n_far, name="up_mine_far", add=[far], waits=[near])
-    near = other_core(near)
-    come_up = [chips_along(sent_up[s - 1], s) for s in shifts]
-
-    low = [gated_first, gated_one]
-    project = functools.partial(project_out, low, held_weight, places, width=depth)
-    theirs = other_core(project(theirs_far, n_col, name="low_theirs", waits=[sent_up]))
-    sent_low = project(mine_far, n_far, name="low_mine_far", add=[theirs])
-    come_low = [chips_along(sent_low[s - 1], s) for s in shifts]
-
-    out = project_last(
-        [gated_two, gated_up], held_weight, places, mine_near, depth, "up_mine_near", [near], 0, come_up, 1, 2
-    )
-    near_low = project(mine_near, 1, name="low_mine_near", add=[theirs], add_first=n_far, dtype=F32, waits=come_up)
-    return finish(near_low, come_low, out, 0)
+
+    project = functools.partial(project_out, out_weight=held_weight, places=places, width=depth)
+
+    half = rows // 2
+    rest = [(gated_rest, slice(0, rows - taps))]
+    theirs = other_core(project(rest, first=theirs_far, n_groups=n_far, name="rest_theirs_far"))
+    sent = project(rest, first=mine_far, n_groups=n_far, name="rest_mine_far", add=[theirs])
+    come = [chips_along(sent[s - 1], s) for s in shifts]
+
+    gated_first = gate_first(halo, mixed_low, q_low, spectrum, forward, inverse, [sent])
+    only = [(gated_first, slice(0, taps))]
+    theirs = other_core(project(only, first=theirs_far, n_groups=n_far, name="first_theirs_far"))
+    sent_first = project(only, first=mine_far, n_groups=n_far, name="first_mine_far", add=[theirs])
+    come_first = [chips_along(sent_first[s - 1], s) for s in shifts]
+
+    upper = [(gated_rest, slice(half - taps, rows - taps))]
+    lower = only + [(gated_rest, slice(0, half - taps))]
+    near = []
+    for part, name in ((lower, "lower"), (upper, "upper")):
+        theirs = other_core(project(part, first=theirs_near, n_groups=1, name=name + "_theirs_near"))
+        near.append(project(part, first=mine_near, n_groups=1, name=name + "_mine_near", add=[theirs], dtype=F32))
+
+    out = total_rows([(near[0], slice(taps, half)), (near[1], slice(0, rows - half))], come, taps, rows, None)
+    return total_rows([(near[0], slice(0, taps))], come_first, 0, rows, out)
 
 
 def solution(mesh):

time: 94 us -> 86.5 us (0.920)
  Pallas kernels: 64.8 us -> 58 us
  waiting for transfers between devices: 17.9 us -> 14.3 us
  local copies, waits for them, and re-layouts: 0.1 us -> 2.28 us
    ppermute x4 -> x3, waiting for transfers between devices: 16.3 us -> 6.31 us  [chips_along(): return lax.ppermute(x, 'tcol', [(i, (i + s) % n_col) for i in range(n_col)])]
    pallas_call x11, Pallas kernels: 44 us -> 37.3 us  [the longest x1 21 us: project_last_part(): pl.pallas_call(functools.partial(last_kernel, first, d_model, taps, n), i...]
    ppermute x1, waiting for transfers between devices: 0.01 us -> 5.71 us  [on_device(): halo = lax.ppermute(tail, 'seq', [(i, i + 1) for i in range(n_seq - 1)])]
    unnamed x4 -> x8, local copies, waits for them, and re-layouts: 0.01 us -> 2.2 us
    ppermute x4 -> x3, starting transfers between devices: 5.29 us -> 5.69 us  [chips_along(): return lax.ppermute(x, 'tcol', [(i, (i + s) % n_col) for i in range(n_col)])]
  transfers between devices with their start and end apart: 11 -> 10, of which waited for: 3 -> 5; matrix products, arithmetic and copies ran while one was open for 0% -> 0% of each run, Pallas kernels for 60% -> 40%
where the time goes in v3:
time: 86.5 us; the launch traced here: 85.9 us
  Pallas kernels  58 us (67%)
  waiting for transfers between devices  14.3 us (17%)
  starting transfers between devices  10.9 us (13%)
  local copies, waits for them, and re-layouts  2.28 us (3%)
    pallas_call x1, Pallas kernels, project_last_part(): pl.pallas_call(functools.partial(last_kernel, first, d_model, taps, n), i...  21 us
    pallas_call x1, Pallas kernels, project_local(): pl.pallas_call(functools.partial(local_kernel, first), in_specs=[SCALARS,...  17.7 us
    pallas_call x8, Pallas kernels, project_out(): pl.pallas_call(functools.partial(out_kernel, slices, len(add), first, add...  14.5 us
    ppermute x3, waiting for transfers between devices, chips_along(): return lax.ppermute(x, 'tcol', [(i, (i + s) % n_col) for i in range(n_col)])  6.31 us
    ppermute x1, waiting for transfers between devices, on_device(): halo = lax.ppermute(tail, 'seq', [(i, i + 1) for i in range(n_seq - 1)])  5.71 us
    ppermute x3, starting transfers between devices, chips_along(): return lax.ppermute(x, 'tcol', [(i, (i + s) % n_col) for i in range(n_col)])  5.69 us
    ppermute x1, starting transfers between devices, on_device(): halo = lax.ppermute(tail, 'seq', [(i, i + 1) for i in range(n_seq - 1)])  3.84 us
    ppermute x6, waiting for transfers between devices, other_core(): return lax.ppermute(x, 'trow', [(0, 1), (1, 0)])  2.31 us
  transfers between devices with their start and end apart: 10, of which 5 were waited for; matrix products, arithmetic and copies ran while one was open for 0% of the time, Pallas kernels for 40%

profile of v3, /device:TPU:0, one launch (start us, length us, event | category | flops | bytes accessed | tf_op | source)
XLA Modules:
  0.0 85.9 jit_solution(13386687695193287293)
XLA Ops:
  0.5 2.5 %collective-permute-start = (bf16[512,1024]{1,0:T(8,128)(2,1)}, bf16[512,1024]{1,0:T(8,128)(2,1)}, u32[]{:S(2)}, u32[]{:S(2)}) collective-permute-start(bf16[512,1024]{1,0:T(8,128)(2,1)} %own_ref.1), channel_id=1, source_target_pairs={{0,1},{1,0},{2,3},{3,2},{4,5},{5,4},{6,7},{7,6},{8,9},{9,8},{10,11... | collective-permute-start | bytes 3145736 | tf_op jit(solution)/shard_map/ppermute | solution.py:387
  3.1 1.0 %copy-done = bf16[512,1024]{1,0:T(8,128)(2,1)} copy-done((bf16[512,1024]{1,0:T(8,128)(2,1)}, bf16[512,1024]{1,0:T(8,128)(2,1)S(1)}, u32[]{:S(2)}) %copy-start) | copy-done | bytes 1048600
  4.0 1.2 %copy-done.1 = bf16[512,1024]{1,0:T(8,128)(2,1)S(1)} copy-done((bf16[512,1024]{1,0:T(8,128)(2,1)S(1)}, bf16[512,1024]{1,0:T(8,128)(2,1)}, u32[]{:S(2)}) %copy-start.1) | copy-done | bytes 1048600
  5.3 17.7 %project_local.1 = (bf16[3,512,2048]{2,1,0:T(8,128)(2,1)S(1)}, f32[512,128]{1,0:T(8,128)S(1)}, bf16[2048,4096]{1,0:T(8,128)(2,1)S(1)}) custom-call(s32[8]{0:T(128)S(1)} %stack.29.places, bf16[512,1024]{1,0:T(8,128)(2,1)} %own_ref.1, bf16[512,1024]{1,0:T(8,128)(2,1)S(1)} %copy-done.1, f32[4,1,1024]{2,1,0:T(1,128)} %bitcast.12, ...), custom_call_target="tpu_custom_call" | custom-call | flops 12884901888 | bytes 27262976 | tf_op jit(solution)/shard_map/project_local/pallas_call | solution.py:258
  23.0 4.1 %collective-permute-done.refs_0_ = bf16[512,1024]{1,0:T(8,128)(2,1)} collective-permute-done((bf16[512,1024]{1,0:T(8,128)(2,1)}, bf16[512,1024]{1,0:T(8,128)(2,1)}, u32[]{:S(2)}, u32[]{:S(2)}) %collective-permute-start) | collective-permute-done | bytes 1048608 | tf_op jit(solution)/shard_map/ppermute | solution.py:387
  27.1 2.1 %filter_transform.1.refs_6_.spec_ref = f32[384,2048]{1,0:T(8,128)S(1)} custom-call(f32[128,2048]{1,0:T(8,128)} %taps_ref.1, f32[1,2048]{1,0:T(1,128)} %bitcast.14, bf16[384,256]{1,0:T(8,128)(2,1)} %constant.29.clone.of_filter_ref, f32[512,128]{1,0:T(8,128)S(1)} %get-tuple-element.12.refs_1_.refs_0_.refs_5_), custom_call_target="tpu_custom_call" | custom-call | flops 402653184 | bytes 1245184 | tf_op jit(solution)/shard_map/filter_transform/pallas_call | solution.py:224
  29.2 0.8 collective-permute-done.2.refs_1_
  30.0 21.0 %project_last_part.1 = (bf16[128,2048]{1,0:T(8,128)(2,1)S(1)}, bf16[128,2048]{1,0:T(8,128)(2,1)S(1)}, bf16[128,2048]{1,0:T(8,128)(2,1)S(1)}, bf16[384,2048]{1,0:T(8,128)(2,1)S(1)}) custom-call(s32[8]{0:T(128)S(1)} %stack.29.places, bf16[512,1024]{1,0:T(8,128)(2,1)} %held_until.1.refs_0_, bf16[512,1024]{1,0:T(8,128)(2,1)S(1)} %collective-permute-done.2.refs_1_, ...), custom_call_target="tpu_custom_call" | custom-call | flops 12884901888 | bytes 27262976 | tf_op jit(solution)/shard_map/project_last_part/pallas_call | solution.py:281
  51.0 2.3 %rest_theirs_far.1 = bf16[1,384,1024]{2,1,0:T(8,128)(2,1)S(1)} custom-call(s32[8]{0:T(128)S(1)} %stack.29.places, bf16[384,2048]{1,0:T(8,128)(2,1)S(1)} %get-tuple-element.17.refs_0_.refs_1_, bf16[2048,4096]{1,0:T(8,128)(2,1)S(1)} %get-tuple-element.18.refs_1_.refs_2_), custom_call_target="tpu_custom_call" | custom-call | flops 1 | bytes 1 | tf_op jit(solution)/shard_map/rest_theirs_far/pallas_call | solution.py:329
  53.5 3.8 %collective-permute-start.3 = (bf16[128,2048]{1,0:T(8,128)(2,1)S(1)}, bf16[128,2048]{1,0:T(8,128)(2,1)S(1)}, u32[]{:S(2)}, u32[]{:S(2)}) collective-permute-start(bf16[128,2048]{1,0:T(8,128)(2,1)S(1)} %get-tuple-element.14), channel_id=1, source_target_pairs={{0,4},{4,8},{8,12},{12,16},{16,20},{20,24},{24,28},{1,5},{5,9},{9,... | collective-permute-start | bytes 1572872 | tf_op jit(solution)/shard_map/ppermute | solution.py:411
  57.4 2.4 %rest_mine_far.1.refs_0_ = bf16[1,384,1024]{2,1,0:T(8,128)(2,1)S(1)} custom-call(s32[8]{0:T(128)S(1)} %stack.29.places, bf16[384,2048]{1,0:T(8,128)(2,1)S(1)} %get-tuple-element.17.refs_0_.refs_1_, bf16[2048,4096]{1,0:T(8,128)(2,1)S(1)} %get-tuple-element.18.refs_1_.refs_2_, bf16[1,384,1024]{2,1,0:T(8,128)(2,1)S(1)} %collective-permute-done.4.refs_2_), custom_call_target="tpu_custom_call" | custom-call | flops 1 | bytes 1 | tf_op jit(solution)/shard_map/rest_mine_far/pallas_call | solution.py:329
  59.8 1.6 %collective-permute-start.9 = (bf16[384,1024]{1,0:T(8,128)(2,1)S(1)}, bf16[384,1024]{1,0:T(8,128)(2,1)S(1)}, u32[]{:S(2)}, u32[]{:S(2)}) collective-permute-start(bf16[384,1024]{1,0:T(8,128)(2,1)S(1)} %bitcast.10), channel_id=1, source_target_pairs={{0,1},{1,0},{2,3},{3,2},{4,5},{5,4},{6,7},{7,6},{8,9},{9,8},{10,11... | collective-permute-start | bytes 2359304 | tf_op jit(solution)/shard_map/ppermute | solution.py:387
  61.3 1.8 %upper_theirs_near.1 = bf16[1,256,1024]{2,1,0:T(8,128)(2,1)S(1)} custom-call(s32[8]{0:T(128)S(1)} %stack.29.places, bf16[384,2048]{1,0:T(8,128)(2,1)S(1)} %get-tuple-element.17.refs_0_.refs_1_, bf16[2048,4096]{1,0:T(8,128)(2,1)S(1)} %get-tuple-element.18.refs_1_.refs_2_), custom_call_target="tpu_custom_call" | custom-call | flops 1 | bytes 1 | tf_op jit(solution)/shard_map/upper_theirs_near/pallas_call | solution.py:329
  63.1 5.7 %collective-permute-done.3.halo_ref = bf16[128,2048]{1,0:T(8,128)(2,1)S(1)} collective-permute-done((bf16[128,2048]{1,0:T(8,128)(2,1)S(1)}, bf16[128,2048]{1,0:T(8,128)(2,1)S(1)}, u32[]{:S(2)}, u32[]{:S(2)}) %collective-permute-start.3) | collective-permute-done | bytes 524320 | tf_op jit(solution)/shard_map/ppermute | solution.py:411
  68.8 1.0 %gate_first.1.refs_0_ = bf16[128,2048]{1,0:T(8,128)(2,1)S(1)} custom-call(bf16[128,2048]{1,0:T(8,128)(2,1)S(1)} %collective-permute-done.3.halo_ref, bf16[128,2048]{1,0:T(8,128)(2,1)S(1)} %get-tuple-element.15.mixed_ref, bf16[128,2048]{1,0:T(8,128)(2,1)S(1)} %get-tuple-element.16.q_ref, f32[384,2048]{1,0:T(8,128)S(1)} %filter_transform.1.refs_6_.spec_ref, ...), custom_call_target="tpu_custom_call" | custom-call | flops 1 | bytes 1 | tf_op jit(solution)/shard_map/gate_first/pallas_call | solution.py:301
  69.9 1.8 %lower_theirs_near.1 = bf16[1,256,1024]{2,1,0:T(8,128)(2,1)S(1)} custom-call(s32[8]{0:T(128)S(1)} %stack.29.places, bf16[128,2048]{1,0:T(8,128)(2,1)S(1)} %gate_first.1.refs_0_, bf16[384,2048]{1,0:T(8,128)(2,1)S(1)} %get-tuple-element.17.refs_0_.refs_1_, bf16[2048,4096]{1,0:T(8,128)(2,1)S(1)} %get-tuple-element.18.refs_1_.refs_2_), custom_call_target="tpu_custom_call" | custom-call | flops 1 | bytes 1 | tf_op jit(solution)/shard_map/lower_theirs_near/pallas_call | solution.py:329
  72.3 1.3 %first_theirs_far.1 = bf16[1,128,1024]{2,1,0:T(8,128)(2,1)S(1)} custom-call(s32[8]{0:T(128)S(1)} %stack.29.places, bf16[128,2048]{1,0:T(8,128)(2,1)S(1)} %gate_first.1.refs_0_, bf16[2048,4096]{1,0:T(8,128)(2,1)S(1)} %get-tuple-element.18.refs_1_.refs_2_), custom_call_target="tpu_custom_call" | custom-call | flops 1 | bytes 1 | tf_op jit(solution)/shard_map/first_theirs_far/pallas_call | solution.py:329
  73.7 1.5 %collective-permute-done.6.refs_2_ = bf16[1,128,1024]{2,1,0:T(8,128)(2,1)S(1)} collective-permute-done((bf16[1,128,1024]{2,1,0:T(8,128)(2,1)S(1)}, bf16[1,128,1024]{2,1,0:T(8,128)(2,1)S(1)}, u32[]{:S(2)}, u32[]{:S(2)}) %collective-permute-start.6) | collective-permute-done | bytes 262176 | tf_op jit(solution)/shard_map/ppermute | solution.py:384
  75.2 1.3 %first_mine_far.1 = bf16[1,128,1024]{2,1,0:T(8,128)(2,1)S(1)} custom-call(s32[8]{0:T(128)S(1)} %stack.29.places, bf16[128,2048]{1,0:T(8,128)(2,1)S(1)} %gate_first.1.refs_0_, bf16[2048,4096]{1,0:T(8,128)(2,1)S(1)} %get-tuple-element.18.refs_1_.refs_2_, bf16[1,128,1024]{2,1,0:T(8,128)(2,1)S(1)} %collective-permute-done.6.refs_2_), custom_call_target="tpu_custom_call" | custom-call | flops 1 | bytes 1 | tf_op jit(solution)/shard_map/first_mine_far/pallas_call | solution.py:329
  76.5 1.6 %collective-permute-start.7 = (bf16[128,1024]{1,0:T(8,128)(2,1)S(1)}, bf16[128,1024]{1,0:T(8,128)(2,1)S(1)}, u32[]{:S(2)}, u32[]{:S(2)}) collective-permute-start(bf16[128,1024]{1,0:T(8,128)(2,1)S(1)} %bitcast.11), channel_id=1, source_target_pairs={{0,1},{1,0},{2,3},{3,2},{4,5},{5,4},{6,7},{7,6},{8,9},{9,8},{10,11... | collective-permute-start | bytes 786440 | tf_op jit(solution)/shard_map/ppermute | solution.py:387
  78.1 1.8 %upper_mine_near.1.refs_1_ = f32[1,256,1024]{2,1,0:T(8,128)S(1)} custom-call(s32[8]{0:T(128)S(1)} %stack.29.places, bf16[384,2048]{1,0:T(8,128)(2,1)S(1)} %get-tuple-element.17.refs_0_.refs_1_, bf16[2048,4096]{1,0:T(8,128)(2,1)S(1)} %get-tuple-element.18.refs_1_.refs_2_, bf16[1,256,1024]{2,1,0:T(8,128)(2,1)S(1)} %collective-permute-done.8.refs_2_), custom_call_target="tpu_custom_call" | custom-call | flops 1 | bytes 1 | tf_op jit(solution)/shard_map/upper_mine_near/pallas_call | solution.py:329
  79.9 1.8 %lower_mine_near.1.refs_0_ = f32[1,256,1024]{2,1,0:T(8,128)S(1)} custom-call(s32[8]{0:T(128)S(1)} %stack.29.places, bf16[128,2048]{1,0:T(8,128)(2,1)S(1)} %gate_first.1.refs_0_, bf16[384,2048]{1,0:T(8,128)(2,1)S(1)} %get-tuple-element.17.refs_0_.refs_1_, bf16[2048,4096]{1,0:T(8,128)(2,1)S(1)} %get-tuple-element.18.refs_1_.refs_2_, ...), custom_call_target="tpu_custom_call" | custom-call | flops 1 | bytes 1 | tf_op jit(solution)/shard_map/lower_mine_near/pallas_call | solution.py:329
  81.7 1.0 %total_rows.2.refs_2_ = bf16[512,1024]{1,0:T(8,128)(2,1)} custom-call(f32[1,256,1024]{2,1,0:T(8,128)S(1)} %lower_mine_near.1.refs_0_, f32[1,256,1024]{2,1,0:T(8,128)S(1)} %upper_mine_near.1.refs_1_, bf16[384,1024]{1,0:T(8,128)(2,1)S(1)} %collective-permute-done.9.refs_2_), custom_call_target="tpu_custom_call" | custom-call | flops 1 | bytes 1 | tf_op jit(solution)/shard_map/total_rows/pallas_call | solution.py:361
  82.8 2.2 %collective-permute-done.7.refs_1_ = bf16[128,1024]{1,0:T(8,128)(2,1)S(1)} collective-permute-done((bf16[128,1024]{1,0:T(8,128)(2,1)S(1)}, bf16[128,1024]{1,0:T(8,128)(2,1)S(1)}, u32[]{:S(2)}, u32[]{:S(2)}) %collective-permute-start.7) | collective-permute-done | bytes 262176 | tf_op jit(solution)/shard_map/ppermute | solution.py:387
  (20 shorter events, 2.2 us)
Async XLA Ops:
  0.0 3.1 %collective-permute-start.1 = (bf16[512,1024]{1,0:T(8,128)(2,1)}, bf16[512,1024]{1,0:T(8,128)(2,1)S(1)}, u32[]{:S(2)}, u32[]{:S(2)}) collective-permute-start(bf16[512,1024]{1,0:T(8,128)(2,1)} %own_ref.1), channel_id=1, source_target_pairs={{0,2},{2,0},{1,3},{3,1},{4,6},{6,4},{5,7},{7,5},{8,10},{10,8},{9,1... | collective-permute-start | bytes 3145736 | tf_op jit(solution)/shard_map/ppermute | solution.py:384
  0.5 26.7 %collective-permute-start = (bf16[512,1024]{1,0:T(8,128)(2,1)}, bf16[512,1024]{1,0:T(8,128)(2,1)}, u32[]{:S(2)}, u32[]{:S(2)}) collective-permute-start(bf16[512,1024]{1,0:T(8,128)(2,1)} %own_ref.1), channel_id=1, source_target_pairs={{0,1},{1,0},{2,3},{3,2},{4,5},{5,4},{6,7},{7,6},{8,9},{9,8},{10,11... | collective-permute-start | bytes 3145736 | tf_op jit(solution)/shard_map/ppermute | solution.py:387
  3.1 1.0 %copy-start = (bf16[512,1024]{1,0:T(8,128)(2,1)}, bf16[512,1024]{1,0:T(8,128)(2,1)S(1)}, u32[]{:S(2)}) copy-start(bf16[512,1024]{1,0:T(8,128)(2,1)S(1)} %collective-permute-done.1.beside_ref) | copy-start | bytes 3145732
  4.0 1.2 %copy-start.1 = (bf16[512,1024]{1,0:T(8,128)(2,1)S(1)}, bf16[512,1024]{1,0:T(8,128)(2,1)}, u32[]{:S(2)}) copy-start(bf16[512,1024]{1,0:T(8,128)(2,1)} %copy-done) | copy-start | bytes 3145732
  5.3 24.7 %copy-start.2 = (bf16[256,256]{1,0:T(8,128)(2,1)S(1)}, bf16[256,256]{1,0:T(8,128)(2,1)}, u32[]{:S(2)}) copy-start(bf16[256,256]{1,0:T(8,128)(2,1)} %constant.27.clone.refs_7_.fwd_ref) | copy-start | bytes 393220
  5.3 24.7 %copy-start.3 = (bf16[128,256]{1,0:T(8,128)(2,1)S(1)}, bf16[128,256]{1,0:T(8,128)(2,1)}, u32[]{:S(2)}) copy-start(bf16[128,256]{1,0:T(8,128)(2,1)} %constant.28.clone.refs_8_.inv_ref) | copy-start | bytes 196612
  27.1 2.9 %collective-permute-start.2 = (bf16[512,1024]{1,0:T(8,128)(2,1)}, bf16[512,1024]{1,0:T(8,128)(2,1)S(1)}, u32[]{:S(2)}, u32[]{:S(2)}) collective-permute-start(bf16[512,1024]{1,0:T(8,128)(2,1)} %held_until.1.refs_0_), channel_id=1, source_target_pairs={{0,2},{2,0},{1,3},{3,1},{4,6},{6,4},{5,7},{7,5},{8,10},{10,8},{9,1... | collective-permute-start | bytes 3145736 | tf_op jit(solution)/shard_map/ppermute | solution.py:384
  53.3 4.0 %collective-permute-start.4 = (bf16[1,384,1024]{2,1,0:T(8,128)(2,1)S(1)}, bf16[1,384,1024]{2,1,0:T(8,128)(2,1)S(1)}, u32[]{:S(2)}, u32[]{:S(2)}) collective-permute-start(bf16[1,384,1024]{2,1,0:T(8,128)(2,1)S(1)} %rest_theirs_far.1), channel_id=1, source_target_pairs={{0,2},{2,0},{1,3},{3,1},{4,6},{6,4},{5,7},{7,5},{8,10},{10,8},{9,1... | collective-permute-start | bytes 2359304 | tf_op jit(solution)/shard_map/ppermute | solution.py:384
  53.5 15.3 %collective-permute-start.3 = (bf16[128,2048]{1,0:T(8,128)(2,1)S(1)}, bf16[128,2048]{1,0:T(8,128)(2,1)S(1)}, u32[]{:S(2)}, u32[]{:S(2)}) collective-permute-start(bf16[128,2048]{1,0:T(8,128)(2,1)S(1)} %get-tuple-element.14), channel_id=1, source_target_pairs={{0,4},{4,8},{8,12},{12,16},{16,20},{20,24},{24,28},{1,5},{5,9},{9,... | collective-permute-start | bytes 1572872 | tf_op jit(solution)/shard_map/ppermute | solution.py:411
  59.8 22.0 %collective-permute-start.9 = (bf16[384,1024]{1,0:T(8,128)(2,1)S(1)}, bf16[384,1024]{1,0:T(8,128)(2,1)S(1)}, u32[]{:S(2)}, u32[]{:S(2)}) collective-permute-start(bf16[384,1024]{1,0:T(8,128)(2,1)S(1)} %bitcast.10), channel_id=1, source_target_pairs={{0,1},{1,0},{2,3},{3,2},{4,5},{5,4},{6,7},{7,6},{8,9},{9,8},{10,11... | collective-permute-start | bytes 2359304 | tf_op jit(solution)/shard_map/ppermute | solution.py:387
  69.9 8.2 %collective-permute-start.8 = (bf16[1,256,1024]{2,1,0:T(8,128)(2,1)S(1)}, bf16[1,256,1024]{2,1,0:T(8,128)(2,1)S(1)}, u32[]{:S(2)}, u32[]{:S(2)}) collective-permute-start(bf16[1,256,1024]{2,1,0:T(8,128)(2,1)S(1)} %upper_theirs_near.1), channel_id=1, source_target_pairs={{0,2},{2,0},{1,3},{3,1},{4,6},{6,4},{5,7},{7,5},{8,10},{10,8},{9,1... | collective-permute-start | bytes 1572872 | tf_op jit(solution)/shard_map/ppermute | solution.py:384
  71.8 8.1 %collective-permute-start.5 = (bf16[1,256,1024]{2,1,0:T(8,128)(2,1)S(1)}, bf16[1,256,1024]{2,1,0:T(8,128)(2,1)S(1)}, u32[]{:S(2)}, u32[]{:S(2)}) collective-permute-start(bf16[1,256,1024]{2,1,0:T(8,128)(2,1)S(1)} %lower_theirs_near.1), channel_id=1, source_target_pairs={{0,2},{2,0},{1,3},{3,1},{4,6},{6,4},{5,7},{7,5},{8,10},{10,8},{9,1... | collective-permute-start | bytes 1572872 | tf_op jit(solution)/shard_map/ppermute | solution.py:384
  73.6 1.6 %collective-permute-start.6 = (bf16[1,128,1024]{2,1,0:T(8,128)(2,1)S(1)}, bf16[1,128,1024]{2,1,0:T(8,128)(2,1)S(1)}, u32[]{:S(2)}, u32[]{:S(2)}) collective-permute-start(bf16[1,128,1024]{2,1,0:T(8,128)(2,1)S(1)} %first_theirs_far.1), channel_id=1, source_target_pairs={{0,2},{2,0},{1,3},{3,1},{4,6},{6,4},{5,7},{7,5},{8,10},{10,8},{9,1... | collective-permute-start | bytes 786440 | tf_op jit(solution)/shard_map/ppermute | solution.py:384
  76.5 8.5 %collective-permute-start.7 = (bf16[128,1024]{1,0:T(8,128)(2,1)S(1)}, bf16[128,1024]{1,0:T(8,128)(2,1)S(1)}, u32[]{:S(2)}, u32[]{:S(2)}) collective-permute-start(bf16[128,1024]{1,0:T(8,128)(2,1)S(1)} %bitcast.11), channel_id=1, source_target_pairs={{0,1},{1,0},{2,3},{3,2},{4,5},{5,4},{6,7},{7,6},{8,9},{9,8},{10,11... | collective-permute-start | bytes 786440 | tf_op jit(solution)/shard_map/ppermute | solution.py:387

commit v4 on v3

v4 whole, which is shorter than its diff:
```python
import functools

import jax
import jax.numpy as jnp
import numpy as np
from jax import lax
from jax.experimental import pallas as pl
from jax.experimental.pallas import tpu as pltpu
from jax.sharding import PartitionSpec as P

BF16 = jnp.bfloat16
F32 = jnp.float32
MIB = 1024 * 1024


def dft_matrices(taps):
    size = 2 * taps
    t = np.arange(size)[None, :]
    k = np.arange(taps)[:, None]
    angle = 2.0 * np.pi * ((k * t) % size) / size
    cos, sin = np.cos(angle), np.sin(angle)
    alternating = (-1.0) ** t
    forward = np.concatenate([cos, alternating, -sin[1:]], axis=0)
    inverse = np.concatenate([cos[:1], 2.0 * cos[1:], alternating, -2.0 * sin[1:]], axis=0).T / size
    short = slice(0, taps)
    of_filter = np.concatenate(
        [cos[:, short], 0.0 * sin[:1, short], -sin[1:, short], alternating[:, short], cos[1:, short]], axis=0
    )
    of_filter = np.concatenate([of_filter, of_filter], axis=1)
    return forward.astype(BF16), inverse[taps:].astype(BF16), of_filter.astype(BF16)


def dot(a, b):
    return jnp.dot(a, b, preferred_element_type=F32)


def convolved(window, spectrum, forward, inverse):
    half = window.shape[0] // 2
    x = dot(forward, window)
    xa, xb = x[:half], x[half:]
    ha, hb, hc = spectrum[:half], spectrum[half : 2 * half], spectrum[2 * half :]
    y = jnp.concatenate([xa * ha - xb * hb, xa * hb + xb * hc], axis=0)
    return dot(inverse, y.astype(BF16))


def columns(step, ct):
    return pl.ds(pl.multiple_of(step * ct, ct), ct)


SLOTS = 3


def weight_copies(first, depth, count, places, weight_ref, ring_ref, sem, tile):
    ct = ring_ref.shape[3]
    slot = lax.rem(tile, SLOTS)
    return [
        pltpu.make_async_copy(
            weight_ref.at[:, pl.ds(pl.multiple_of(places[first + i] * depth, depth), depth), columns(tile, ct)],
            ring_ref.at[slot, :, pl.ds(i * depth, depth)],
            sem.at[slot, i],
        )
        for i in range(count)
    ]


def scaled(x_ref, gain, xg_ref, at):
    x = x_ref[...].astype(F32)
    xg_ref[:, at] = (x * gain).astype(BF16)
    return jnp.sum(x * x, axis=1, keepdims=True)


def products(copies, tiles, xg_ref, ring_ref, loaded, use):
    ahead = min(SLOTS - 1, tiles)

    def step(tile, _):
        @pl.when(tile + ahead < tiles)
        def _():
            for copy in copies(tile + ahead):
                copy.start()

        @pl.when(tile >= loaded)
        def _():
            for copy in copies(tile):
                copy.wait()

        slot = lax.rem(tile, SLOTS)
        use(tile, [dot(xg_ref[...], ring_ref[slot, j]) for j in range(3)])
        return 0

    lax.fori_loop(0, tiles, step, 0)


def local_kernel(first, places, own_ref, beside_ref, gain_ref, weight_ref, out_w_ref, acc_ref, ssq_ref, held_w_ref,
                 own_held, xg_ref, ring_ref, sem, own_sem, out_sem):
    ct, depth = ring_ref.shape[3], own_ref.shape[1]
    tiles = weight_ref.shape[2] // ct
    piece = out_w_ref.shape[0] // tiles
    copies = functools.partial(weight_copies, first, depth, 2, places, weight_ref, ring_ref, sem)

    def piece_copy(tile):
        rows = pl.ds(pl.multiple_of(tile * piece, piece), piece)
        return pltpu.make_async_copy(out_w_ref.at[rows], held_w_ref.at[rows], out_sem.at[tile])

    def use(tile, streams):
        piece_copy(tile).start()
        for j in range(3):
            acc_ref[j, :, columns(tile, ct)] = streams[j].astype(BF16)

    load = pltpu.make_async_copy(own_ref, own_held, own_sem)
    load.start()
    for tile in range(min(SLOTS - 1, tiles)):
        for copy in copies(tile):
            copy.start()
    total = scaled(beside_ref, gain_ref[places[first + 1]], xg_ref, slice(depth, 2 * depth))
    load.wait()
    total = total + scaled(own_held, gain_ref[places[first]], xg_ref, slice(0, depth))
    ssq_ref[...] = jnp.broadcast_to(total, ssq_ref.shape)
    products(copies, tiles, xg_ref, ring_ref, 0, use)
    for tile in range(tiles):
        piece_copy(tile).wait()


def ready_kernel(first, depth, count, places, taps_ref, skip_ref, of_filter_ref, weight_ref, _, spec_ref, ring_ref,
                 taps_held, taps_sem, sem):
    load = pltpu.make_async_copy(taps_ref, taps_held, taps_sem)
    load.start()
    tiles = weight_ref.shape[2] // ring_ref.shape[3]
    copies = functools.partial(weight_copies, first, depth, count, places, weight_ref, ring_ref, sem)
    ahead = min(SLOTS - 1, tiles)
    for tile in range(ahead):
        for copy in copies(tile):
            copy.start()
    load.wait()
    channels = taps_ref.shape[1]
    wide = column_tile(channels, 512)
    for at in range(0, channels, wide):
        at = slice(at, at + wide)
        h = taps_held[:, at]
        at_first = lax.broadcasted_iota(jnp.int32, h.shape, 0) == 0
        h = h + jnp.where(at_first, skip_ref[:, at], 0.0)
        high = h.astype(BF16)
        low = (h - high.astype(F32)).astype(BF16)
        spec_ref[:, at] = dot(of_filter_ref[...], jnp.concatenate([high, low], axis=0))
    for tile in range(ahead):
        for copy in copies(tile):
            copy.wait()


def scaled_kernel(first, n_lhs, places, *refs):
    tokens = refs[:n_lhs]
    gain_ref, ssq_in_ref, xg_ref, ssq_ref = refs[n_lhs:]
    depth = tokens[0].shape[1]
    total = ssq_in_ref[...]
    for i, x_ref in enumerate(tokens):
        total = total + scaled(x_ref, gain_ref[places[first + i]], xg_ref, slice(i * depth, (i + 1) * depth))
    ssq_ref[...] = total


def gate(before, now, query, at, spec_ref, fwd_ref, inv_ref):
    window = jnp.concatenate([before, now], axis=0)
    filtered = convolved(window, spec_ref[:, at], fwd_ref[...], inv_ref[...])
    return (query.astype(F32) * filtered).astype(BF16)


def last_kernel(first, d_model, taps, n_lhs, places, *refs):
    tokens = refs[:n_lhs]
    gain_ref, weight_ref, acc_ref, ssq_ref, spec_ref, fwd_ref, inv_ref, _, _ = refs[n_lhs : n_lhs + 9]
    tail_ref, q_ref, mixed_ref, gated_ref, xg_ref, ring_ref, q_rest, mixed_rest, sem = refs[n_lhs + 9 :]
    channels, ct = weight_ref.shape[2], ring_ref.shape[3]
    tiles = channels // ct
    depth = tokens[0].shape[1]
    copies = functools.partial(weight_copies, first, depth, 2 * n_lhs, places, weight_ref, ring_ref, sem)

    total = ssq_ref[:, :1]
    for i, x_ref in enumerate(tokens, n_lhs):
        total = total + scaled(x_ref, gain_ref[places[first + i]], xg_ref, slice(i * depth, (i + 1) * depth))
    scale = lax.rsqrt(total / d_model + 1e-06)

    def use(tile, streams):
        at = columns(tile, ct)
        query, keys, values = [((acc_ref[j, :, at].astype(F32) + streams[j]) * scale).astype(BF16) for j in range(3)]
        mixed = (keys.astype(F32) * values.astype(F32)).astype(BF16)
        q_ref[:, at] = query[:taps]
        q_rest[:, at] = query[taps:]
        mixed_ref[:, at] = mixed[:taps]
        mixed_rest[:, at] = mixed[taps:]
        tail_ref[:, at] = mixed[mixed.shape[0] - taps :]

    products(copies, tiles, xg_ref, ring_ref, min(SLOTS - 1, tiles), use)
    wide = column_tile(channels, 1024)
    for at in range(0, channels, wide):
        at = slice(at, at + wide)
        before = mixed_ref[:, at]
        for row in range(0, mixed_rest.shape[0], taps):
            rows = slice(row, row + taps)
            now = mixed_rest[rows, at]
            gated_ref[rows, at] = gate(before, now, q_rest[rows, at], at, spec_ref, fwd_ref, inv_ref)
            before = now


def block_columns(places, first, group, width, piece=0, pieces=1):
    return pl.ds(pl.multiple_of((places[first + group] * pieces + piece) * width, width), width)


def first_kernel(has_before, first, places, halo_ref, mixed_ref, q_ref, spec_ref, fwd_ref, inv_ref, w_ref, *refs):
    gated_ref, far_ref = refs[-2:]
    channels = q_ref.shape[1]
    ct = column_tile(channels, 1024)
    for at in range(0, channels, ct):
        at = slice(at, at + ct)
        before = jnp.where(places[has_before] > 0, halo_ref[:, at].astype(F32), 0.0).astype(BF16)
        gated_ref[:, at] = gate(before, mixed_ref[:, at], q_ref[:, at], at, spec_ref, fwd_ref, inv_ref)
    n_far, _, width = far_ref.shape
    for g in range(n_far):
        far_ref[g] = dot(gated_ref[...], w_ref[:, block_columns(places, first, g, width)]).astype(BF16)


def params(mib, steps=1):
    return pltpu.CompilerParams(dimension_semantics=("arbitrary",) * steps, vmem_limit_bytes=mib * MIB)


def in_hbm(x):
    return pltpu.with_memory_space_constraint(x, pltpu.HBM)


def in_vmem(x):
    return pltpu.with_memory_space_constraint(x, pltpu.VMEM)


RESIDENT = pl.BlockSpec(memory_space=pltpu.VMEM)


def whole(shape):
    return pl.BlockSpec(shape, lambda ch, *_: (0,) * len(shape))


def cost(rows, depth, width, extra=0):
    return pl.CostEstimate(
        flops=2 * rows * depth * width, bytes_accessed=2 * (rows * depth + depth * width) + extra, transcendentals=0
    )


def column_tile(channels, most=256):
    return most if channels % most == 0 else channels


def nothing_kernel(*refs):
    pass


def held_until(x, *others):
    return pl.pallas_call(
        nothing_kernel,
        in_specs=[pl.BlockSpec(memory_space=pl.ANY)] * (1 + len(others)),
        out_specs=pl.BlockSpec(memory_space=pl.ANY),
        out_shape=jax.ShapeDtypeStruct(x.shape, x.dtype),
        input_output_aliases={0: 0},
        compiler_params=pltpu.CompilerParams(vmem_limit_bytes=2 * MIB),
        name="held_until",
    )(x, *others)


BRIEF = pl.CostEstimate(flops=1, bytes_accessed=1, transcendentals=0)
IN_PLACE = pl.BlockSpec(memory_space=pl.ANY)
SCALARS = pl.BlockSpec(memory_space=pltpu.SMEM)


def ring_of(depth, channels):
    return pltpu.VMEM((SLOTS, 3, depth, column_tile(channels)), BF16)


def gain_rows(norm_gain, depth):
    return in_hbm(norm_gain.reshape(-1, 1, depth))


def project_local(own, beside, places, first, norm_gain, in_weight, out_weight):
    rows, depth = own.shape
    channels = in_weight.shape[2]
    ct = column_tile(channels)
    held = 2 * (rows * depth * 3 + SLOTS * 3 * 2 * depth * ct)
    return pl.pallas_call(
        functools.partial(local_kernel, first),
        in_specs=[SCALARS, IN_PLACE, RESIDENT, RESIDENT, IN_PLACE, IN_PLACE],
        out_specs=[RESIDENT] * 3,
        out_shape=[
            pltpu.VMEM((3, rows, channels), BF16),
            pltpu.VMEM((rows, 128), F32),
            pltpu.VMEM(out_weight.shape, BF16),
        ],
        scratch_shapes=[
            pltpu.VMEM((rows, depth), BF16),
            pltpu.VMEM((rows, 2 * depth), BF16),
            ring_of(2 * depth, channels),
            pltpu.SemaphoreType.DMA((SLOTS, 2)),
            pltpu.SemaphoreType.DMA,
            pltpu.SemaphoreType.DMA((channels // ct,)),
        ],
        compiler_params=pltpu.CompilerParams(vmem_limit_bytes=held + 10 * MIB),
        cost_estimate=cost(rows, depth * 2, 3 * channels),
        name="project_local",
    )(places, in_hbm(own), in_vmem(beside), gain_rows(norm_gain, depth), in_hbm(in_weight), in_hbm(out_weight))


def get_ready(places, first, depth, count, filter_taps, conv_skip, of_filter, in_weight, wait):
    taps, channels = filter_taps.shape
    return pl.pallas_call(
        functools.partial(ready_kernel, first, depth, count),
        in_specs=[SCALARS, IN_PLACE, RESIDENT, RESIDENT, IN_PLACE, IN_PLACE],
        out_specs=[RESIDENT] * 2,
        out_shape=[pltpu.VMEM((3 * taps, channels), F32), ring_of(depth * count, channels)],
        scratch_shapes=[
            pltpu.VMEM((taps, channels), F32),
            pltpu.SemaphoreType.DMA,
            pltpu.SemaphoreType.DMA((SLOTS, count)),
        ],
        compiler_params=pltpu.CompilerParams(vmem_limit_bytes=8 * MIB),
        cost_estimate=BRIEF,
        name="get_ready",
    )(places, in_hbm(filter_taps), conv_skip.reshape(1, -1), of_filter, in_hbm(in_weight), wait)


def scale_far(far, places, first, norm_gain, ssq):
    n, (rows, depth) = len(far), far[0].shape
    return pl.pallas_call(
        functools.partial(scaled_kernel, first, n),
        in_specs=[SCALARS] + [RESIDENT] * (n + 2),
        out_specs=[RESIDENT] * 2,
        out_shape=[pltpu.VMEM((rows, 2 * n * depth), BF16), pltpu.VMEM(ssq.shape, F32)],
        compiler_params=pltpu.CompilerParams(vmem_limit_bytes=8 * MIB),
        cost_estimate=BRIEF,
        name="scale_far",
    )(places, *[in_vmem(x) for x in far], gain_rows(norm_gain, depth), in_vmem(ssq))


def project_rest(lhs, places, first, norm_gain, in_weight, resident, xg, ring, d_model, taps):
    n, (rows, depth) = len(lhs), lhs[0].shape
    channels = in_weight.shape[2]
    rest = rows - taps
    at = n + 3 + len(resident)
    out = pl.pallas_call(
        functools.partial(last_kernel, first, d_model, taps, n),
        in_specs=[SCALARS] + [RESIDENT] * (n + 1) + [IN_PLACE] + [RESIDENT] * (len(resident) + 2),
        out_specs=[RESIDENT] * 6,
        out_shape=[pltpu.VMEM((r, channels), BF16) for r in (taps, taps, taps, rest)]
        + [pltpu.VMEM(x.shape, BF16) for x in (xg, ring)],
        input_output_aliases={at: 4, at + 1: 5},
        scratch_shapes=[pltpu.VMEM((rest, channels), BF16)] * 2 + [pltpu.SemaphoreType.DMA((SLOTS, 2 * n))],
        compiler_params=pltpu.CompilerParams(vmem_limit_bytes=4 * rest * channels + 10 * MIB),
        cost_estimate=cost(rows, d_model // 2, 3 * channels),
        name="project_rest",
    )(
        places,
        *[in_vmem(x) for x in lhs],
        gain_rows(norm_gain, depth),
        in_hbm(in_weight),
        *[in_vmem(x) for x in (*resident, xg, ring)],
    )
    return out[:4]


def gate_first(halo, mixed, query, spectrum, forward, inverse, out_weight, places, has_before, first, n_far, width, waits):
    taps, channels = mixed.shape
    resident = (halo, mixed, query, spectrum, forward, inverse, out_weight)
    return pl.pallas_call(
        functools.partial(first_kernel, has_before, first),
        in_specs=[SCALARS] + [RESIDENT] * len(resident) + [IN_PLACE] * len(waits),
        out_specs=[RESIDENT] * 2,
        out_shape=[pltpu.VMEM((taps, channels), BF16), pltpu.VMEM((n_far, taps, width), BF16)],
        compiler_params=pltpu.CompilerParams(vmem_limit_bytes=12 * MIB),
        cost_estimate=BRIEF,
        name="gate_first",
    )(places, *[in_vmem(x) for x in resident], *waits)


def out_kernel(n_add, first, piece, pieces, places, *refs):
    part_ref, w_ref, add, o_ref = refs[0], refs[1], refs[2 : 2 + n_add], refs[-1]
    width = o_ref.shape[-1]
    for g in range(o_ref.shape[0]):
        at = block_columns(places, first, g, width, piece, pieces)
        product = dot(part_ref[...], w_ref[:, at])
        for x in add:
            product = product + x[g].astype(F32)
        o_ref[g] = product.astype(o_ref.dtype)


def project_out(part, out_weight, places, first, n_groups, width, name, add=(), dtype=BF16, waits=(), piece=0, pieces=1):
    rows = part.shape[0]
    return pl.pallas_call(
        functools.partial(out_kernel, len(add), first, piece, pieces),
        in_specs=[SCALARS] + [RESIDENT] * (2 + len(add)) + [IN_PLACE] * len(waits),
        out_specs=RESIDENT,
        out_shape=pltpu.VMEM((n_groups, rows, width // pieces), dtype),
        compiler_params=pltpu.CompilerParams(vmem_limit_bytes=12 * MIB),
        cost_estimate=BRIEF,
        name=name,
    )(places, *[in_vmem(x) for x in (part, out_weight, *add)], *waits)


def total_kernel(n_near, n_come, first_row, *refs):
    near, come = refs[:n_near], refs[n_near : n_near + n_come]
    out_ref, held, sem = refs[-3:]
    width = held.shape[1] // n_near
    for i, x_ref in enumerate(near):
        at = slice(i * width, (i + 1) * width)
        total = x_ref[0]
        for x in come:
            total = total + x[:, at].astype(F32)
        held[:, at] = total.astype(BF16)
    copy = pltpu.make_async_copy(held, out_ref.at[pl.ds(first_row, held.shape[0])], sem)
    copy.start()
    copy.wait()


def total_rows(near, come, first_row, rows, into):
    part, width = come[0].shape
    given = [] if into is None else [into]
    n = len(near) + len(come)
    return pl.pallas_call(
        functools.partial(total_kernel, len(near), len(come), first_row),
        in_specs=[RESIDENT] * n + [IN_PLACE] * len(given),
        out_specs=IN_PLACE,
        out_shape=jax.ShapeDtypeStruct((rows, width), BF16),
        input_output_aliases={n: 0} if given else {},
        scratch_shapes=[pltpu.VMEM((part, width), BF16), pltpu.SemaphoreType.DMA],
        compiler_params=pltpu.CompilerParams(vmem_limit_bytes=8 * MIB),
        cost_estimate=BRIEF,
        name="total_rows",
    )(*[in_vmem(x) for x in (*near, *come)], *given)


def on_device(tokens, norm_gain, in_weight, filter_taps, conv_skip, out_weight):
    n_row, n_col, n_seq = lax.axis_size("trow"), lax.axis_size("tcol"), lax.axis_size("seq")
    r, c = lax.axis_index("trow"), lax.axis_index("tcol")
    rows, depth = tokens.shape
    taps = filter_taps.shape[0]
    d_model = depth * n_row * n_col
    assert n_row == 2 and rows % taps == 0
    forward, inverse, of_filter = (jnp.asarray(m) for m in dft_matrices(taps))

    def other_core(x):
        return lax.ppermute(x, "trow", [(0, 1), (1, 0)])

    def chips_along(x, s):
        return lax.ppermute(x, "tcol", [(i, (i + s) % n_col) for i in range(n_col)])

    def block_of(row, s):
        return row * n_col + lax.rem(c + s + n_col, n_col)

    shifts = range(1, n_col)
    n_far = n_col - 1
    beside = other_core(tokens)
    far = [chips_along(tokens, s) for s in shifts]
    places = jnp.stack(
        [block_of(r, 0), block_of(1 - r, 0)]
        + [block_of(row, -s) for row in (r, 1 - r) for s in shifts]
        + [block_of(row, s) for row in (1 - r, r) for s in (*shifts, 0)]
        + [jnp.minimum(lax.axis_index("seq"), 1)]
    )
    has_before = 2 + 4 * n_far + 2
    theirs_far = 2 + 2 * n_far
    theirs_near, mine_far = theirs_far + n_far, theirs_far + n_col
    mine_near = mine_far + n_far
    acc, ssq, held_weight = project_local(tokens, beside, places, 0, norm_gain, in_weight, out_weight)
    spectrum, ring = get_ready(places, 2, depth, 2 * n_far, filter_taps, conv_skip, of_filter, in_weight, ssq)
    far = [held_until(x, spectrum) for x in far]
    lhs = [other_core(x) for x in far]
    xg, ssq = scale_far(far, places, 2, norm_gain, ssq)
    resident = [acc, ssq, spectrum, forward, inverse]
    tail, q_low, mixed_low, gated_rest = project_rest(
        lhs, places, 2, norm_gain, in_weight, resident, xg, ring, d_model, taps
    )
    halo = lax.ppermute(tail, "seq", [(i, (i + 1) % n_seq) for i in range(n_seq)])

    project = functools.partial(project_out, out_weight=held_weight, places=places, width=depth)

    theirs = other_core(project(gated_rest, first=theirs_far, n_groups=n_far, name="rest_theirs_far"))
    sent = project(gated_rest, first=mine_far, n_groups=n_far, name="rest_mine_far", add=[theirs])
    come = [chips_along(sent[s - 1], s) for s in shifts]
    halves = [
        project(gated_rest, first=theirs_near, n_groups=1, name="rest_theirs_near", piece=i, pieces=2, waits=[sent])
        for i in range(2)
    ]

    gated_first, theirs = gate_first(
        halo, mixed_low, q_low, spectrum, forward, inverse, held_weight, places, has_before, theirs_far, n_far, depth, halves
    )
    sent_first = project(gated_first, first=mine_far, n_groups=n_far, name="first_mine_far", add=[other_core(theirs)])
    come_first = [chips_along(sent_first[s - 1], s) for s in shifts]

    near = [
        project(gated_rest, first=mine_near, n_groups=1, name="rest_mine_near", piece=i, pieces=2, add=[other_core(x)], dtype=F32)
        for i, x in enumerate(halves)
    ]
    theirs = other_core(project(gated_first, first=theirs_near, n_groups=1, name="first_theirs_near"))
    near_first = project(
        gated_first, first=mine_near, n_groups=1, name="first_mine_near", add=[theirs], dtype=F32
    )
    out = total_rows(near, come, taps, rows, None)
    return total_rows([near_first], come_first, 0, rows, out)


def solution(mesh):
    placed = (
        P("seq", ("trow", "tcol")),
        P(),
        P(None, None, ("trow", "tcol")),
        P(None, ("trow", "tcol")),
        P(("trow", "tcol")),
        P(("trow", "tcol"), None),
    )
    return jax.shard_map(
        on_device, mesh=mesh, in_specs=placed, out_specs=P("seq", ("trow", "tcol")), check_vma=False
    )
```

time: 86.5 us -> 84.9 us (0.982)
  waiting for transfers between devices: 14.3 us -> 10.7 us
  Pallas kernels: 58 us -> 60.1 us
    ppermute x3, waiting for transfers between devices: 6.31 us -> 1.49 us  [chips_along(): return lax.ppermute(x, 'tcol', [(i, (i + s) % n_col) for i in range(n_col)])]
    ppermute x1, waiting for transfers between devices: 5.71 us -> 7.83 us  [on_device(): lax.ppermute(tail, 'seq', [(i, (i + 1) % n_seq) for i in range(n_seq)])]
    pallas_call x13 -> x15, Pallas kernels: 40.3 us -> 42.4 us  [the longest x1 18.9 us: project_rest(): pl.pallas_call(functools.partial(last_kernel, first, d_model, taps, n), i...]
    ppermute x1, starting transfers between devices: 3.84 us -> 2.73 us  [on_device(): lax.ppermute(tail, 'seq', [(i, (i + 1) % n_seq) for i in range(n_seq)])]
    ppermute x6 -> x7, waiting for transfers between devices: 2.31 us -> 1.36 us  [other_core(): return lax.ppermute(x, 'trow', [(0, 1), (1, 0)])]
    ppermute x6 -> x7, starting transfers between devices: 1.37 us -> 2.08 us  [other_core(): return lax.ppermute(x, 'trow', [(0, 1), (1, 0)])]
    unnamed x8 -> x12, local copies, waits for them, and re-layouts: 2.2 us -> 2.21 us
  transfers between devices with their start and end apart: 10 -> 11, of which waited for: 5 -> 4; matrix products, arithmetic and copies ran while one was open for 0% -> 0% of each run, Pallas kernels for 40% -> 45%
where the time goes in v4:
time: 84.9 us; the launch traced here: 84.5 us
  Pallas kernels  60.1 us (71%)
  starting transfers between devices  11 us (13%)
  waiting for transfers between devices  10.7 us (13%)
  local copies, waits for them, and re-layouts  2.3 us (3%)
    pallas_call x1, Pallas kernels, project_rest(): pl.pallas_call(functools.partial(last_kernel, first, d_model, taps, n), i...  18.9 us
    pallas_call x1, Pallas kernels, project_local(): pl.pallas_call(functools.partial(local_kernel, first), in_specs=[SCALARS,...  17.7 us
    pallas_call x9, Pallas kernels, project_out(): pl.pallas_call(functools.partial(out_kernel, len(add), first, piece, piec...  14.6 us
    ppermute x1, waiting for transfers between devices, on_device(): lax.ppermute(tail, 'seq', [(i, (i + 1) % n_seq) for i in range(n_seq)])  7.83 us
    ppermute x3, starting transfers between devices, chips_along(): return lax.ppermute(x, 'tcol', [(i, (i + s) % n_col) for i in range(n_col)])  6.23 us
    pallas_call x1, Pallas kernels, get_ready(): pl.pallas_call(functools.partial(ready_kernel, first, depth, count), in_s...  3.84 us
    ppermute x1, starting transfers between devices, on_device(): lax.ppermute(tail, 'seq', [(i, (i + 1) % n_seq) for i in range(n_seq)])  2.73 us
    unnamed x12, local copies, waits for them, and re-layouts  2.21 us
  transfers between devices with their start and end apart: 11, of which 4 were waited for; matrix products, arithmetic and copies ran while one was open for 0% of the time, Pallas kernels for 45%

profile of v4, /device:TPU:0, one launch (start us, length us, event | category | flops | bytes accessed | tf_op | source)
XLA Modules:
  0.0 84.5 jit_solution(11752393396666283795)
XLA Ops:
  0.5 2.5 %collective-permute-start = (bf16[512,1024]{1,0:T(8,128)(2,1)}, bf16[512,1024]{1,0:T(8,128)(2,1)S(1)}, u32[]{:S(2)}, u32[]{:S(2)}) collective-permute-start(bf16[512,1024]{1,0:T(8,128)(2,1)} %own_ref.1), channel_id=1, source_target_pairs={{0,1},{1,0},{2,3},{3,2},{4,5},{5,4},{6,7},{7,6},{8,9},{9,8},{10,11... | collective-permute-start | bytes 3145736 | tf_op jit(solution)/shard_map/ppermute | solution.py:444
  3.1 1.0 %copy-done = bf16[512,1024]{1,0:T(8,128)(2,1)} copy-done((bf16[512,1024]{1,0:T(8,128)(2,1)}, bf16[512,1024]{1,0:T(8,128)(2,1)S(1)}, u32[]{:S(2)}) %copy-start) | copy-done | bytes 1048600
  4.0 1.2 %copy-done.1 = bf16[512,1024]{1,0:T(8,128)(2,1)S(1)} copy-done((bf16[512,1024]{1,0:T(8,128)(2,1)S(1)}, bf16[512,1024]{1,0:T(8,128)(2,1)}, u32[]{:S(2)}) %copy-start.1) | copy-done | bytes 1048600
  5.3 17.7 %project_local.1 = (bf16[3,512,2048]{2,1,0:T(8,128)(2,1)S(1)}, f32[512,128]{1,0:T(8,128)S(1)}, bf16[2048,4096]{1,0:T(8,128)(2,1)S(1)}) custom-call(s32[9]{0:T(128)S(1)} %stack.33.places, bf16[512,1024]{1,0:T(8,128)(2,1)} %own_ref.1, bf16[512,1024]{1,0:T(8,128)(2,1)S(1)} %copy-done.1, f32[4,1,1024]{2,1,0:T(1,128)} %bitcast.14, ...), custom_call_target="tpu_custom_call" | custom-call | flops 12884901888 | bytes 27262976 | tf_op jit(solution)/shard_map/project_local/pallas_call | solution.py:281
  23.0 3.8 %get_ready.1 = (f32[384,2048]{1,0:T(8,128)S(1)}, bf16[3,3,2048,256]{3,2,1,0:T(8,128)(2,1)S(1)}) custom-call(s32[9]{0:T(128)S(1)} %stack.33.places, f32[128,2048]{1,0:T(8,128)} %taps_ref.1, f32[1,2048]{1,0:T(1,128)S(1)} %bitcast.13, bf16[384,256]{1,0:T(8,128)(2,1)S(1)} %copy-done.4, bf16[3,4096,2048]{2,1,0:T(8,128)(2,1)} %refs_2_.1, ...), custom_call_target="tpu_custom_call" | custom-call | flops 1 | bytes 1 | tf_op jit(solution)/shard_map/get_ready/pallas_call | solution.py:306
  27.2 1.1 %scale_far.1 = (bf16[512,2048]{1,0:T(8,128)(2,1)S(1)}, f32[512,128]{1,0:T(8,128)S(1)}) custom-call(s32[9]{0:T(128)S(1)} %stack.33.places, bf16[512,1024]{1,0:T(8,128)(2,1)S(1)} %held_until.1.refs_0_, f32[4,1,1024]{2,1,0:T(1,128)} %bitcast.15, f32[512,128]{1,0:T(8,128)S(1)} %get-tuple-element.18._.refs_2_), custom_call_target="tpu_custom_call" | custom-call | flops 1 | bytes 1 | tf_op jit(solution)/shard_map/scale_far/pallas_call | solution.py:324
  28.3 1.3 %collective-permute-done.2.refs_0_ = bf16[512,1024]{1,0:T(8,128)(2,1)S(1)} collective-permute-done((bf16[512,1024]{1,0:T(8,128)(2,1)S(1)}, bf16[512,1024]{1,0:T(8,128)(2,1)S(1)}, u32[]{:S(2)}, u32[]{:S(2)}) %collective-permute-start.2) | collective-permute-done | bytes 1048608 | tf_op jit(solution)/shard_map/ppermute | solution.py:441
  29.7 18.9 %project_rest.1 = (bf16[128,2048]{1,0:T(8,128)(2,1)S(1)}, bf16[128,2048]{1,0:T(8,128)(2,1)S(1)}, bf16[128,2048]{1,0:T(8,128)(2,1)S(1)}, bf16[384,2048]{1,0:T(8,1...) custom-call(s32[9]{0:T(128)S(1)} %stack.33.places, ...), custom_call_target="tpu_custom_call", output_to_operand_aliasing={{4}: (9, {}), {5}: (10, {})} | custom-call | flops 12884901888 | bytes 27262976 | tf_op jit(solution)/shard_map/project_rest/pallas_call | solution.py:340
  48.6 2.3 %rest_theirs_far.1 = bf16[1,384,1024]{2,1,0:T(8,128)(2,1)S(1)} custom-call(s32[9]{0:T(128)S(1)} %stack.33.places, bf16[384,2048]{1,0:T(8,128)(2,1)S(1)} %get-tuple-element.28.refs_0_, bf16[2048,4096]{1,0:T(8,128)(2,1)S(1)} %get-tuple-element.27.refs_1_.w_ref), custom_call_target="tpu_custom_call" | custom-call | flops 1 | bytes 1 | tf_op jit(solution)/shard_map/rest_theirs_far/pallas_call | solution.py:388
  51.3 2.7 %collective-permute-start.3 = (bf16[128,2048]{1,0:T(8,128)(2,1)S(1)}, bf16[128,2048]{1,0:T(8,128)(2,1)S(1)}, u32[]{:S(2)}, u32[]{:S(2)}) collective-permute-start(bf16[128,2048]{1,0:T(8,128)(2,1)S(1)} %get-tuple-element.24), channel_id=1, source_target_pairs={{0,4},{4,8},{8,12},{12,16},{16,20},{20,24},{24,28},{28,0},{1,5},{5... | collective-permute-start | bytes 1572872 | tf_op jit(solution)/shard_map/ppermute | solution.py:472
  54.0 2.4 %rest_mine_far.1.refs_2_ = bf16[1,384,1024]{2,1,0:T(8,128)(2,1)S(1)} custom-call(s32[9]{0:T(128)S(1)} %stack.33.places, bf16[384,2048]{1,0:T(8,128)(2,1)S(1)} %get-tuple-element.28.refs_0_, bf16[2048,4096]{1,0:T(8,128)(2,1)S(1)} %get-tuple-element.27.refs_1_.w_ref, bf16[1,384,1024]{2,1,0:T(8,128)(2,1)S(1)} %collective-permute-done.4.refs_2_), custom_call_target="tpu_custom_call" | custom-call | flops 1 | bytes 1 | tf_op jit(solution)/shard_map/rest_mine_far/pallas_call | solution.py:388
  56.4 2.1 %collective-permute-start.10 = (bf16[384,1024]{1,0:T(8,128)(2,1)S(1)}, bf16[384,1024]{1,0:T(8,128)(2,1)S(1)}, u32[]{:S(2)}, u32[]{:S(2)}) collective-permute-start(bf16[384,1024]{1,0:T(8,128)(2,1)S(1)} %bitcast.11), channel_id=1, source_target_pairs={{0,1},{1,0},{2,3},{3,2},{4,5},{5,4},{6,7},{7,6},{8,9},{9,8},{10,11... | collective-permute-start | bytes 2359304 | tf_op jit(solution)/shard_map/ppermute | solution.py:444
  58.5 1.5 %rest_theirs_near.3.refs_1_ = bf16[1,384,512]{2,1,0:T(8,128)(2,1)S(1)} custom-call(s32[9]{0:T(128)S(1)} %stack.33.places, bf16[384,2048]{1,0:T(8,128)(2,1)S(1)} %get-tuple-element.28.refs_0_, bf16[2048,4096]{1,0:T(8,128)(2,1)S(1)} %get-tuple-element.27.refs_1_.w_ref, bf16[1,384,1024]{2,1,0:T(8,128)(2,1)S(1)} %rest_mine_far.1.refs_2_), custom_call_target="tpu_custom_call" | custom-call | flops 1 | bytes 1 | tf_op jit(solution)/shard_map/rest_theirs_near/pallas_call | solution.py:388
  60.0 1.5 %rest_theirs_near.2.refs_0_ = bf16[1,384,512]{2,1,0:T(8,128)(2,1)S(1)} custom-call(s32[9]{0:T(128)S(1)} %stack.33.places, bf16[384,2048]{1,0:T(8,128)(2,1)S(1)} %get-tuple-element.28.refs_0_, bf16[2048,4096]{1,0:T(8,128)(2,1)S(1)} %get-tuple-element.27.refs_1_.w_ref, bf16[1,384,1024]{2,1,0:T(8,128)(2,1)S(1)} %rest_mine_far.1.refs_2_), custom_call_target="tpu_custom_call" | custom-call | flops 1 | bytes 1 | tf_op jit(solution)/shard_map/rest_theirs_near/pallas_call | solution.py:388
  61.6 7.8 %collective-permute-done.3.halo_ref = bf16[128,2048]{1,0:T(8,128)(2,1)S(1)} collective-permute-done((bf16[128,2048]{1,0:T(8,128)(2,1)S(1)}, bf16[128,2048]{1,0:T(8,128)(2,1)S(1)}, u32[]{:S(2)}, u32[]{:S(2)}) %collective-permute-start.3) | collective-permute-done | bytes 524320 | tf_op jit(solution)/shard_map/ppermute | solution.py:472
  69.4 2.1 %gate_first.1 = (bf16[128,2048]{1,0:T(8,128)(2,1)S(1)}, bf16[1,128,1024]{2,1,0:T(8,128)(2,1)S(1)}) custom-call(s32[9]{0:T(128)S(1)} %stack.33.places, bf16[128,2048]{1,0:T(8,128)(2,1)S(1)} %collective-permute-done.3.halo_ref, bf16[128,2048]{1,0:T(8,128)(2,1)S(1)} %get-tuple-element.25.mixed_ref, bf16[128,2048]{1,0:T(8,128)(2,1)S(1)} %get-tuple-element.26.q_ref, ...), custom_call_target="tpu_custom_call" | custom-call | flops 1 | bytes 1 | tf_op jit(solution)/shard_map/gate_first/pallas_call | solution.py:364
  72.1 1.3 %first_theirs_near.1 = bf16[1,128,1024]{2,1,0:T(8,128)(2,1)S(1)} custom-call(s32[9]{0:T(128)S(1)} %stack.33.places, bf16[128,2048]{1,0:T(8,128)(2,1)S(1)} %get-tuple-element.29.refs_0_, bf16[2048,4096]{1,0:T(8,128)(2,1)S(1)} %get-tuple-element.27.refs_1_.w_ref), custom_call_target="tpu_custom_call" | custom-call | flops 1 | bytes 1 | tf_op jit(solution)/shard_map/first_theirs_near/pallas_call | solution.py:388
  73.9 1.3 %first_mine_far.1 = bf16[1,128,1024]{2,1,0:T(8,128)(2,1)S(1)} custom-call(s32[9]{0:T(128)S(1)} %stack.33.places, bf16[128,2048]{1,0:T(8,128)(2,1)S(1)} %get-tuple-element.29.refs_0_, bf16[2048,4096]{1,0:T(8,128)(2,1)S(1)} %get-tuple-element.27.refs_1_.w_ref, bf16[1,128,1024]{2,1,0:T(8,128)(2,1)S(1)} %collective-permute-done.6.refs_2_), custom_call_target="tpu_custom_call" | custom-call | flops 1 | bytes 1 | tf_op jit(solution)/shard_map/first_mine_far/pallas_call | solution.py:388
  75.2 1.6 %collective-permute-start.7 = (bf16[128,1024]{1,0:T(8,128)(2,1)S(1)}, bf16[128,1024]{1,0:T(8,128)(2,1)S(1)}, u32[]{:S(2)}, u32[]{:S(2)}) collective-permute-start(bf16[128,1024]{1,0:T(8,128)(2,1)S(1)} %bitcast.12), channel_id=1, source_target_pairs={{0,1},{1,0},{2,3},{3,2},{4,5},{5,4},{6,7},{7,6},{8,9},{9,8},{10,11... | collective-permute-start | bytes 786440 | tf_op jit(solution)/shard_map/ppermute | solution.py:444
  76.8 1.3 %first_mine_near.1.refs_0_ = f32[1,128,1024]{2,1,0:T(8,128)S(1)} custom-call(s32[9]{0:T(128)S(1)} %stack.33.places, bf16[128,2048]{1,0:T(8,128)(2,1)S(1)} %get-tuple-element.29.refs_0_, bf16[2048,4096]{1,0:T(8,128)(2,1)S(1)} %get-tuple-element.27.refs_1_.w_ref, bf16[1,128,1024]{2,1,0:T(8,128)(2,1)S(1)} %collective-permute-done.5.refs_2_), custom_call_target="tpu_custom_call" | custom-call | flops 1 | bytes 1 | tf_op jit(solution)/shard_map/first_mine_near/pallas_call | solution.py:388
  78.1 1.5 %rest_mine_near.2.refs_0_ = f32[1,384,512]{2,1,0:T(8,128)S(1)} custom-call(s32[9]{0:T(128)S(1)} %stack.33.places, bf16[384,2048]{1,0:T(8,128)(2,1)S(1)} %get-tuple-element.28.refs_0_, bf16[2048,4096]{1,0:T(8,128)(2,1)S(1)} %get-tuple-element.27.refs_1_.w_ref, bf16[1,384,512]{2,1,0:T(8,128)(2,1)S(1)} %collective-permute-done.8.refs_2_), custom_call_target="tpu_custom_call" | custom-call | flops 1 | bytes 1 | tf_op jit(solution)/shard_map/rest_mine_near/pallas_call | solution.py:388
  79.7 1.5 %rest_mine_near.3.refs_1_ = f32[1,384,512]{2,1,0:T(8,128)S(1)} custom-call(s32[9]{0:T(128)S(1)} %stack.33.places, bf16[384,2048]{1,0:T(8,128)(2,1)S(1)} %get-tuple-element.28.refs_0_, bf16[2048,4096]{1,0:T(8,128)(2,1)S(1)} %get-tuple-element.27.refs_1_.w_ref, bf16[1,384,512]{2,1,0:T(8,128)(2,1)S(1)} %collective-permute-done.9.refs_2_), custom_call_target="tpu_custom_call" | custom-call | flops 1 | bytes 1 | tf_op jit(solution)/shard_map/rest_mine_near/pallas_call | solution.py:388
  81.2 1.0 %total_rows.2.refs_2_ = bf16[512,1024]{1,0:T(8,128)(2,1)} custom-call(f32[1,384,512]{2,1,0:T(8,128)S(1)} %rest_mine_near.2.refs_0_, f32[1,384,512]{2,1,0:T(8,128)S(1)} %rest_mine_near.3.refs_1_, bf16[384,1024]{1,0:T(8,128)(2,1)S(1)} %collective-permute-done.10.refs_2_), custom_call_target="tpu_custom_call" | custom-call | flops 1 | bytes 1 | tf_op jit(solution)/shard_map/total_rows/pallas_call | solution.py:418
  82.2 1.3 %collective-permute-done.7.refs_1_ = bf16[128,1024]{1,0:T(8,128)(2,1)S(1)} collective-permute-done((bf16[128,1024]{1,0:T(8,128)(2,1)S(1)}, bf16[128,1024]{1,0:T(8,128)(2,1)S(1)}, u32[]{:S(2)}, u32[]{:S(2)}) %collective-permute-start.7) | collective-permute-done | bytes 262176 | tf_op jit(solution)/shard_map/ppermute | solution.py:444
  (28 shorter events, 3.1 us)
Async XLA Ops:
  0.0 3.1 %collective-permute-start.1 = (bf16[512,1024]{1,0:T(8,128)(2,1)}, bf16[512,1024]{1,0:T(8,128)(2,1)S(1)}, u32[]{:S(2)}, u32[]{:S(2)}) collective-permute-start(bf16[512,1024]{1,0:T(8,128)(2,1)} %own_ref.1), channel_id=1, source_target_pairs={{0,2},{2,0},{1,3},{3,1},{4,6},{6,4},{5,7},{7,5},{8,10},{10,8},{9,1... | collective-permute-start | bytes 3145736 | tf_op jit(solution)/shard_map/ppermute | solution.py:441
  0.5 26.6 %collective-permute-start = (bf16[512,1024]{1,0:T(8,128)(2,1)}, bf16[512,1024]{1,0:T(8,128)(2,1)S(1)}, u32[]{:S(2)}, u32[]{:S(2)}) collective-permute-start(bf16[512,1024]{1,0:T(8,128)(2,1)} %own_ref.1), channel_id=1, source_target_pairs={{0,1},{1,0},{2,3},{3,2},{4,5},{5,4},{6,7},{7,6},{8,9},{9,8},{10,11... | collective-permute-start | bytes 3145736 | tf_op jit(solution)/shard_map/ppermute | solution.py:444
  3.1 1.0 %copy-start = (bf16[512,1024]{1,0:T(8,128)(2,1)}, bf16[512,1024]{1,0:T(8,128)(2,1)S(1)}, u32[]{:S(2)}) copy-start(bf16[512,1024]{1,0:T(8,128)(2,1)S(1)} %collective-permute-done.1.beside_ref) | copy-start | bytes 3145732
  4.0 1.2 %copy-start.1 = (bf16[512,1024]{1,0:T(8,128)(2,1)S(1)}, bf16[512,1024]{1,0:T(8,128)(2,1)}, u32[]{:S(2)}) copy-start(bf16[512,1024]{1,0:T(8,128)(2,1)} %copy-done) | copy-start | bytes 3145732
  5.3 17.7 %copy-start.4 = (bf16[384,256]{1,0:T(8,128)(2,1)S(1)}, bf16[384,256]{1,0:T(8,128)(2,1)}, u32[]{:S(2)}) copy-start(bf16[384,256]{1,0:T(8,128)(2,1)} %constant.35.clone.of_filter_ref) | copy-start | bytes 589828
  5.3 17.7 %copy-start.5 = (f32[2048]{0:T(1024)S(1)}, f32[2048]{0:T(1024)}, u32[]{:S(2)}) copy-start(f32[2048]{0:T(1024)} %param.13) | copy-start | bytes 24580
  23.0 6.7 %copy-start.2 = (bf16[256,256]{1,0:T(8,128)(2,1)S(1)}, bf16[256,256]{1,0:T(8,128)(2,1)}, u32[]{:S(2)}) copy-start(bf16[256,256]{1,0:T(8,128)(2,1)} %constant.33.clone.refs_6_.fwd_ref) | copy-start | bytes 393220
  23.0 6.7 %copy-start.3 = (bf16[128,256]{1,0:T(8,128)(2,1)S(1)}, bf16[128,256]{1,0:T(8,128)(2,1)}, u32[]{:S(2)}) copy-start(bf16[128,256]{1,0:T(8,128)(2,1)} %constant.34.clone.refs_7_.inv_ref) | copy-start | bytes 196612
  27.0 2.7 %collective-permute-start.2 = (bf16[512,1024]{1,0:T(8,128)(2,1)S(1)}, bf16[512,1024]{1,0:T(8,128)(2,1)S(1)}, u32[]{:S(2)}, u32[]{:S(2)}) collective-permute-start(bf16[512,1024]{1,0:T(8,128)(2,1)S(1)} %held_until.1.refs_0_), channel_id=1, source_target_pairs={{0,2},{2,0},{1,3},{3,1},{4,6},{6,4},{5,7},{7,5},{8,10},{10,8},{9,1... | collective-permute-start | bytes 3145736 | tf_op jit(solution)/shard_map/ppermute | solution.py:441
  51.0 3.0 %collective-permute-start.4 = (bf16[1,384,1024]{2,1,0:T(8,128)(2,1)S(1)}, bf16[1,384,1024]{2,1,0:T(8,128)(2,1)S(1)}, u32[]{:S(2)}, u32[]{:S(2)}) collective-permute-start(bf16[1,384,1024]{2,1,0:T(8,128)(2,1)S(1)} %rest_theirs_far.1), channel_id=1, source_target_pairs={{0,2},{2,0},{1,3},{3,1},{4,6},{6,4},{5,7},{7,5},{8,10},{10,8},{9,1... | collective-permute-start | bytes 2359304 | tf_op jit(solution)/shard_map/ppermute | solution.py:441
  51.3 18.1 %collective-permute-start.3 = (bf16[128,2048]{1,0:T(8,128)(2,1)S(1)}, bf16[128,2048]{1,0:T(8,128)(2,1)S(1)}, u32[]{:S(2)}, u32[]{:S(2)}) collective-permute-start(bf16[128,2048]{1,0:T(8,128)(2,1)S(1)} %get-tuple-element.24), channel_id=1, source_target_pairs={{0,4},{4,8},{8,12},{12,16},{16,20},{20,24},{24,28},{28,0},{1,5},{5... | collective-permute-start | bytes 1572872 | tf_op jit(solution)/shard_map/ppermute | solution.py:472
  56.4 24.8 %collective-permute-start.10 = (bf16[384,1024]{1,0:T(8,128)(2,1)S(1)}, bf16[384,1024]{1,0:T(8,128)(2,1)S(1)}, u32[]{:S(2)}, u32[]{:S(2)}) collective-permute-start(bf16[384,1024]{1,0:T(8,128)(2,1)S(1)} %bitcast.11), channel_id=1, source_target_pairs={{0,1},{1,0},{2,3},{3,2},{4,5},{5,4},{6,7},{7,6},{8,9},{9,8},{10,11... | collective-permute-start | bytes 2359304 | tf_op jit(solution)/shard_map/ppermute | solution.py:444
  71.5 2.4 %collective-permute-start.6 = (bf16[1,128,1024]{2,1,0:T(8,128)(2,1)S(1)}, bf16[1,128,1024]{2,1,0:T(8,128)(2,1)S(1)}, u32[]{:S(2)}, u32[]{:S(2)}) collective-permute-start(bf16[1,128,1024]{2,1,0:T(8,128)(2,1)S(1)} %get-tuple-element.30), channel_id=1, source_target_pairs={{0,2},{2,0},{1,3},{3,1},{4,6},{6,4},{5,7},{7,5},{8,10},{10,8},{9,1... | collective-permute-start | bytes 786440 | tf_op jit(solution)/shard_map/ppermute | solution.py:441
  71.6 6.5 %collective-permute-start.8 = (bf16[1,384,512]{2,1,0:T(8,128)(2,1)S(1)}, bf16[1,384,512]{2,1,0:T(8,128)(2,1)S(1)}, u32[]{:S(2)}, u32[]{:S(2)}) collective-permute-start(bf16[1,384,512]{2,1,0:T(8,128)(2,1)S(1)} %rest_theirs_near.2.refs_0_), channel_id=1, source_target_pairs={{0,2},{2,0},{1,3},{3,1},{4,6},{6,4},{5,7},{7,5},{8,10},{10,8},{9,1... | collective-permute-start | bytes 1179656 | tf_op jit(solution)/shard_map/ppermute | solution.py:441
  72.1 7.6 %collective-permute-start.9 = (bf16[1,384,512]{2,1,0:T(8,128)(2,1)S(1)}, bf16[1,384,512]{2,1,0:T(8,128)(2,1)S(1)}, u32[]{:S(2)}, u32[]{:S(2)}) collective-permute-start(bf16[1,384,512]{2,1,0:T(8,128)(2,1)S(1)} %rest_theirs_near.3.refs_1_), channel_id=1, source_target_pairs={{0,2},{2,0},{1,3},{3,1},{4,6},{6,4},{5,7},{7,5},{8,10},{10,8},{9,1... | collective-permute-start | bytes 1179656 | tf_op jit(solution)/shard_map/ppermute | solution.py:441
  73.4 3.4 %collective-permute-start.5 = (bf16[1,128,1024]{2,1,0:T(8,128)(2,1)S(1)}, bf16[1,128,1024]{2,1,0:T(8,128)(2,1)S(1)}, u32[]{:S(2)}, u32[]{:S(2)}) collective-permute-start(bf16[1,128,1024]{2,1,0:T(8,128)(2,1)S(1)} %first_theirs_near.1), channel_id=1, source_target_pairs={{0,2},{2,0},{1,3},{3,1},{4,6},{6,4},{5,7},{7,5},{8,10},{10,8},{9,1... | collective-permute-start | bytes 786440 | tf_op jit(solution)/shard_map/ppermute | solution.py:441
  75.2 8.4 %collective-permute-start.7 = (bf16[128,1024]{1,0:T(8,128)(2,1)S(1)}, bf16[128,1024]{1,0:T(8,128)(2,1)S(1)}, u32[]{:S(2)}, u32[]{:S(2)}) collective-permute-start(bf16[128,1024]{1,0:T(8,128)(2,1)S(1)} %bitcast.12), channel_id=1, source_target_pairs={{0,1},{1,0},{2,3},{3,2},{4,5},{5,4},{6,7},{7,6},{8,9},{9,8},{10,11... | collective-permute-start | bytes 786440 | tf_op jit(solution)/shard_map/ppermute | solution.py:444

commit v5 on v4

--- a/solution.py
+++ b/solution.py
@@ -378,9 +378,27 @@
     for g in range(o_ref.shape[0]):
         at = block_columns(places, first, g, width, piece, pieces)
         product = dot(part_ref[...], w_ref[:, at])
-        for x in add:
-            product = product + x[g].astype(F32)
-        o_ref[g] = product.astype(o_ref.dtype)
+        if not add:
+            o_ref[g] = product.astype(o_ref.dtype)
+        for i, x in enumerate(add):
+            at = slice(i * width // n_add, (i + 1) * width // n_add)
+            o_ref[g, :, at] = (product[:, at] + x[g].astype(F32)).astype(o_ref.dtype)
+
+
+def add_kernel(a_ref, b_ref, o_ref):
+    o_ref[...] = (a_ref[...] + b_ref[...].astype(F32)).astype(o_ref.dtype)
+
+
+def added(a, b):
+    return pl.pallas_call(
+        add_kernel,
+        in_specs=[RESIDENT] * 2,
+        out_specs=RESIDENT,
+        out_shape=pltpu.VMEM(b.shape, b.dtype),
+        compiler_params=pltpu.CompilerParams(vmem_limit_bytes=8 * MIB),
+        cost_estimate=BRIEF,
+        name="added",
+    )(in_vmem(a), in_vmem(b))
 
 
 def project_out(part, out_weight, places, first, n_groups, width, name, add=(), dtype=BF16, waits=(), piece=0, pieces=1):
@@ -396,16 +414,13 @@
     )(places, *[in_vmem(x) for x in (part, out_weight, *add)], *waits)
 
 
-def total_kernel(n_near, n_come, first_row, *refs):
-    near, come = refs[:n_near], refs[n_near : n_near + n_come]
+def total_kernel(n_come, first_row, *refs):
+    near_ref, come = refs[0], refs[1 : 1 + n_come]
     out_ref, held, sem = refs[-3:]
-    width = held.shape[1] // n_near
-    for i, x_ref in enumerate(near):
-        at = slice(i * width, (i + 1) * width)
-        total = x_ref[0]
-        for x in come:
-            total = total + x[:, at].astype(F32)
-        held[:, at] = total.astype(BF16)
+    total = near_ref[0]
+    for x in come:
+        total = total + x[...].astype(F32)
+    held[...] = total.astype(BF16)
     copy = pltpu.make_async_copy(held, out_ref.at[pl.ds(first_row, held.shape[0])], sem)
     copy.start()
     copy.wait()
@@ -414,9 +429,9 @@
 def total_rows(near, come, first_row, rows, into):
     part, width = come[0].shape
     given = [] if into is None else [into]
-    n = len(near) + len(come)
-    return pl.pallas_call(
-        functools.partial(total_kernel, len(near), len(come), first_row),
+    n = 1 + len(come)
+    return pl.pallas_call(
+        functools.partial(total_kernel, len(come), first_row),
         in_specs=[RESIDENT] * n + [IN_PLACE] * len(given),
         out_specs=IN_PLACE,
         out_shape=jax.ShapeDtypeStruct((rows, width), BF16),
@@ -425,7 +440,7 @@
         compiler_params=pltpu.CompilerParams(vmem_limit_bytes=8 * MIB),
         cost_estimate=BRIEF,
         name="total_rows",
-    )(*[in_vmem(x) for x in (*near, *come)], *given)
+    )(*[in_vmem(x) for x in (near, *come)], *given)
 
 
 def on_device(tokens, norm_gain, in_weight, filter_taps, conv_skip, out_weight):
@@ -484,19 +499,23 @@
     gated_first, theirs = gate_first(
         halo, mixed_low, q_low, spectrum, forward, inverse, held_weight, places, has_before, theirs_far, n_far, depth, halves
     )
-    sent_first = project(gated_first, first=mine_far, n_groups=n_far, name="first_mine_far", add=[other_core(theirs)])
+    mine = project(gated_first, first=mine_far, n_groups=n_far, name="first_mine_far", dtype=F32)
+    sent_first = added(mine, other_core(theirs))
     come_first = [chips_along(sent_first[s - 1], s) for s in shifts]
-
-    near = [
-        project(gated_rest, first=mine_near, n_groups=1, name="rest_mine_near", piece=i, pieces=2, add=[other_core(x)], dtype=F32)
-        for i, x in enumerate(halves)
+    halves_first = [
+        project(gated_first, first=theirs_near, n_groups=1, name="first_theirs_near", piece=i, pieces=2, waits=[sent_first])
+        for i in range(2)
     ]
-    theirs = other_core(project(gated_first, first=theirs_near, n_groups=1, name="first_theirs_near"))
-    near_first = project(
-        gated_first, first=mine_near, n_groups=1, name="first_mine_near", add=[theirs], dtype=F32
-    )
+
+    near, near_first = [
+        project(part, first=mine_near, n_groups=1, name=name, add=[other_core(x) for x in pieces], dtype=F32)
+        for part, name, pieces in (
+            (gated_rest, "rest_mine_near", halves),
+            (gated_first, "first_mine_near", halves_first),
+        )
+    ]
     out = total_rows(near, come, taps, rows, None)
-    return total_rows([near_first], come_first, 0, rows, out)
+    return total_rows(near_first, come_first, 0, rows, out)
 
 
 def solution(mesh):

time: 84.9 us -> 83.7 us (0.986)
  waiting for transfers between devices: 10.7 us -> 9.25 us
    ppermute x3, waiting for transfers between devices: 1.49 us -> 0.14 us  [chips_along(): return lax.ppermute(x, 'tcol', [(i, (i + s) % n_col) for i in range(n_col)])]
    ppermute x7 -> x8, starting transfers between devices: 2.08 us -> 2.14 us  [other_core(): return lax.ppermute(x, 'trow', [(0, 1), (1, 0)])]
    pallas_call x2 -> x3, Pallas kernels: 1.78 us -> 1.83 us  [the longest x2 1.78 us: total_rows(): pl.pallas_call(functools.partial(total_kernel, len(come), first_row), in_...]
  transfers between devices with their start and end apart: 11 -> 12, of which waited for: 4 -> 3; matrix products, arithmetic and copies ran while one was open for 0% -> 0% of each run, Pallas kernels for 45% -> 46%
where the time goes in v5:
time: 83.7 us; the launch traced here: 83.2 us
  Pallas kernels  60.2 us (72%)
  starting transfers between devices  11.1 us (13%)
  waiting for transfers between devices  9.25 us (11%)
  local copies, waits for them, and re-layouts  2.3 us (3%)
    pallas_call x1, Pallas kernels, project_rest(): pl.pallas_call(functools.partial(last_kernel, first, d_model, taps, n), i...  18.9 us
    pallas_call x1, Pallas kernels, project_local(): pl.pallas_call(functools.partial(local_kernel, first), in_specs=[SCALARS,...  17.7 us
    pallas_call x9, Pallas kernels, project_out(): pl.pallas_call(functools.partial(out_kernel, len(add), first, piece, piec...  14.6 us
    ppermute x1, waiting for transfers between devices, on_device(): lax.ppermute(tail, 'seq', [(i, (i + 1) % n_seq) for i in range(n_seq)])  7.75 us
    ppermute x3, starting transfers between devices, chips_along(): return lax.ppermute(x, 'tcol', [(i, (i + s) % n_col) for i in range(n_col)])  6.23 us
    pallas_call x1, Pallas kernels, get_ready(): pl.pallas_call(functools.partial(ready_kernel, first, depth, count), in_s...  3.84 us
    ppermute x1, starting transfers between devices, on_device(): lax.ppermute(tail, 'seq', [(i, (i + 1) % n_seq) for i in range(n_seq)])  2.73 us
    unnamed x12, local copies, waits for them, and re-layouts  2.21 us
  transfers between devices with their start and end apart: 12, of which 3 were waited for; matrix products, arithmetic and copies ran while one was open for 0% of the time, Pallas kernels for 46%

profile of v5, /device:TPU:0, one launch (start us, length us, event | category | flops | bytes accessed | tf_op | source)
XLA Modules:
  0.0 83.2 jit_solution(14201980857503700742)
XLA Ops:
  0.5 2.5 %collective-permute-start = (bf16[512,1024]{1,0:T(8,128)(2,1)}, bf16[512,1024]{1,0:T(8,128)(2,1)S(1)}, u32[]{:S(2)}, u32[]{:S(2)}) collective-permute-start(bf16[512,1024]{1,0:T(8,128)(2,1)} %own_ref.1), channel_id=1, source_target_pairs={{0,1},{1,0},{2,3},{3,2},{4,5},{5,4},{6,7},{7,6},{8,9},{9,8},{10,11... | collective-permute-start | bytes 3145736 | tf_op jit(solution)/shard_map/ppermute | solution.py:459
  3.1 1.0 %copy-done = bf16[512,1024]{1,0:T(8,128)(2,1)} copy-done((bf16[512,1024]{1,0:T(8,128)(2,1)}, bf16[512,1024]{1,0:T(8,128)(2,1)S(1)}, u32[]{:S(2)}) %copy-start) | copy-done | bytes 1048600
  4.0 1.2 %copy-done.1 = bf16[512,1024]{1,0:T(8,128)(2,1)S(1)} copy-done((bf16[512,1024]{1,0:T(8,128)(2,1)S(1)}, bf16[512,1024]{1,0:T(8,128)(2,1)}, u32[]{:S(2)}) %copy-start.1) | copy-done | bytes 1048600
  5.3 17.7 %project_local.1 = (bf16[3,512,2048]{2,1,0:T(8,128)(2,1)S(1)}, f32[512,128]{1,0:T(8,128)S(1)}, bf16[2048,4096]{1,0:T(8,128)(2,1)S(1)}) custom-call(s32[9]{0:T(128)S(1)} %stack.33.places, bf16[512,1024]{1,0:T(8,128)(2,1)} %own_ref.1, bf16[512,1024]{1,0:T(8,128)(2,1)S(1)} %copy-done.1, f32[4,1,1024]{2,1,0:T(1,128)} %bitcast.14, ...), custom_call_target="tpu_custom_call" | custom-call | flops 12884901888 | bytes 27262976 | tf_op jit(solution)/shard_map/project_local/pallas_call | solution.py:281
  23.0 3.8 %get_ready.1 = (f32[384,2048]{1,0:T(8,128)S(1)}, bf16[3,3,2048,256]{3,2,1,0:T(8,128)(2,1)S(1)}) custom-call(s32[9]{0:T(128)S(1)} %stack.33.places, f32[128,2048]{1,0:T(8,128)} %taps_ref.1, f32[1,2048]{1,0:T(1,128)S(1)} %bitcast.13, bf16[384,256]{1,0:T(8,128)(2,1)S(1)} %copy-done.4, bf16[3,4096,2048]{2,1,0:T(8,128)(2,1)} %refs_2_.1, ...), custom_call_target="tpu_custom_call" | custom-call | flops 1 | bytes 1 | tf_op jit(solution)/shard_map/get_ready/pallas_call | solution.py:306
  27.2 1.1 %scale_far.1 = (bf16[512,2048]{1,0:T(8,128)(2,1)S(1)}, f32[512,128]{1,0:T(8,128)S(1)}) custom-call(s32[9]{0:T(128)S(1)} %stack.33.places, bf16[512,1024]{1,0:T(8,128)(2,1)S(1)} %held_until.1.refs_0_, f32[4,1,1024]{2,1,0:T(1,128)} %bitcast.15, f32[512,128]{1,0:T(8,128)S(1)} %get-tuple-element.18._.refs_2_), custom_call_target="tpu_custom_call" | custom-call | flops 1 | bytes 1 | tf_op jit(solution)/shard_map/scale_far/pallas_call | solution.py:324
  28.3 1.3 %collective-permute-done.2.refs_0_ = bf16[512,1024]{1,0:T(8,128)(2,1)S(1)} collective-permute-done((bf16[512,1024]{1,0:T(8,128)(2,1)S(1)}, bf16[512,1024]{1,0:T(8,128)(2,1)S(1)}, u32[]{:S(2)}, u32[]{:S(2)}) %collective-permute-start.2) | collective-permute-done | bytes 1048608 | tf_op jit(solution)/shard_map/ppermute | solution.py:456
  29.7 18.9 %project_rest.1 = (bf16[128,2048]{1,0:T(8,128)(2,1)S(1)}, bf16[128,2048]{1,0:T(8,128)(2,1)S(1)}, bf16[128,2048]{1,0:T(8,128)(2,1)S(1)}, bf16[384,2048]{1,0:T(8,1...) custom-call(s32[9]{0:T(128)S(1)} %stack.33.places, ...), custom_call_target="tpu_custom_call", output_to_operand_aliasing={{4}: (9, {}), {5}: (10, {})} | custom-call | flops 12884901888 | bytes 27262976 | tf_op jit(solution)/shard_map/project_rest/pallas_call | solution.py:340
  48.6 2.3 %rest_theirs_far.1 = bf16[1,384,1024]{2,1,0:T(8,128)(2,1)S(1)} custom-call(s32[9]{0:T(128)S(1)} %stack.33.places, bf16[384,2048]{1,0:T(8,128)(2,1)S(1)} %get-tuple-element.28.refs_0_, bf16[2048,4096]{1,0:T(8,128)(2,1)S(1)} %get-tuple-element.27.refs_1_.w_ref), custom_call_target="tpu_custom_call" | custom-call | flops 1 | bytes 1 | tf_op jit(solution)/shard_map/rest_theirs_far/pallas_call | solution.py:406
  51.3 2.7 %collective-permute-start.3 = (bf16[128,2048]{1,0:T(8,128)(2,1)S(1)}, bf16[128,2048]{1,0:T(8,128)(2,1)S(1)}, u32[]{:S(2)}, u32[]{:S(2)}) collective-permute-start(bf16[128,2048]{1,0:T(8,128)(2,1)S(1)} %get-tuple-element.24), channel_id=1, source_target_pairs={{0,4},{4,8},{8,12},{12,16},{16,20},{20,24},{24,28},{28,0},{1,5},{5... | collective-permute-start | bytes 1572872 | tf_op jit(solution)/shard_map/ppermute | solution.py:487
  54.0 2.4 %rest_mine_far.1.refs_2_ = bf16[1,384,1024]{2,1,0:T(8,128)(2,1)S(1)} custom-call(s32[9]{0:T(128)S(1)} %stack.33.places, bf16[384,2048]{1,0:T(8,128)(2,1)S(1)} %get-tuple-element.28.refs_0_, bf16[2048,4096]{1,0:T(8,128)(2,1)S(1)} %get-tuple-element.27.refs_1_.w_ref, bf16[1,384,1024]{2,1,0:T(8,128)(2,1)S(1)} %collective-permute-done.4.refs_2_), custom_call_target="tpu_custom_call" | custom-call | flops 1 | bytes 1 | tf_op jit(solution)/shard_map/rest_mine_far/pallas_call | solution.py:406
  56.4 2.1 %collective-permute-start.11 = (bf16[384,1024]{1,0:T(8,128)(2,1)S(1)}, bf16[384,1024]{1,0:T(8,128)(2,1)S(1)}, u32[]{:S(2)}, u32[]{:S(2)}) collective-permute-start(bf16[384,1024]{1,0:T(8,128)(2,1)S(1)} %bitcast.11), channel_id=1, source_target_pairs={{0,1},{1,0},{2,3},{3,2},{4,5},{5,4},{6,7},{7,6},{8,9},{9,8},{10,11... | collective-permute-start | bytes 2359304 | tf_op jit(solution)/shard_map/ppermute | solution.py:459
  58.5 1.5 %rest_theirs_near.3.refs_1_ = bf16[1,384,512]{2,1,0:T(8,128)(2,1)S(1)} custom-call(s32[9]{0:T(128)S(1)} %stack.33.places, bf16[384,2048]{1,0:T(8,128)(2,1)S(1)} %get-tuple-element.28.refs_0_, bf16[2048,4096]{1,0:T(8,128)(2,1)S(1)} %get-tuple-element.27.refs_1_.w_ref, bf16[1,384,1024]{2,1,0:T(8,128)(2,1)S(1)} %rest_mine_far.1.refs_2_), custom_call_target="tpu_custom_call" | custom-call | flops 1 | bytes 1 | tf_op jit(solution)/shard_map/rest_theirs_near/pallas_call | solution.py:406
  60.0 1.5 %rest_theirs_near.2.refs_0_ = bf16[1,384,512]{2,1,0:T(8,128)(2,1)S(1)} custom-call(s32[9]{0:T(128)S(1)} %stack.33.places, bf16[384,2048]{1,0:T(8,128)(2,1)S(1)} %get-tuple-element.28.refs_0_, bf16[2048,4096]{1,0:T(8,128)(2,1)S(1)} %get-tuple-element.27.refs_1_.w_ref, bf16[1,384,1024]{2,1,0:T(8,128)(2,1)S(1)} %rest_mine_far.1.refs_2_), custom_call_target="tpu_custom_call" | custom-call | flops 1 | bytes 1 | tf_op jit(solution)/shard_map/rest_theirs_near/pallas_call | solution.py:406
  61.6 7.7 %collective-permute-done.3.halo_ref = bf16[128,2048]{1,0:T(8,128)(2,1)S(1)} collective-permute-done((bf16[128,2048]{1,0:T(8,128)(2,1)S(1)}, bf16[128,2048]{1,0:T(8,128)(2,1)S(1)}, u32[]{:S(2)}, u32[]{:S(2)}) %collective-permute-start.3) | collective-permute-done | bytes 524320 | tf_op jit(solution)/shard_map/ppermute | solution.py:487
  69.4 2.1 %gate_first.1 = (bf16[128,2048]{1,0:T(8,128)(2,1)S(1)}, bf16[1,128,1024]{2,1,0:T(8,128)(2,1)S(1)}) custom-call(s32[9]{0:T(128)S(1)} %stack.33.places, bf16[128,2048]{1,0:T(8,128)(2,1)S(1)} %collective-permute-done.3.halo_ref, bf16[128,2048]{1,0:T(8,128)(2,1)S(1)} %get-tuple-element.25.mixed_ref, bf16[128,2048]{1,0:T(8,128)(2,1)S(1)} %get-tuple-element.26.q_ref, ...), custom_call_target="tpu_custom_call" | custom-call | flops 1 | bytes 1 | tf_op jit(solution)/shard_map/gate_first/pallas_call | solution.py:364
  72.1 1.3 %first_mine_far.1.a_ref = f32[1,128,1024]{2,1,0:T(8,128)S(1)} custom-call(s32[9]{0:T(128)S(1)} %stack.33.places, bf16[128,2048]{1,0:T(8,128)(2,1)S(1)} %get-tuple-element.29.refs_0_, bf16[2048,4096]{1,0:T(8,128)(2,1)S(1)} %get-tuple-element.27.refs_1_.w_ref), custom_call_target="tpu_custom_call" | custom-call | flops 1 | bytes 1 | tf_op jit(solution)/shard_map/first_mine_far/pallas_call | solution.py:406
  73.4 1.6 %collective-permute-start.8 = (bf16[128,1024]{1,0:T(8,128)(2,1)S(1)}, bf16[128,1024]{1,0:T(8,128)(2,1)S(1)}, u32[]{:S(2)}, u32[]{:S(2)}) collective-permute-start(bf16[128,1024]{1,0:T(8,128)(2,1)S(1)} %bitcast.12), channel_id=1, source_target_pairs={{0,1},{1,0},{2,3},{3,2},{4,5},{5,4},{6,7},{7,6},{8,9},{9,8},{10,11... | collective-permute-start | bytes 786440 | tf_op jit(solution)/shard_map/ppermute | solution.py:459
  75.0 1.0 %first_theirs_near.3 = bf16[1,128,512]{2,1,0:T(8,128)(2,1)S(1)} custom-call(s32[9]{0:T(128)S(1)} %stack.33.places, bf16[128,2048]{1,0:T(8,128)(2,1)S(1)} %get-tuple-element.29.refs_0_, bf16[2048,4096]{1,0:T(8,128)(2,1)S(1)} %get-tuple-element.27.refs_1_.w_ref, bf16[1,128,1024]{2,1,0:T(8,128)(2,1)S(1)} %added.1.refs_2_), custom_call_target="tpu_custom_call" | custom-call | flops 1 | bytes 1 | tf_op jit(solution)/shard_map/first_theirs_near/pallas_call | solution.py:406
  76.0 1.0 %first_theirs_near.2 = bf16[1,128,512]{2,1,0:T(8,128)(2,1)S(1)} custom-call(s32[9]{0:T(128)S(1)} %stack.33.places, bf16[128,2048]{1,0:T(8,128)(2,1)S(1)} %get-tuple-element.29.refs_0_, bf16[2048,4096]{1,0:T(8,128)(2,1)S(1)} %get-tuple-element.27.refs_1_.w_ref, bf16[1,128,1024]{2,1,0:T(8,128)(2,1)S(1)} %added.1.refs_2_), custom_call_target="tpu_custom_call" | custom-call | flops 1 | bytes 1 | tf_op jit(solution)/shard_map/first_theirs_near/pallas_call | solution.py:406
  77.6 2.3 %rest_mine_near.1.refs_0_ = f32[1,384,1024]{2,1,0:T(8,128)S(1)} custom-call(s32[9]{0:T(128)S(1)} %stack.33.places, bf16[384,2048]{1,0:T(8,128)(2,1)S(1)} %get-tuple-element.28.refs_0_, bf16[2048,4096]{1,0:T(8,128)(2,1)S(1)} %get-tuple-element.27.refs_1_.w_ref, bf16[1,384,512]{2,1,0:T(8,128)(2,1)S(1)} %collective-permute-done.9.refs_2_, ...), custom_call_target="tpu_custom_call" | custom-call | flops 1 | bytes 1 | tf_op jit(solution)/shard_map/rest_mine_near/pallas_call | solution.py:406
  80.0 1.3 %first_mine_near.1.refs_0_ = f32[1,128,1024]{2,1,0:T(8,128)S(1)} custom-call(s32[9]{0:T(128)S(1)} %stack.33.places, bf16[128,2048]{1,0:T(8,128)(2,1)S(1)} %get-tuple-element.29.refs_0_, bf16[2048,4096]{1,0:T(8,128)(2,1)S(1)} %get-tuple-element.27.refs_1_.w_ref, bf16[1,128,512]{2,1,0:T(8,128)(2,1)S(1)} %collective-permute-done.6.refs_2_, ...), custom_call_target="tpu_custom_call" | custom-call | flops 1 | bytes 1 | tf_op jit(solution)/shard_map/first_mine_near/pallas_call | solution.py:406
  81.3 1.0 %total_rows.2.refs_2_ = bf16[512,1024]{1,0:T(8,128)(2,1)} custom-call(f32[1,384,1024]{2,1,0:T(8,128)S(1)} %rest_mine_near.1.refs_0_, bf16[384,1024]{1,0:T(8,128)(2,1)S(1)} %collective-permute-done.11.refs_1_), custom_call_target="tpu_custom_call" | custom-call | flops 1 | bytes 1 | tf_op jit(solution)/shard_map/total_rows/pallas_call | solution.py:433
  82.3 0.8 total_rows.3
  (31 shorter events, 2.5 us)
Async XLA Ops:
  0.0 3.1 %collective-permute-start.1 = (bf16[512,1024]{1,0:T(8,128)(2,1)}, bf16[512,1024]{1,0:T(8,128)(2,1)S(1)}, u32[]{:S(2)}, u32[]{:S(2)}) collective-permute-start(bf16[512,1024]{1,0:T(8,128)(2,1)} %own_ref.1), channel_id=1, source_target_pairs={{0,2},{2,0},{1,3},{3,1},{4,6},{6,4},{5,7},{7,5},{8,10},{10,8},{9,1... | collective-permute-start | bytes 3145736 | tf_op jit(solution)/shard_map/ppermute | solution.py:456
  0.5 26.6 %collective-permute-start = (bf16[512,1024]{1,0:T(8,128)(2,1)}, bf16[512,1024]{1,0:T(8,128)(2,1)S(1)}, u32[]{:S(2)}, u32[]{:S(2)}) collective-permute-start(bf16[512,1024]{1,0:T(8,128)(2,1)} %own_ref.1), channel_id=1, source_target_pairs={{0,1},{1,0},{2,3},{3,2},{4,5},{5,4},{6,7},{7,6},{8,9},{9,8},{10,11... | collective-permute-start | bytes 3145736 | tf_op jit(solution)/shard_map/ppermute | solution.py:459
  3.1 1.0 %copy-start = (bf16[512,1024]{1,0:T(8,128)(2,1)}, bf16[512,1024]{1,0:T(8,128)(2,1)S(1)}, u32[]{:S(2)}) copy-start(bf16[512,1024]{1,0:T(8,128)(2,1)S(1)} %collective-permute-done.1.beside_ref) | copy-start | bytes 3145732
  4.0 1.2 %copy-start.1 = (bf16[512,1024]{1,0:T(8,128)(2,1)S(1)}, bf16[512,1024]{1,0:T(8,128)(2,1)}, u32[]{:S(2)}) copy-start(bf16[512,1024]{1,0:T(8,128)(2,1)} %copy-done) | copy-start | bytes 3145732
  5.3 17.7 %copy-start.4 = (bf16[384,256]{1,0:T(8,128)(2,1)S(1)}, bf16[384,256]{1,0:T(8,128)(2,1)}, u32[]{:S(2)}) copy-start(bf16[384,256]{1,0:T(8,128)(2,1)} %constant.35.clone.of_filter_ref) | copy-start | bytes 589828
  5.3 17.7 %copy-start.5 = (f32[2048]{0:T(1024)S(1)}, f32[2048]{0:T(1024)}, u32[]{:S(2)}) copy-start(f32[2048]{0:T(1024)} %param.13) | copy-start | bytes 24580
  26.8 2.8 %copy-start.2 = (bf16[256,256]{1,0:T(8,128)(2,1)S(1)}, bf16[256,256]{1,0:T(8,128)(2,1)}, u32[]{:S(2)}) copy-start(bf16[256,256]{1,0:T(8,128)(2,1)} %constant.33.clone.refs_6_.fwd_ref) | copy-start | bytes 393220
  26.9 2.8 %copy-start.3 = (bf16[128,256]{1,0:T(8,128)(2,1)S(1)}, bf16[128,256]{1,0:T(8,128)(2,1)}, u32[]{:S(2)}) copy-start(bf16[128,256]{1,0:T(8,128)(2,1)} %constant.34.clone.refs_7_.inv_ref) | copy-start | bytes 196612
  27.0 2.7 %collective-permute-start.2 = (bf16[512,1024]{1,0:T(8,128)(2,1)S(1)}, bf16[512,1024]{1,0:T(8,128)(2,1)S(1)}, u32[]{:S(2)}, u32[]{:S(2)}) collective-permute-start(bf16[512,1024]{1,0:T(8,128)(2,1)S(1)} %held_until.1.refs_0_), channel_id=1, source_target_pairs={{0,2},{2,0},{1,3},{3,1},{4,6},{6,4},{5,7},{7,5},{8,10},{10,8},{9,1... | collective-permute-start | bytes 3145736 | tf_op jit(solution)/shard_map/ppermute | solution.py:456
  51.0 3.0 %collective-permute-start.4 = (bf16[1,384,1024]{2,1,0:T(8,128)(2,1)S(1)}, bf16[1,384,1024]{2,1,0:T(8,128)(2,1)S(1)}, u32[]{:S(2)}, u32[]{:S(2)}) collective-permute-start(bf16[1,384,1024]{2,1,0:T(8,128)(2,1)S(1)} %rest_theirs_far.1), channel_id=1, source_target_pairs={{0,2},{2,0},{1,3},{3,1},{4,6},{6,4},{5,7},{7,5},{8,10},{10,8},{9,1... | collective-permute-start | bytes 2359304 | tf_op jit(solution)/shard_map/ppermute | solution.py:456
  51.3 18.1 %collective-permute-start.3 = (bf16[128,2048]{1,0:T(8,128)(2,1)S(1)}, bf16[128,2048]{1,0:T(8,128)(2,1)S(1)}, u32[]{:S(2)}, u32[]{:S(2)}) collective-permute-start(bf16[128,2048]{1,0:T(8,128)(2,1)S(1)} %get-tuple-element.24), channel_id=1, source_target_pairs={{0,4},{4,8},{8,12},{12,16},{16,20},{20,24},{24,28},{28,0},{1,5},{5... | collective-permute-start | bytes 1572872 | tf_op jit(solution)/shard_map/ppermute | solution.py:487
  56.4 24.9 %collective-permute-start.11 = (bf16[384,1024]{1,0:T(8,128)(2,1)S(1)}, bf16[384,1024]{1,0:T(8,128)(2,1)S(1)}, u32[]{:S(2)}, u32[]{:S(2)}) collective-permute-start(bf16[384,1024]{1,0:T(8,128)(2,1)S(1)} %bitcast.11), channel_id=1, source_target_pairs={{0,1},{1,0},{2,3},{3,2},{4,5},{5,4},{6,7},{7,6},{8,9},{9,8},{10,11... | collective-permute-start | bytes 2359304 | tf_op jit(solution)/shard_map/ppermute | solution.py:459
  61.6 15.5 %collective-permute-start.9 = (bf16[1,384,512]{2,1,0:T(8,128)(2,1)S(1)}, bf16[1,384,512]{2,1,0:T(8,128)(2,1)S(1)}, u32[]{:S(2)}, u32[]{:S(2)}) collective-permute-start(bf16[1,384,512]{2,1,0:T(8,128)(2,1)S(1)} %rest_theirs_near.2.refs_0_), channel_id=1, source_target_pairs={{0,2},{2,0},{1,3},{3,1},{4,6},{6,4},{5,7},{7,5},{8,10},{10,8},{9,1... | collective-permute-start | bytes 1179656 | tf_op jit(solution)/shard_map/ppermute | solution.py:456
  71.5 1.9 %collective-permute-start.5 = (bf16[1,128,1024]{2,1,0:T(8,128)(2,1)S(1)}, bf16[1,128,1024]{2,1,0:T(8,128)(2,1)S(1)}, u32[]{:S(2)}, u32[]{:S(2)}) collective-permute-start(bf16[1,128,1024]{2,1,0:T(8,128)(2,1)S(1)} %get-tuple-element.30), channel_id=1, source_target_pairs={{0,2},{2,0},{1,3},{3,1},{4,6},{6,4},{5,7},{7,5},{8,10},{10,8},{9,1... | collective-permute-start | bytes 786440 | tf_op jit(solution)/shard_map/ppermute | solution.py:456
  71.6 6.0 %collective-permute-start.10 = (bf16[1,384,512]{2,1,0:T(8,128)(2,1)S(1)}, bf16[1,384,512]{2,1,0:T(8,128)(2,1)S(1)}, u32[]{:S(2)}, u32[]{:S(2)}) collective-permute-start(bf16[1,384,512]{2,1,0:T(8,128)(2,1)S(1)} %rest_theirs_near.3.refs_1_), channel_id=1, source_target_pairs={{0,2},{2,0},{1,3},{3,1},{4,6},{6,4},{5,7},{7,5},{8,10},{10,8},{9,1... | collective-permute-start | bytes 1179656 | tf_op jit(solution)/shard_map/ppermute | solution.py:456
  73.4 8.9 %collective-permute-start.8 = (bf16[128,1024]{1,0:T(8,128)(2,1)S(1)}, bf16[128,1024]{1,0:T(8,128)(2,1)S(1)}, u32[]{:S(2)}, u32[]{:S(2)}) collective-permute-start(bf16[128,1024]{1,0:T(8,128)(2,1)S(1)} %bitcast.12), channel_id=1, source_target_pairs={{0,1},{1,0},{2,3},{3,2},{4,5},{5,4},{6,7},{7,6},{8,9},{9,8},{10,11... | collective-permute-start | bytes 786440 | tf_op jit(solution)/shard_map/ppermute | solution.py:459
  77.0 2.9 %collective-permute-start.6 = (bf16[1,128,512]{2,1,0:T(8,128)(2,1)S(1)}, bf16[1,128,512]{2,1,0:T(8,128)(2,1)S(1)}, u32[]{:S(2)}, u32[]{:S(2)}) collective-permute-start(bf16[1,128,512]{2,1,0:T(8,128)(2,1)S(1)} %first_theirs_near.2), channel_id=1, source_target_pairs={{0,2},{2,0},{1,3},{3,1},{4,6},{6,4},{5,7},{7,5},{8,10},{10,8},{9,1... | collective-permute-start | bytes 393224 | tf_op jit(solution)/shard_map/ppermute | solution.py:456
  77.1 2.9 %collective-permute-start.7 = (bf16[1,128,512]{2,1,0:T(8,128)(2,1)S(1)}, bf16[1,128,512]{2,1,0:T(8,128)(2,1)S(1)}, u32[]{:S(2)}, u32[]{:S(2)}) collective-permute-start(bf16[1,128,512]{2,1,0:T(8,128)(2,1)S(1)} %first_theirs_near.3), channel_id=1, source_target_pairs={{0,2},{2,0},{1,3},{3,1},{4,6},{6,4},{5,7},{7,5},{8,10},{10,8},{9,1... | collective-permute-start | bytes 393224 | tf_op jit(solution)/shard_map/ppermute | solution.py:456

commit v6 on v5

--- a/solution.py
+++ b/solution.py
@@ -187,7 +187,7 @@
         tail_ref[:, at] = mixed[mixed.shape[0] - taps :]
 
     products(copies, tiles, xg_ref, ring_ref, min(SLOTS - 1, tiles), use)
-    wide = column_tile(channels, 1024)
+    wide = column_tile(channels, 2048)
     for at in range(0, channels, wide):
         at = slice(at, at + wide)
         before = mixed_ref[:, at]
@@ -205,7 +205,7 @@
 def first_kernel(has_before, first, places, halo_ref, mixed_ref, q_ref, spec_ref, fwd_ref, inv_ref, w_ref, *refs):
     gated_ref, far_ref = refs[-2:]
     channels = q_ref.shape[1]
-    ct = column_tile(channels, 1024)
+    ct = column_tile(channels, 2048)
     for at in range(0, channels, ct):
         at = slice(at, at + ct)
         before = jnp.where(places[has_before] > 0, halo_ref[:, at].astype(F32), 0.0).astype(BF16)

time: 83.7 us -> 83.3 us (level)
  no operation moved by 1% of the time
where the time goes in v6:
time: 83.3 us; the launch traced here: 82.8 us
  Pallas kernels  59.8 us (72%)
  starting transfers between devices  11.1 us (13%)
  waiting for transfers between devices  9.26 us (11%)
  local copies, waits for them, and re-layouts  2.3 us (3%)
    pallas_call x1, Pallas kernels, project_rest(): pl.pallas_call(functools.partial(last_kernel, first, d_model, taps, n), i...  18.6 us
    pallas_call x1, Pallas kernels, project_local(): pl.pallas_call(functools.partial(local_kernel, first), in_specs=[SCALARS,...  17.7 us
    pallas_call x9, Pallas kernels, project_out(): pl.pallas_call(functools.partial(out_kernel, len(add), first, piece, piec...  14.6 us
    ppermute x1, waiting for transfers between devices, on_device(): lax.ppermute(tail, 'seq', [(i, (i + 1) % n_seq) for i in range(n_seq)])  7.75 us
    ppermute x3, starting transfers between devices, chips_along(): return lax.ppermute(x, 'tcol', [(i, (i + s) % n_col) for i in range(n_col)])  6.23 us
    pallas_call x1, Pallas kernels, get_ready(): pl.pallas_call(functools.partial(ready_kernel, first, depth, count), in_s...  3.84 us
    ppermute x1, starting transfers between devices, on_device(): lax.ppermute(tail, 'seq', [(i, (i + 1) % n_seq) for i in range(n_seq)])  2.73 us
    unnamed x12, local copies, waits for them, and re-layouts  2.21 us
  transfers between devices with their start and end apart: 12, of which 3 were waited for; matrix products, arithmetic and copies ran while one was open for 0% of the time, Pallas kernels for 46%

profile of v6, /device:TPU:0, one launch (start us, length us, event | category | flops | bytes accessed | tf_op | source)
XLA Modules:
  0.0 82.8 jit_solution(9069234330399784501)
XLA Ops:
  0.5 2.5 %collective-permute-start = (bf16[512,1024]{1,0:T(8,128)(2,1)}, bf16[512,1024]{1,0:T(8,128)(2,1)S(1)}, u32[]{:S(2)}, u32[]{:S(2)}) collective-permute-start(bf16[512,1024]{1,0:T(8,128)(2,1)} %own_ref.1), channel_id=1, source_target_pairs={{0,1},{1,0},{2,3},{3,2},{4,5},{5,4},{6,7},{7,6},{8,9},{9,8},{10,11... | collective-permute-start | bytes 3145736 | tf_op jit(solution)/shard_map/ppermute | solution.py:459
  3.1 1.0 %copy-done = bf16[512,1024]{1,0:T(8,128)(2,1)} copy-done((bf16[512,1024]{1,0:T(8,128)(2,1)}, bf16[512,1024]{1,0:T(8,128)(2,1)S(1)}, u32[]{:S(2)}) %copy-start) | copy-done | bytes 1048600
  4.0 1.2 %copy-done.1 = bf16[512,1024]{1,0:T(8,128)(2,1)S(1)} copy-done((bf16[512,1024]{1,0:T(8,128)(2,1)S(1)}, bf16[512,1024]{1,0:T(8,128)(2,1)}, u32[]{:S(2)}) %copy-start.1) | copy-done | bytes 1048600
  5.3 17.7 %project_local.1 = (bf16[3,512,2048]{2,1,0:T(8,128)(2,1)S(1)}, f32[512,128]{1,0:T(8,128)S(1)}, bf16[2048,4096]{1,0:T(8,128)(2,1)S(1)}) custom-call(s32[9]{0:T(128)S(1)} %stack.33.places, bf16[512,1024]{1,0:T(8,128)(2,1)} %own_ref.1, bf16[512,1024]{1,0:T(8,128)(2,1)S(1)} %copy-done.1, f32[4,1,1024]{2,1,0:T(1,128)} %bitcast.14, ...), custom_call_target="tpu_custom_call" | custom-call | flops 12884901888 | bytes 27262976 | tf_op jit(solution)/shard_map/project_local/pallas_call | solution.py:281
  23.0 3.8 %get_ready.1 = (f32[384,2048]{1,0:T(8,128)S(1)}, bf16[3,3,2048,256]{3,2,1,0:T(8,128)(2,1)S(1)}) custom-call(s32[9]{0:T(128)S(1)} %stack.33.places, f32[128,2048]{1,0:T(8,128)} %taps_ref.1, f32[1,2048]{1,0:T(1,128)S(1)} %bitcast.13, bf16[384,256]{1,0:T(8,128)(2,1)S(1)} %copy-done.4, bf16[3,4096,2048]{2,1,0:T(8,128)(2,1)} %refs_2_.1, ...), custom_call_target="tpu_custom_call" | custom-call | flops 1 | bytes 1 | tf_op jit(solution)/shard_map/get_ready/pallas_call | solution.py:306
  27.2 1.1 %scale_far.1 = (bf16[512,2048]{1,0:T(8,128)(2,1)S(1)}, f32[512,128]{1,0:T(8,128)S(1)}) custom-call(s32[9]{0:T(128)S(1)} %stack.33.places, bf16[512,1024]{1,0:T(8,128)(2,1)S(1)} %held_until.1.refs_0_, f32[4,1,1024]{2,1,0:T(1,128)} %bitcast.15, f32[512,128]{1,0:T(8,128)S(1)} %get-tuple-element.18._.refs_2_), custom_call_target="tpu_custom_call" | custom-call | flops 1 | bytes 1 | tf_op jit(solution)/shard_map/scale_far/pallas_call | solution.py:324
  28.3 1.3 %collective-permute-done.2.refs_0_ = bf16[512,1024]{1,0:T(8,128)(2,1)S(1)} collective-permute-done((bf16[512,1024]{1,0:T(8,128)(2,1)S(1)}, bf16[512,1024]{1,0:T(8,128)(2,1)S(1)}, u32[]{:S(2)}, u32[]{:S(2)}) %collective-permute-start.2) | collective-permute-done | bytes 1048608 | tf_op jit(solution)/shard_map/ppermute | solution.py:456
  29.7 18.6 %project_rest.1 = (bf16[128,2048]{1,0:T(8,128)(2,1)S(1)}, bf16[128,2048]{1,0:T(8,128)(2,1)S(1)}, bf16[128,2048]{1,0:T(8,128)(2,1)S(1)}, bf16[384,2048]{1,0:T(8,1...) custom-call(s32[9]{0:T(128)S(1)} %stack.33.places, ...), custom_call_target="tpu_custom_call", output_to_operand_aliasing={{4}: (9, {}), {5}: (10, {})} | custom-call | flops 12884901888 | bytes 27262976 | tf_op jit(solution)/shard_map/project_rest/pallas_call | solution.py:340
  48.3 2.3 %rest_theirs_far.1 = bf16[1,384,1024]{2,1,0:T(8,128)(2,1)S(1)} custom-call(s32[9]{0:T(128)S(1)} %stack.33.places, bf16[384,2048]{1,0:T(8,128)(2,1)S(1)} %get-tuple-element.28.refs_0_, bf16[2048,4096]{1,0:T(8,128)(2,1)S(1)} %get-tuple-element.27.refs_1_.w_ref), custom_call_target="tpu_custom_call" | custom-call | flops 1 | bytes 1 | tf_op jit(solution)/shard_map/rest_theirs_far/pallas_call | solution.py:406
  50.9 2.7 %collective-permute-start.3 = (bf16[128,2048]{1,0:T(8,128)(2,1)S(1)}, bf16[128,2048]{1,0:T(8,128)(2,1)S(1)}, u32[]{:S(2)}, u32[]{:S(2)}) collective-permute-start(bf16[128,2048]{1,0:T(8,128)(2,1)S(1)} %get-tuple-element.24), channel_id=1, source_target_pairs={{0,4},{4,8},{8,12},{12,16},{16,20},{20,24},{24,28},{28,0},{1,5},{5... | collective-permute-start | bytes 1572872 | tf_op jit(solution)/shard_map/ppermute | solution.py:487
  53.7 2.4 %rest_mine_far.1.refs_2_ = bf16[1,384,1024]{2,1,0:T(8,128)(2,1)S(1)} custom-call(s32[9]{0:T(128)S(1)} %stack.33.places, bf16[384,2048]{1,0:T(8,128)(2,1)S(1)} %get-tuple-element.28.refs_0_, bf16[2048,4096]{1,0:T(8,128)(2,1)S(1)} %get-tuple-element.27.refs_1_.w_ref, bf16[1,384,1024]{2,1,0:T(8,128)(2,1)S(1)} %collective-permute-done.4.refs_2_), custom_call_target="tpu_custom_call" | custom-call | flops 1 | bytes 1 | tf_op jit(solution)/shard_map/rest_mine_far/pallas_call | solution.py:406
  56.0 2.1 %collective-permute-start.11 = (bf16[384,1024]{1,0:T(8,128)(2,1)S(1)}, bf16[384,1024]{1,0:T(8,128)(2,1)S(1)}, u32[]{:S(2)}, u32[]{:S(2)}) collective-permute-start(bf16[384,1024]{1,0:T(8,128)(2,1)S(1)} %bitcast.11), channel_id=1, source_target_pairs={{0,1},{1,0},{2,3},{3,2},{4,5},{5,4},{6,7},{7,6},{8,9},{9,8},{10,11... | collective-permute-start | bytes 2359304 | tf_op jit(solution)/shard_map/ppermute | solution.py:459
  58.2 1.5 %rest_theirs_near.3.refs_1_ = bf16[1,384,512]{2,1,0:T(8,128)(2,1)S(1)} custom-call(s32[9]{0:T(128)S(1)} %stack.33.places, bf16[384,2048]{1,0:T(8,128)(2,1)S(1)} %get-tuple-element.28.refs_0_, bf16[2048,4096]{1,0:T(8,128)(2,1)S(1)} %get-tuple-element.27.refs_1_.w_ref, bf16[1,384,1024]{2,1,0:T(8,128)(2,1)S(1)} %rest_mine_far.1.refs_2_), custom_call_target="tpu_custom_call" | custom-call | flops 1 | bytes 1 | tf_op jit(solution)/shard_map/rest_theirs_near/pallas_call | solution.py:406
  59.7 1.5 %rest_theirs_near.2.refs_0_ = bf16[1,384,512]{2,1,0:T(8,128)(2,1)S(1)} custom-call(s32[9]{0:T(128)S(1)} %stack.33.places, bf16[384,2048]{1,0:T(8,128)(2,1)S(1)} %get-tuple-element.28.refs_0_, bf16[2048,4096]{1,0:T(8,128)(2,1)S(1)} %get-tuple-element.27.refs_1_.w_ref, bf16[1,384,1024]{2,1,0:T(8,128)(2,1)S(1)} %rest_mine_far.1.refs_2_), custom_call_target="tpu_custom_call" | custom-call | flops 1 | bytes 1 | tf_op jit(solution)/shard_map/rest_theirs_near/pallas_call | solution.py:406
  61.3 7.8 %collective-permute-done.3.halo_ref = bf16[128,2048]{1,0:T(8,128)(2,1)S(1)} collective-permute-done((bf16[128,2048]{1,0:T(8,128)(2,1)S(1)}, bf16[128,2048]{1,0:T(8,128)(2,1)S(1)}, u32[]{:S(2)}, u32[]{:S(2)}) %collective-permute-start.3) | collective-permute-done | bytes 524320 | tf_op jit(solution)/shard_map/ppermute | solution.py:487
  69.1 2.0 %gate_first.1 = (bf16[128,2048]{1,0:T(8,128)(2,1)S(1)}, bf16[1,128,1024]{2,1,0:T(8,128)(2,1)S(1)}) custom-call(s32[9]{0:T(128)S(1)} %stack.33.places, bf16[128,2048]{1,0:T(8,128)(2,1)S(1)} %collective-permute-done.3.halo_ref, bf16[128,2048]{1,0:T(8,128)(2,1)S(1)} %get-tuple-element.25.mixed_ref, bf16[128,2048]{1,0:T(8,128)(2,1)S(1)} %get-tuple-element.26.q_ref, ...), custom_call_target="tpu_custom_call" | custom-call | flops 1 | bytes 1 | tf_op jit(solution)/shard_map/gate_first/pallas_call | solution.py:364
  71.7 1.3 %first_mine_far.1.a_ref = f32[1,128,1024]{2,1,0:T(8,128)S(1)} custom-call(s32[9]{0:T(128)S(1)} %stack.33.places, bf16[128,2048]{1,0:T(8,128)(2,1)S(1)} %get-tuple-element.29.refs_0_, bf16[2048,4096]{1,0:T(8,128)(2,1)S(1)} %get-tuple-element.27.refs_1_.w_ref), custom_call_target="tpu_custom_call" | custom-call | flops 1 | bytes 1 | tf_op jit(solution)/shard_map/first_mine_far/pallas_call | solution.py:406
  73.0 1.6 %collective-permute-start.8 = (bf16[128,1024]{1,0:T(8,128)(2,1)S(1)}, bf16[128,1024]{1,0:T(8,128)(2,1)S(1)}, u32[]{:S(2)}, u32[]{:S(2)}) collective-permute-start(bf16[128,1024]{1,0:T(8,128)(2,1)S(1)} %bitcast.12), channel_id=1, source_target_pairs={{0,1},{1,0},{2,3},{3,2},{4,5},{5,4},{6,7},{7,6},{8,9},{9,8},{10,11... | collective-permute-start | bytes 786440 | tf_op jit(solution)/shard_map/ppermute | solution.py:459
  74.6 1.0 %first_theirs_near.3 = bf16[1,128,512]{2,1,0:T(8,128)(2,1)S(1)} custom-call(s32[9]{0:T(128)S(1)} %stack.33.places, bf16[128,2048]{1,0:T(8,128)(2,1)S(1)} %get-tuple-element.29.refs_0_, bf16[2048,4096]{1,0:T(8,128)(2,1)S(1)} %get-tuple-element.27.refs_1_.w_ref, bf16[1,128,1024]{2,1,0:T(8,128)(2,1)S(1)} %added.1.refs_2_), custom_call_target="tpu_custom_call" | custom-call | flops 1 | bytes 1 | tf_op jit(solution)/shard_map/first_theirs_near/pallas_call | solution.py:406
  75.6 1.0 %first_theirs_near.2 = bf16[1,128,512]{2,1,0:T(8,128)(2,1)S(1)} custom-call(s32[9]{0:T(128)S(1)} %stack.33.places, bf16[128,2048]{1,0:T(8,128)(2,1)S(1)} %get-tuple-element.29.refs_0_, bf16[2048,4096]{1,0:T(8,128)(2,1)S(1)} %get-tuple-element.27.refs_1_.w_ref, bf16[1,128,1024]{2,1,0:T(8,128)(2,1)S(1)} %added.1.refs_2_), custom_call_target="tpu_custom_call" | custom-call | flops 1 | bytes 1 | tf_op jit(solution)/shard_map/first_theirs_near/pallas_call | solution.py:406
  77.2 2.3 %rest_mine_near.1.refs_0_ = f32[1,384,1024]{2,1,0:T(8,128)S(1)} custom-call(s32[9]{0:T(128)S(1)} %stack.33.places, bf16[384,2048]{1,0:T(8,128)(2,1)S(1)} %get-tuple-element.28.refs_0_, bf16[2048,4096]{1,0:T(8,128)(2,1)S(1)} %get-tuple-element.27.refs_1_.w_ref, bf16[1,384,512]{2,1,0:T(8,128)(2,1)S(1)} %collective-permute-done.9.refs_2_, ...), custom_call_target="tpu_custom_call" | custom-call | flops 1 | bytes 1 | tf_op jit(solution)/shard_map/rest_mine_near/pallas_call | solution.py:406
  79.6 1.3 %first_mine_near.1.refs_0_ = f32[1,128,1024]{2,1,0:T(8,128)S(1)} custom-call(s32[9]{0:T(128)S(1)} %stack.33.places, bf16[128,2048]{1,0:T(8,128)(2,1)S(1)} %get-tuple-element.29.refs_0_, bf16[2048,4096]{1,0:T(8,128)(2,1)S(1)} %get-tuple-element.27.refs_1_.w_ref, bf16[1,128,512]{2,1,0:T(8,128)(2,1)S(1)} %collective-permute-done.6.refs_2_, ...), custom_call_target="tpu_custom_call" | custom-call | flops 1 | bytes 1 | tf_op jit(solution)/shard_map/first_mine_near/pallas_call | solution.py:406
  80.9 1.0 %total_rows.2.refs_2_ = bf16[512,1024]{1,0:T(8,128)(2,1)} custom-call(f32[1,384,1024]{2,1,0:T(8,128)S(1)} %rest_mine_near.1.refs_0_, bf16[384,1024]{1,0:T(8,128)(2,1)S(1)} %collective-permute-done.11.refs_1_), custom_call_target="tpu_custom_call" | custom-call | flops 1 | bytes 1 | tf_op jit(solution)/shard_map/total_rows/pallas_call | solution.py:433
  81.9 0.8 total_rows.3
  (31 shorter events, 2.5 us)
Async XLA Ops:
  0.0 3.1 %collective-permute-start.1 = (bf16[512,1024]{1,0:T(8,128)(2,1)}, bf16[512,1024]{1,0:T(8,128)(2,1)S(1)}, u32[]{:S(2)}, u32[]{:S(2)}) collective-permute-start(bf16[512,1024]{1,0:T(8,128)(2,1)} %own_ref.1), channel_id=1, source_target_pairs={{0,2},{2,0},{1,3},{3,1},{4,6},{6,4},{5,7},{7,5},{8,10},{10,8},{9,1... | collective-permute-start | bytes 3145736 | tf_op jit(solution)/shard_map/ppermute | solution.py:456
  0.5 26.6 %collective-permute-start = (bf16[512,1024]{1,0:T(8,128)(2,1)}, bf16[512,1024]{1,0:T(8,128)(2,1)S(1)}, u32[]{:S(2)}, u32[]{:S(2)}) collective-permute-start(bf16[512,1024]{1,0:T(8,128)(2,1)} %own_ref.1), channel_id=1, source_target_pairs={{0,1},{1,0},{2,3},{3,2},{4,5},{5,4},{6,7},{7,6},{8,9},{9,8},{10,11... | collective-permute-start | bytes 3145736 | tf_op jit(solution)/shard_map/ppermute | solution.py:459
  3.1 1.0 %copy-start = (bf16[512,1024]{1,0:T(8,128)(2,1)}, bf16[512,1024]{1,0:T(8,128)(2,1)S(1)}, u32[]{:S(2)}) copy-start(bf16[512,1024]{1,0:T(8,128)(2,1)S(1)} %collective-permute-done.1.beside_ref) | copy-start | bytes 3145732
  4.0 1.2 %copy-start.1 = (bf16[512,1024]{1,0:T(8,128)(2,1)S(1)}, bf16[512,1024]{1,0:T(8,128)(2,1)}, u32[]{:S(2)}) copy-start(bf16[512,1024]{1,0:T(8,128)(2,1)} %copy-done) | copy-start | bytes 3145732
  5.3 17.7 %copy-start.4 = (bf16[384,256]{1,0:T(8,128)(2,1)S(1)}, bf16[384,256]{1,0:T(8,128)(2,1)}, u32[]{:S(2)}) copy-start(bf16[384,256]{1,0:T(8,128)(2,1)} %constant.35.clone.of_filter_ref) | copy-start | bytes 589828
  5.3 17.7 %copy-start.5 = (f32[2048]{0:T(1024)S(1)}, f32[2048]{0:T(1024)}, u32[]{:S(2)}) copy-start(f32[2048]{0:T(1024)} %param.13) | copy-start | bytes 24580
  26.8 2.8 %copy-start.2 = (bf16[256,256]{1,0:T(8,128)(2,1)S(1)}, bf16[256,256]{1,0:T(8,128)(2,1)}, u32[]{:S(2)}) copy-start(bf16[256,256]{1,0:T(8,128)(2,1)} %constant.33.clone.refs_6_.fwd_ref) | copy-start | bytes 393220
  26.9 2.8 %copy-start.3 = (bf16[128,256]{1,0:T(8,128)(2,1)S(1)}, bf16[128,256]{1,0:T(8,128)(2,1)}, u32[]{:S(2)}) copy-start(bf16[128,256]{1,0:T(8,128)(2,1)} %constant.34.clone.refs_7_.inv_ref) | copy-start | bytes 196612
  27.0 2.7 %collective-permute-start.2 = (bf16[512,1024]{1,0:T(8,128)(2,1)S(1)}, bf16[512,1024]{1,0:T(8,128)(2,1)S(1)}, u32[]{:S(2)}, u32[]{:S(2)}) collective-permute-start(bf16[512,1024]{1,0:T(8,128)(2,1)S(1)} %held_until.1.refs_0_), channel_id=1, source_target_pairs={{0,2},{2,0},{1,3},{3,1},{4,6},{6,4},{5,7},{7,5},{8,10},{10,8},{9,1... | collective-permute-start | bytes 3145736 | tf_op jit(solution)/shard_map/ppermute | solution.py:456
  50.7 3.0 %collective-permute-start.4 = (bf16[1,384,1024]{2,1,0:T(8,128)(2,1)S(1)}, bf16[1,384,1024]{2,1,0:T(8,128)(2,1)S(1)}, u32[]{:S(2)}, u32[]{:S(2)}) collective-permute-start(bf16[1,384,1024]{2,1,0:T(8,128)(2,1)S(1)} %rest_theirs_far.1), channel_id=1, source_target_pairs={{0,2},{2,0},{1,3},{3,1},{4,6},{6,4},{5,7},{7,5},{8,10},{10,8},{9,1... | collective-permute-start | bytes 2359304 | tf_op jit(solution)/shard_map/ppermute | solution.py:456
  50.9 18.1 %collective-permute-start.3 = (bf16[128,2048]{1,0:T(8,128)(2,1)S(1)}, bf16[128,2048]{1,0:T(8,128)(2,1)S(1)}, u32[]{:S(2)}, u32[]{:S(2)}) collective-permute-start(bf16[128,2048]{1,0:T(8,128)(2,1)S(1)} %get-tuple-element.24), channel_id=1, source_target_pairs={{0,4},{4,8},{8,12},{12,16},{16,20},{20,24},{24,28},{28,0},{1,5},{5... | collective-permute-start | bytes 1572872 | tf_op jit(solution)/shard_map/ppermute | solution.py:487
  56.0 24.8 %collective-permute-start.11 = (bf16[384,1024]{1,0:T(8,128)(2,1)S(1)}, bf16[384,1024]{1,0:T(8,128)(2,1)S(1)}, u32[]{:S(2)}, u32[]{:S(2)}) collective-permute-start(bf16[384,1024]{1,0:T(8,128)(2,1)S(1)} %bitcast.11), channel_id=1, source_target_pairs={{0,1},{1,0},{2,3},{3,2},{4,5},{5,4},{6,7},{7,6},{8,9},{9,8},{10,11... | collective-permute-start | bytes 2359304 | tf_op jit(solution)/shard_map/ppermute | solution.py:459
  61.2 15.5 %collective-permute-start.9 = (bf16[1,384,512]{2,1,0:T(8,128)(2,1)S(1)}, bf16[1,384,512]{2,1,0:T(8,128)(2,1)S(1)}, u32[]{:S(2)}, u32[]{:S(2)}) collective-permute-start(bf16[1,384,512]{2,1,0:T(8,128)(2,1)S(1)} %rest_theirs_near.2.refs_0_), channel_id=1, source_target_pairs={{0,2},{2,0},{1,3},{3,1},{4,6},{6,4},{5,7},{7,5},{8,10},{10,8},{9,1... | collective-permute-start | bytes 1179656 | tf_op jit(solution)/shard_map/ppermute | solution.py:456
  71.1 1.9 %collective-permute-start.5 = (bf16[1,128,1024]{2,1,0:T(8,128)(2,1)S(1)}, bf16[1,128,1024]{2,1,0:T(8,128)(2,1)S(1)}, u32[]{:S(2)}, u32[]{:S(2)}) collective-permute-start(bf16[1,128,1024]{2,1,0:T(8,128)(2,1)S(1)} %get-tuple-element.30), channel_id=1, source_target_pairs={{0,2},{2,0},{1,3},{3,1},{4,6},{6,4},{5,7},{7,5},{8,10},{10,8},{9,1... | collective-permute-start | bytes 786440 | tf_op jit(solution)/shard_map/ppermute | solution.py:456
  71.2 6.0 %collective-permute-start.10 = (bf16[1,384,512]{2,1,0:T(8,128)(2,1)S(1)}, bf16[1,384,512]{2,1,0:T(8,128)(2,1)S(1)}, u32[]{:S(2)}, u32[]{:S(2)}) collective-permute-start(bf16[1,384,512]{2,1,0:T(8,128)(2,1)S(1)} %rest_theirs_near.3.refs_1_), channel_id=1, source_target_pairs={{0,2},{2,0},{1,3},{3,1},{4,6},{6,4},{5,7},{7,5},{8,10},{10,8},{9,1... | collective-permute-start | bytes 1179656 | tf_op jit(solution)/shard_map/ppermute | solution.py:456
  73.0 8.9 %collective-permute-start.8 = (bf16[128,1024]{1,0:T(8,128)(2,1)S(1)}, bf16[128,1024]{1,0:T(8,128)(2,1)S(1)}, u32[]{:S(2)}, u32[]{:S(2)}) collective-permute-start(bf16[128,1024]{1,0:T(8,128)(2,1)S(1)} %bitcast.12), channel_id=1, source_target_pairs={{0,1},{1,0},{2,3},{3,2},{4,5},{5,4},{6,7},{7,6},{8,9},{9,8},{10,11... | collective-permute-start | bytes 786440 | tf_op jit(solution)/shard_map/ppermute | solution.py:459
  76.6 2.9 %collective-permute-start.6 = (bf16[1,128,512]{2,1,0:T(8,128)(2,1)S(1)}, bf16[1,128,512]{2,1,0:T(8,128)(2,1)S(1)}, u32[]{:S(2)}, u32[]{:S(2)}) collective-permute-start(bf16[1,128,512]{2,1,0:T(8,128)(2,1)S(1)} %first_theirs_near.2), channel_id=1, source_target_pairs={{0,2},{2,0},{1,3},{3,1},{4,6},{6,4},{5,7},{7,5},{8,10},{10,8},{9,1... | collective-permute-start | bytes 393224 | tf_op jit(solution)/shard_map/ppermute | solution.py:456
  76.7 2.9 %collective-permute-start.7 = (bf16[1,128,512]{2,1,0:T(8,128)(2,1)S(1)}, bf16[1,128,512]{2,1,0:T(8,128)(2,1)S(1)}, u32[]{:S(2)}, u32[]{:S(2)}) collective-permute-start(bf16[1,128,512]{2,1,0:T(8,128)(2,1)S(1)} %first_theirs_near.3), channel_id=1, source_target_pairs={{0,2},{2,0},{1,3},{3,1},{4,6},{6,4},{5,7},{7,5},{8,10},{10,8},{9,1... | collective-permute-start | bytes 393224 | tf_op jit(solution)/shard_map/ppermute | solution.py:456

commit v7 on v6

--- a/solution.py
+++ b/solution.py
@@ -198,8 +198,8 @@
             before = now
 
 
-def block_columns(places, first, group, width, piece=0, pieces=1):
-    return pl.ds(pl.multiple_of((places[first + group] * pieces + piece) * width, width), width)
+def block_columns(places, first, group, width):
+    return pl.ds(pl.multiple_of(places[first + group] * width, width), width)
 
 
 def first_kernel(has_before, first, places, halo_ref, mixed_ref, q_ref, spec_ref, fwd_ref, inv_ref, w_ref, *refs):
@@ -372,17 +372,19 @@
     )(places, *[in_vmem(x) for x in resident], *waits)
 
 
-def out_kernel(n_add, first, piece, pieces, places, *refs):
-    part_ref, w_ref, add, o_ref = refs[0], refs[1], refs[2 : 2 + n_add], refs[-1]
-    width = o_ref.shape[-1]
-    for g in range(o_ref.shape[0]):
-        at = block_columns(places, first, g, width, piece, pieces)
-        product = dot(part_ref[...], w_ref[:, at])
-        if not add:
-            o_ref[g] = product.astype(o_ref.dtype)
+def out_kernel(n_add, n_out, first, places, *refs):
+    part_ref, w_ref, add, out = refs[0], refs[1], refs[2 : 2 + n_add], refs[-n_out:]
+    width = out[0].shape[-1] * n_out
+    for g in range(out[0].shape[0]):
+        product = dot(part_ref[...], w_ref[:, block_columns(places, first, g, width)])
+        if n_out > 1:
+            for i, o_ref in enumerate(out):
+                o_ref[g] = product[:, i * width // n_out : (i + 1) * width // n_out].astype(o_ref.dtype)
+        elif not add:
+            out[0][g] = product.astype(out[0].dtype)
         for i, x in enumerate(add):
             at = slice(i * width // n_add, (i + 1) * width // n_add)
-            o_ref[g, :, at] = (product[:, at] + x[g].astype(F32)).astype(o_ref.dtype)
+            out[0][g, :, at] = (product[:, at] + x[g].astype(F32)).astype(out[0].dtype)
 
 
 def add_kernel(a_ref, b_ref, o_ref):
@@ -401,17 +403,18 @@
     )(in_vmem(a), in_vmem(b))
 
 
-def project_out(part, out_weight, places, first, n_groups, width, name, add=(), dtype=BF16, waits=(), piece=0, pieces=1):
+def project_out(part, out_weight, places, first, n_groups, width, name, add=(), dtype=BF16, waits=(), n_out=1):
     rows = part.shape[0]
-    return pl.pallas_call(
-        functools.partial(out_kernel, len(add), first, piece, pieces),
+    out = pl.pallas_call(
+        functools.partial(out_kernel, len(add), n_out, first),
         in_specs=[SCALARS] + [RESIDENT] * (2 + len(add)) + [IN_PLACE] * len(waits),
-        out_specs=RESIDENT,
-        out_shape=pltpu.VMEM((n_groups, rows, width // pieces), dtype),
+        out_specs=[RESIDENT] * n_out,
+        out_shape=[pltpu.VMEM((n_groups, rows, width // n_out), dtype)] * n_out,
         compiler_params=pltpu.CompilerParams(vmem_limit_bytes=12 * MIB),
         cost_estimate=BRIEF,
         name=name,
     )(places, *[in_vmem(x) for x in (part, out_weight, *add)], *waits)
+    return out if n_out > 1 else out[0]
 
 
 def total_kernel(n_come, first_row, *refs):
@@ -491,10 +494,7 @@
     theirs = other_core(project(gated_rest, first=theirs_far, n_groups=n_far, name="rest_theirs_far"))
     sent = project(gated_rest, first=mine_far, n_groups=n_far, name="rest_mine_far", add=[theirs])
     come = [chips_along(sent[s - 1], s) for s in shifts]
-    halves = [
-        project(gated_rest, first=theirs_near, n_groups=1, name="rest_theirs_near", piece=i, pieces=2, waits=[sent])
-        for i in range(2)
-    ]
+    halves = project(gated_rest, first=theirs_near, n_groups=1, name="rest_theirs_near", waits=[sent], n_out=2)
 
     gated_first, theirs = gate_first(
         halo, mixed_low, q_low, spectrum, forward, inverse, held_weight, places, has_before, theirs_far, n_far, depth, halves
@@ -502,10 +502,9 @@
     mine = project(gated_first, first=mine_far, n_groups=n_far, name="first_mine_far", dtype=F32)
     sent_first = added(mine, other_core(theirs))
     come_first = [chips_along(sent_first[s - 1], s) for s in shifts]
-    halves_first = [
-        project(gated_first, first=theirs_near, n_groups=1, name="first_theirs_near", piece=i, pieces=2, waits=[sent_first])
-        for i in range(2)
-    ]
+    halves_first = project(
+        gated_first, first=theirs_near, n_groups=1, name="first_theirs_near", waits=[sent_first], n_out=2
+    )
 
     near, near_first = [
         project(part, first=mine_near, n_groups=1, name=name, add=[other_core(x) for x in pieces], dtype=F32)

time: 83.3 us -> 83 us (level)
  Pallas kernels: 59.8 us -> 58.3 us
  waiting for transfers between devices: 9.26 us -> 10.4 us
    pallas_call x9 -> x7, Pallas kernels: 14.6 us -> 13.2 us  [project_out(): pl.pallas_call(functools.partial(out_kernel, len(add), n_out, first), in_...]
  transfers between devices with their start and end apart: 12 -> 12, of which waited for: 3 -> 4; matrix products, arithmetic and copies ran while one was open for 0% -> 0% of each run, Pallas kernels for 46% -> 44%
where the time goes in v7:
time: 83 us; the launch traced here: 82.6 us
  Pallas kernels  58.3 us (70%)
  starting transfers between devices  11.1 us (13%)
  waiting for transfers between devices  10.4 us (13%)
  local copies, waits for them, and re-layouts  2.3 us (3%)
    pallas_call x1, Pallas kernels, project_rest(): pl.pallas_call(functools.partial(last_kernel, first, d_model, taps, n), i...  18.6 us
    pallas_call x1, Pallas kernels, project_local(): pl.pallas_call(functools.partial(local_kernel, first), in_specs=[SCALARS,...  17.7 us
    pallas_call x7, Pallas kernels, project_out(): pl.pallas_call(functools.partial(out_kernel, len(add), n_out, first), in_...  13.2 us
    ppermute x1, waiting for transfers between devices, on_device(): lax.ppermute(tail, 'seq', [(i, (i + 1) % n_seq) for i in range(n_seq)])  8.47 us
    ppermute x3, starting transfers between devices, chips_along(): return lax.ppermute(x, 'tcol', [(i, (i + s) % n_col) for i in range(n_col)])  6.23 us
    pallas_call x1, Pallas kernels, get_ready(): pl.pallas_call(functools.partial(ready_kernel, first, depth, count), in_s...  3.84 us
    ppermute x1, starting transfers between devices, on_device(): lax.ppermute(tail, 'seq', [(i, (i + 1) % n_seq) for i in range(n_seq)])  2.73 us
    unnamed x12, local copies, waits for them, and re-layouts  2.21 us
  transfers between devices with their start and end apart: 12, of which 4 were waited for; matrix products, arithmetic and copies ran while one was open for 0% of the time, Pallas kernels for 44%

profile of v7, /device:TPU:0, one launch (start us, length us, event | category | flops | bytes accessed | tf_op | source)
XLA Modules:
  0.0 82.6 jit_solution(13757656538936848118)
XLA Ops:
  0.5 2.5 %collective-permute-start = (bf16[512,1024]{1,0:T(8,128)(2,1)}, bf16[512,1024]{1,0:T(8,128)(2,1)S(1)}, u32[]{:S(2)}, u32[]{:S(2)}) collective-permute-start(bf16[512,1024]{1,0:T(8,128)(2,1)} %own_ref.1), channel_id=1, source_target_pairs={{0,1},{1,0},{2,3},{3,2},{4,5},{5,4},{6,7},{7,6},{8,9},{9,8},{10,11... | collective-permute-start | bytes 3145736 | tf_op jit(solution)/shard_map/ppermute | solution.py:462
  3.1 1.0 %copy-done = bf16[512,1024]{1,0:T(8,128)(2,1)} copy-done((bf16[512,1024]{1,0:T(8,128)(2,1)}, bf16[512,1024]{1,0:T(8,128)(2,1)S(1)}, u32[]{:S(2)}) %copy-start) | copy-done | bytes 1048600
  4.0 1.2 %copy-done.1 = bf16[512,1024]{1,0:T(8,128)(2,1)S(1)} copy-done((bf16[512,1024]{1,0:T(8,128)(2,1)S(1)}, bf16[512,1024]{1,0:T(8,128)(2,1)}, u32[]{:S(2)}) %copy-start.1) | copy-done | bytes 1048600
  5.3 17.7 %project_local.1 = (bf16[3,512,2048]{2,1,0:T(8,128)(2,1)S(1)}, f32[512,128]{1,0:T(8,128)S(1)}, bf16[2048,4096]{1,0:T(8,128)(2,1)S(1)}) custom-call(s32[9]{0:T(128)S(1)} %stack.33.places, bf16[512,1024]{1,0:T(8,128)(2,1)} %own_ref.1, bf16[512,1024]{1,0:T(8,128)(2,1)S(1)} %copy-done.1, f32[4,1,1024]{2,1,0:T(1,128)} %bitcast.14, ...), custom_call_target="tpu_custom_call" | custom-call | flops 12884901888 | bytes 27262976 | tf_op jit(solution)/shard_map/project_local/pallas_call | solution.py:281
  23.0 3.8 %get_ready.1 = (f32[384,2048]{1,0:T(8,128)S(1)}, bf16[3,3,2048,256]{3,2,1,0:T(8,128)(2,1)S(1)}) custom-call(s32[9]{0:T(128)S(1)} %stack.33.places, f32[128,2048]{1,0:T(8,128)} %taps_ref.1, f32[1,2048]{1,0:T(1,128)S(1)} %bitcast.13, bf16[384,256]{1,0:T(8,128)(2,1)S(1)} %copy-done.4, bf16[3,4096,2048]{2,1,0:T(8,128)(2,1)} %refs_2_.1, ...), custom_call_target="tpu_custom_call" | custom-call | flops 1 | bytes 1 | tf_op jit(solution)/shard_map/get_ready/pallas_call | solution.py:306
  27.2 1.1 %scale_far.1 = (bf16[512,2048]{1,0:T(8,128)(2,1)S(1)}, f32[512,128]{1,0:T(8,128)S(1)}) custom-call(s32[9]{0:T(128)S(1)} %stack.33.places, bf16[512,1024]{1,0:T(8,128)(2,1)S(1)} %held_until.1.refs_0_, f32[4,1,1024]{2,1,0:T(1,128)} %bitcast.15, f32[512,128]{1,0:T(8,128)S(1)} %get-tuple-element.22._.refs_2_), custom_call_target="tpu_custom_call" | custom-call | flops 1 | bytes 1 | tf_op jit(solution)/shard_map/scale_far/pallas_call | solution.py:324
  28.3 1.3 %collective-permute-done.2.refs_0_ = bf16[512,1024]{1,0:T(8,128)(2,1)S(1)} collective-permute-done((bf16[512,1024]{1,0:T(8,128)(2,1)S(1)}, bf16[512,1024]{1,0:T(8,128)(2,1)S(1)}, u32[]{:S(2)}, u32[]{:S(2)}) %collective-permute-start.2) | collective-permute-done | bytes 1048608 | tf_op jit(solution)/shard_map/ppermute | solution.py:459
  29.7 18.6 %project_rest.1 = (bf16[128,2048]{1,0:T(8,128)(2,1)S(1)}, bf16[128,2048]{1,0:T(8,128)(2,1)S(1)}, bf16[128,2048]{1,0:T(8,128)(2,1)S(1)}, bf16[384,2048]{1,0:T(8,1...) custom-call(s32[9]{0:T(128)S(1)} %stack.33.places, ...), custom_call_target="tpu_custom_call", output_to_operand_aliasing={{4}: (9, {}), {5}: (10, {})} | custom-call | flops 12884901888 | bytes 27262976 | tf_op jit(solution)/shard_map/project_rest/pallas_call | solution.py:340
  48.3 2.3 %rest_theirs_far.1 = bf16[1,384,1024]{2,1,0:T(8,128)(2,1)S(1)} custom-call(s32[9]{0:T(128)S(1)} %stack.33.places, bf16[384,2048]{1,0:T(8,128)(2,1)S(1)} %get-tuple-element.32.refs_0_, bf16[2048,4096]{1,0:T(8,128)(2,1)S(1)} %get-tuple-element.31.refs_1_.w_ref), custom_call_target="tpu_custom_call" | custom-call | flops 1 | bytes 1 | tf_op jit(solution)/shard_map/rest_theirs_far/pallas_call | solution.py:408
  50.9 2.7 %collective-permute-start.3 = (bf16[128,2048]{1,0:T(8,128)(2,1)S(1)}, bf16[128,2048]{1,0:T(8,128)(2,1)S(1)}, u32[]{:S(2)}, u32[]{:S(2)}) collective-permute-start(bf16[128,2048]{1,0:T(8,128)(2,1)S(1)} %get-tuple-element.28), channel_id=1, source_target_pairs={{0,4},{4,8},{8,12},{12,16},{16,20},{20,24},{24,28},{28,0},{1,5},{5... | collective-permute-start | bytes 1572872 | tf_op jit(solution)/shard_map/ppermute | solution.py:490
  53.7 2.4 %rest_mine_far.1.refs_2_ = bf16[1,384,1024]{2,1,0:T(8,128)(2,1)S(1)} custom-call(s32[9]{0:T(128)S(1)} %stack.33.places, bf16[384,2048]{1,0:T(8,128)(2,1)S(1)} %get-tuple-element.32.refs_0_, bf16[2048,4096]{1,0:T(8,128)(2,1)S(1)} %get-tuple-element.31.refs_1_.w_ref, bf16[1,384,1024]{2,1,0:T(8,128)(2,1)S(1)} %collective-permute-done.4.refs_2_), custom_call_target="tpu_custom_call" | custom-call | flops 1 | bytes 1 | tf_op jit(solution)/shard_map/rest_mine_far/pallas_call | solution.py:408
  56.0 2.1 %collective-permute-start.11 = (bf16[384,1024]{1,0:T(8,128)(2,1)S(1)}, bf16[384,1024]{1,0:T(8,128)(2,1)S(1)}, u32[]{:S(2)}, u32[]{:S(2)}) collective-permute-start(bf16[384,1024]{1,0:T(8,128)(2,1)S(1)} %bitcast.11), channel_id=1, source_target_pairs={{0,1},{1,0},{2,3},{3,2},{4,5},{5,4},{6,7},{7,6},{8,9},{9,8},{10,11... | collective-permute-start | bytes 2359304 | tf_op jit(solution)/shard_map/ppermute | solution.py:462
  58.2 2.3 %rest_theirs_near.1 = (bf16[1,384,512]{2,1,0:T(8,128)(2,1)S(1)}, bf16[1,384,512]{2,1,0:T(8,128)(2,1)S(1)}) custom-call(s32[9]{0:T(128)S(1)} %stack.33.places, bf16[384,2048]{1,0:T(8,128)(2,1)S(1)} %get-tuple-element.32.refs_0_, bf16[2048,4096]{1,0:T(8,128)(2,1)S(1)} %get-tuple-element.31.refs_1_.w_ref, bf16[1,384,1024]{2,1,0:T(8,128)(2,1)S(1)} %rest_mine_far.1.refs_2_), custom_call_target="tpu_custom_call" | custom-call | flops 1 | bytes 1 | tf_op jit(solution)/shard_map/rest_theirs_near/pallas_call | solution.py:408
  60.6 8.5 %collective-permute-done.3.halo_ref = bf16[128,2048]{1,0:T(8,128)(2,1)S(1)} collective-permute-done((bf16[128,2048]{1,0:T(8,128)(2,1)S(1)}, bf16[128,2048]{1,0:T(8,128)(2,1)S(1)}, u32[]{:S(2)}, u32[]{:S(2)}) %collective-permute-start.3) | collective-permute-done | bytes 524320 | tf_op jit(solution)/shard_map/ppermute | solution.py:490
  69.1 2.0 %gate_first.1 = (bf16[128,2048]{1,0:T(8,128)(2,1)S(1)}, bf16[1,128,1024]{2,1,0:T(8,128)(2,1)S(1)}) custom-call(s32[9]{0:T(128)S(1)} %stack.33.places, bf16[128,2048]{1,0:T(8,128)(2,1)S(1)} %collective-permute-done.3.halo_ref, bf16[128,2048]{1,0:T(8,128)(2,1)S(1)} %get-tuple-element.29.mixed_ref, bf16[128,2048]{1,0:T(8,128)(2,1)S(1)} %get-tuple-element.30.q_ref, ...), custom_call_target="tpu_custom_call" | custom-call | flops 1 | bytes 1 | tf_op jit(solution)/shard_map/gate_first/pallas_call | solution.py:364
  71.2 0.5 collective-permute-start.10
  71.7 1.3 %first_mine_far.1.a_ref = f32[1,128,1024]{2,1,0:T(8,128)S(1)} custom-call(s32[9]{0:T(128)S(1)} %stack.33.places, bf16[128,2048]{1,0:T(8,128)(2,1)S(1)} %get-tuple-element.35.refs_0_, bf16[2048,4096]{1,0:T(8,128)(2,1)S(1)} %get-tuple-element.31.refs_1_.w_ref), custom_call_target="tpu_custom_call" | custom-call | flops 1 | bytes 1 | tf_op jit(solution)/shard_map/first_mine_far/pallas_call | solution.py:408
  73.0 1.6 %collective-permute-start.8 = (bf16[128,1024]{1,0:T(8,128)(2,1)S(1)}, bf16[128,1024]{1,0:T(8,128)(2,1)S(1)}, u32[]{:S(2)}, u32[]{:S(2)}) collective-permute-start(bf16[128,1024]{1,0:T(8,128)(2,1)S(1)} %bitcast.12), channel_id=1, source_target_pairs={{0,1},{1,0},{2,3},{3,2},{4,5},{5,4},{6,7},{7,6},{8,9},{9,8},{10,11... | collective-permute-start | bytes 786440 | tf_op jit(solution)/shard_map/ppermute | solution.py:462
  74.6 1.3 %first_theirs_near.1 = (bf16[1,128,512]{2,1,0:T(8,128)(2,1)S(1)}, bf16[1,128,512]{2,1,0:T(8,128)(2,1)S(1)}) custom-call(s32[9]{0:T(128)S(1)} %stack.33.places, bf16[128,2048]{1,0:T(8,128)(2,1)S(1)} %get-tuple-element.35.refs_0_, bf16[2048,4096]{1,0:T(8,128)(2,1)S(1)} %get-tuple-element.31.refs_1_.w_ref, bf16[1,128,1024]{2,1,0:T(8,128)(2,1)S(1)} %added.1.refs_2_), custom_call_target="tpu_custom_call" | custom-call | flops 1 | bytes 1 | tf_op jit(solution)/shard_map/first_theirs_near/pallas_call | solution.py:408
  76.0 0.5 collective-permute-start.7
  76.5 2.3 %rest_mine_near.1.refs_0_ = f32[1,384,1024]{2,1,0:T(8,128)S(1)} custom-call(s32[9]{0:T(128)S(1)} %stack.33.places, bf16[384,2048]{1,0:T(8,128)(2,1)S(1)} %get-tuple-element.32.refs_0_, bf16[2048,4096]{1,0:T(8,128)(2,1)S(1)} %get-tuple-element.31.refs_1_.w_ref, bf16[1,384,512]{2,1,0:T(8,128)(2,1)S(1)} %collective-permute-done.9.refs_2_, ...), custom_call_target="tpu_custom_call" | custom-call | flops 1 | bytes 1 | tf_op jit(solution)/shard_map/rest_mine_near/pallas_call | solution.py:408
  78.8 1.3 %first_mine_near.1.refs_0_ = f32[1,128,1024]{2,1,0:T(8,128)S(1)} custom-call(s32[9]{0:T(128)S(1)} %stack.33.places, bf16[128,2048]{1,0:T(8,128)(2,1)S(1)} %get-tuple-element.35.refs_0_, bf16[2048,4096]{1,0:T(8,128)(2,1)S(1)} %get-tuple-element.31.refs_1_.w_ref, bf16[1,128,512]{2,1,0:T(8,128)(2,1)S(1)} %collective-permute-done.6.refs_2_, ...), custom_call_target="tpu_custom_call" | custom-call | flops 1 | bytes 1 | tf_op jit(solution)/shard_map/first_mine_near/pallas_call | solution.py:408
  80.1 1.0 %total_rows.2.refs_2_ = bf16[512,1024]{1,0:T(8,128)(2,1)} custom-call(f32[1,384,1024]{2,1,0:T(8,128)S(1)} %rest_mine_near.1.refs_0_, bf16[384,1024]{1,0:T(8,128)(2,1)S(1)} %collective-permute-done.11.refs_1_), custom_call_target="tpu_custom_call" | custom-call | flops 1 | bytes 1 | tf_op jit(solution)/shard_map/total_rows/pallas_call | solution.py:436
  81.6 0.8 total_rows.3
  (29 shorter events, 1.9 us)
Async XLA Ops:
  0.0 3.1 %collective-permute-start.1 = (bf16[512,1024]{1,0:T(8,128)(2,1)}, bf16[512,1024]{1,0:T(8,128)(2,1)S(1)}, u32[]{:S(2)}, u32[]{:S(2)}) collective-permute-start(bf16[512,1024]{1,0:T(8,128)(2,1)} %own_ref.1), channel_id=1, source_target_pairs={{0,2},{2,0},{1,3},{3,1},{4,6},{6,4},{5,7},{7,5},{8,10},{10,8},{9,1... | collective-permute-start | bytes 3145736 | tf_op jit(solution)/shard_map/ppermute | solution.py:459
  0.5 26.6 %collective-permute-start = (bf16[512,1024]{1,0:T(8,128)(2,1)}, bf16[512,1024]{1,0:T(8,128)(2,1)S(1)}, u32[]{:S(2)}, u32[]{:S(2)}) collective-permute-start(bf16[512,1024]{1,0:T(8,128)(2,1)} %own_ref.1), channel_id=1, source_target_pairs={{0,1},{1,0},{2,3},{3,2},{4,5},{5,4},{6,7},{7,6},{8,9},{9,8},{10,11... | collective-permute-start | bytes 3145736 | tf_op jit(solution)/shard_map/ppermute | solution.py:462
  3.1 1.0 %copy-start = (bf16[512,1024]{1,0:T(8,128)(2,1)}, bf16[512,1024]{1,0:T(8,128)(2,1)S(1)}, u32[]{:S(2)}) copy-start(bf16[512,1024]{1,0:T(8,128)(2,1)S(1)} %collective-permute-done.1.beside_ref) | copy-start | bytes 3145732
  4.0 1.2 %copy-start.1 = (bf16[512,1024]{1,0:T(8,128)(2,1)S(1)}, bf16[512,1024]{1,0:T(8,128)(2,1)}, u32[]{:S(2)}) copy-start(bf16[512,1024]{1,0:T(8,128)(2,1)} %copy-done) | copy-start | bytes 3145732
  5.3 17.7 %copy-start.4 = (bf16[384,256]{1,0:T(8,128)(2,1)S(1)}, bf16[384,256]{1,0:T(8,128)(2,1)}, u32[]{:S(2)}) copy-start(bf16[384,256]{1,0:T(8,128)(2,1)} %constant.35.clone.of_filter_ref) | copy-start | bytes 589828
  5.3 17.7 %copy-start.5 = (f32[2048]{0:T(1024)S(1)}, f32[2048]{0:T(1024)}, u32[]{:S(2)}) copy-start(f32[2048]{0:T(1024)} %param.13) | copy-start | bytes 24580
  26.8 2.8 %copy-start.2 = (bf16[256,256]{1,0:T(8,128)(2,1)S(1)}, bf16[256,256]{1,0:T(8,128)(2,1)}, u32[]{:S(2)}) copy-start(bf16[256,256]{1,0:T(8,128)(2,1)} %constant.33.clone.refs_6_.fwd_ref) | copy-start | bytes 393220
  26.9 2.8 %copy-start.3 = (bf16[128,256]{1,0:T(8,128)(2,1)S(1)}, bf16[128,256]{1,0:T(8,128)(2,1)}, u32[]{:S(2)}) copy-start(bf16[128,256]{1,0:T(8,128)(2,1)} %constant.34.clone.refs_7_.inv_ref) | copy-start | bytes 196612
  27.0 2.7 %collective-permute-start.2 = (bf16[512,1024]{1,0:T(8,128)(2,1)S(1)}, bf16[512,1024]{1,0:T(8,128)(2,1)S(1)}, u32[]{:S(2)}, u32[]{:S(2)}) collective-permute-start(bf16[512,1024]{1,0:T(8,128)(2,1)S(1)} %held_until.1.refs_0_), channel_id=1, source_target_pairs={{0,2},{2,0},{1,3},{3,1},{4,6},{6,4},{5,7},{7,5},{8,10},{10,8},{9,1... | collective-permute-start | bytes 3145736 | tf_op jit(solution)/shard_map/ppermute | solution.py:459
  50.7 3.0 %collective-permute-start.4 = (bf16[1,384,1024]{2,1,0:T(8,128)(2,1)S(1)}, bf16[1,384,1024]{2,1,0:T(8,128)(2,1)S(1)}, u32[]{:S(2)}, u32[]{:S(2)}) collective-permute-start(bf16[1,384,1024]{2,1,0:T(8,128)(2,1)S(1)} %rest_theirs_far.1), channel_id=1, source_target_pairs={{0,2},{2,0},{1,3},{3,1},{4,6},{6,4},{5,7},{7,5},{8,10},{10,8},{9,1... | collective-permute-start | bytes 2359304 | tf_op jit(solution)/shard_map/ppermute | solution.py:459
  50.9 18.1 %collective-permute-start.3 = (bf16[128,2048]{1,0:T(8,128)(2,1)S(1)}, bf16[128,2048]{1,0:T(8,128)(2,1)S(1)}, u32[]{:S(2)}, u32[]{:S(2)}) collective-permute-start(bf16[128,2048]{1,0:T(8,128)(2,1)S(1)} %get-tuple-element.28), channel_id=1, source_target_pairs={{0,4},{4,8},{8,12},{12,16},{16,20},{20,24},{24,28},{28,0},{1,5},{5... | collective-permute-start | bytes 1572872 | tf_op jit(solution)/shard_map/ppermute | solution.py:490
  56.0 24.1 %collective-permute-start.11 = (bf16[384,1024]{1,0:T(8,128)(2,1)S(1)}, bf16[384,1024]{1,0:T(8,128)(2,1)S(1)}, u32[]{:S(2)}, u32[]{:S(2)}) collective-permute-start(bf16[384,1024]{1,0:T(8,128)(2,1)S(1)} %bitcast.11), channel_id=1, source_target_pairs={{0,1},{1,0},{2,3},{3,2},{4,5},{5,4},{6,7},{7,6},{8,9},{9,8},{10,11... | collective-permute-start | bytes 2359304 | tf_op jit(solution)/shard_map/ppermute | solution.py:462
  60.5 15.4 %collective-permute-start.9 = (bf16[1,384,512]{2,1,0:T(8,128)(2,1)S(1)}, bf16[1,384,512]{2,1,0:T(8,128)(2,1)S(1)}, u32[]{:S(2)}, u32[]{:S(2)}) collective-permute-start(bf16[1,384,512]{2,1,0:T(8,128)(2,1)S(1)} %get-tuple-element.33.refs_0_), channel_id=1, source_target_pairs={{0,2},{2,0},{1,3},{3,1},{4,6},{6,4},{5,7},{7,5},{8,10},{10,8},{9,1... | collective-permute-start | bytes 1179656 | tf_op jit(solution)/shard_map/ppermute | solution.py:459
  71.1 1.9 %collective-permute-start.5 = (bf16[1,128,1024]{2,1,0:T(8,128)(2,1)S(1)}, bf16[1,128,1024]{2,1,0:T(8,128)(2,1)S(1)}, u32[]{:S(2)}, u32[]{:S(2)}) collective-permute-start(bf16[1,128,1024]{2,1,0:T(8,128)(2,1)S(1)} %get-tuple-element.36), channel_id=1, source_target_pairs={{0,2},{2,0},{1,3},{3,1},{4,6},{6,4},{5,7},{7,5},{8,10},{10,8},{9,1... | collective-permute-start | bytes 786440 | tf_op jit(solution)/shard_map/ppermute | solution.py:459
  71.2 5.3 %collective-permute-start.10 = (bf16[1,384,512]{2,1,0:T(8,128)(2,1)S(1)}, bf16[1,384,512]{2,1,0:T(8,128)(2,1)S(1)}, u32[]{:S(2)}, u32[]{:S(2)}) collective-permute-start(bf16[1,384,512]{2,1,0:T(8,128)(2,1)S(1)} %get-tuple-element.34.refs_1_), channel_id=1, source_target_pairs={{0,2},{2,0},{1,3},{3,1},{4,6},{6,4},{5,7},{7,5},{8,10},{10,8},{9,1... | collective-permute-start | bytes 1179656 | tf_op jit(solution)/shard_map/ppermute | solution.py:459
  73.0 8.6 %collective-permute-start.8 = (bf16[128,1024]{1,0:T(8,128)(2,1)S(1)}, bf16[128,1024]{1,0:T(8,128)(2,1)S(1)}, u32[]{:S(2)}, u32[]{:S(2)}) collective-permute-start(bf16[128,1024]{1,0:T(8,128)(2,1)S(1)} %bitcast.12), channel_id=1, source_target_pairs={{0,1},{1,0},{2,3},{3,2},{4,5},{5,4},{6,7},{7,6},{8,9},{9,8},{10,11... | collective-permute-start | bytes 786440 | tf_op jit(solution)/shard_map/ppermute | solution.py:462
  75.9 2.9 %collective-permute-start.6 = (bf16[1,128,512]{2,1,0:T(8,128)(2,1)S(1)}, bf16[1,128,512]{2,1,0:T(8,128)(2,1)S(1)}, u32[]{:S(2)}, u32[]{:S(2)}) collective-permute-start(bf16[1,128,512]{2,1,0:T(8,128)(2,1)S(1)} %get-tuple-element.37), channel_id=1, source_target_pairs={{0,2},{2,0},{1,3},{3,1},{4,6},{6,4},{5,7},{7,5},{8,10},{10,8},{9,1... | collective-permute-start | bytes 393224 | tf_op jit(solution)/shard_map/ppermute | solution.py:459
  76.0 2.9 %collective-permute-start.7 = (bf16[1,128,512]{2,1,0:T(8,128)(2,1)S(1)}, bf16[1,128,512]{2,1,0:T(8,128)(2,1)S(1)}, u32[]{:S(2)}, u32[]{:S(2)}) collective-permute-start(bf16[1,128,512]{2,1,0:T(8,128)(2,1)S(1)} %get-tuple-element.38), channel_id=1, source_target_pairs={{0,2},{2,0},{1,3},{3,1},{4,6},{6,4},{5,7},{7,5},{8,10},{10,8},{9,1... | collective-permute-start | bytes 393224 | tf_op jit(solution)/shard_map/ppermute | solution.py:459

commit v8 on v7

--- a/solution.py
+++ b/solution.py
@@ -69,7 +69,7 @@
     return jnp.sum(x * x, axis=1, keepdims=True)
 
 
-def products(copies, tiles, xg_ref, ring_ref, loaded, use):
+def products(copies, tiles, xg_ref, ring_ref, loaded, use, begun_ref=None, done=0):
     ahead = min(SLOTS - 1, tiles)
 
     def step(tile, _):
@@ -87,7 +87,12 @@
         use(tile, [dot(xg_ref[...], ring_ref[slot, j]) for j in range(3)])
         return 0
 
-    lax.fori_loop(0, tiles, step, 0)
+    if done:
+        if ahead < tiles:
+            for copy in copies(ahead):
+                copy.start()
+        use(0, [begun_ref[j].astype(F32) + dot(xg_ref[:, done:], ring_ref[0, j, done:]) for j in range(3)])
+    lax.fori_loop(1 if done else 0, tiles, step, 0)
 
 
 def local_kernel(first, places, own_ref, beside_ref, gain_ref, weight_ref, out_w_ref, acc_ref, ssq_ref, held_w_ref,
@@ -148,12 +153,15 @@
 
 def scaled_kernel(first, n_lhs, places, *refs):
     tokens = refs[:n_lhs]
-    gain_ref, ssq_in_ref, xg_ref, ssq_ref = refs[n_lhs:]
+    gain_ref, ssq_in_ref, ring_ref, xg_ref, ssq_ref, begun_ref = refs[n_lhs:]
     depth = tokens[0].shape[1]
     total = ssq_in_ref[...]
     for i, x_ref in enumerate(tokens):
         total = total + scaled(x_ref, gain_ref[places[first + i]], xg_ref, slice(i * depth, (i + 1) * depth))
     ssq_ref[...] = total
+    half = n_lhs * depth
+    for j in range(3):
+        begun_ref[j] = dot(xg_ref[:, :half], ring_ref[0, j, :half]).astype(BF16)
 
 
 def gate(before, now, query, at, spec_ref, fwd_ref, inv_ref):
@@ -164,8 +172,8 @@
 
 def last_kernel(first, d_model, taps, n_lhs, places, *refs):
     tokens = refs[:n_lhs]
-    gain_ref, weight_ref, acc_ref, ssq_ref, spec_ref, fwd_ref, inv_ref, _, _ = refs[n_lhs : n_lhs + 9]
-    tail_ref, q_ref, mixed_ref, gated_ref, xg_ref, ring_ref, q_rest, mixed_rest, sem = refs[n_lhs + 9 :]
+    gain_ref, weight_ref, acc_ref, ssq_ref, begun_ref, spec_ref, fwd_ref, inv_ref, _, _ = refs[n_lhs : n_lhs + 10]
+    tail_ref, q_ref, mixed_ref, gated_ref, xg_ref, ring_ref, mixed_rest, sem = refs[n_lhs + 10 :]
     channels, ct = weight_ref.shape[2], ring_ref.shape[3]
     tiles = channels // ct
     depth = tokens[0].shape[1]
@@ -181,12 +189,12 @@
         query, keys, values = [((acc_ref[j, :, at].astype(F32) + streams[j]) * scale).astype(BF16) for j in range(3)]
         mixed = (keys.astype(F32) * values.astype(F32)).astype(BF16)
         q_ref[:, at] = query[:taps]
-        q_rest[:, at] = query[taps:]
+        gated_ref[:, at] = query[taps:]
         mixed_ref[:, at] = mixed[:taps]
         mixed_rest[:, at] = mixed[taps:]
         tail_ref[:, at] = mixed[mixed.shape[0] - taps :]
 
-    products(copies, tiles, xg_ref, ring_ref, min(SLOTS - 1, tiles), use)
+    products(copies, tiles, xg_ref, ring_ref, min(SLOTS - 1, tiles), use, begun_ref, n_lhs * depth)
     wide = column_tile(channels, 2048)
     for at in range(0, channels, wide):
         at = slice(at, at + wide)
@@ -194,7 +202,7 @@
         for row in range(0, mixed_rest.shape[0], taps):
             rows = slice(row, row + taps)
             now = mixed_rest[rows, at]
-            gated_ref[rows, at] = gate(before, now, q_rest[rows, at], at, spec_ref, fwd_ref, inv_ref)
+            gated_ref[rows, at] = gate(before, now, gated_ref[rows, at], at, spec_ref, fwd_ref, inv_ref)
             before = now
 
 
@@ -319,17 +327,21 @@
     )(places, in_hbm(filter_taps), conv_skip.reshape(1, -1), of_filter, in_hbm(in_weight), wait)
 
 
-def scale_far(far, places, first, norm_gain, ssq):
+def scale_far(far, places, first, norm_gain, ssq, ring):
     n, (rows, depth) = len(far), far[0].shape
     return pl.pallas_call(
         functools.partial(scaled_kernel, first, n),
-        in_specs=[SCALARS] + [RESIDENT] * (n + 2),
-        out_specs=[RESIDENT] * 2,
-        out_shape=[pltpu.VMEM((rows, 2 * n * depth), BF16), pltpu.VMEM(ssq.shape, F32)],
+        in_specs=[SCALARS] + [RESIDENT] * (n + 3),
+        out_specs=[RESIDENT] * 3,
+        out_shape=[
+            pltpu.VMEM((rows, 2 * n * depth), BF16),
+            pltpu.VMEM(ssq.shape, F32),
+            pltpu.VMEM((3, rows, ring.shape[3]), BF16),
+        ],
         compiler_params=pltpu.CompilerParams(vmem_limit_bytes=8 * MIB),
         cost_estimate=BRIEF,
         name="scale_far",
-    )(places, *[in_vmem(x) for x in far], gain_rows(norm_gain, depth), in_vmem(ssq))
+    )(places, *[in_vmem(x) for x in far], gain_rows(norm_gain, depth), *[in_vmem(x) for x in (ssq, ring)])
 
 
 def project_rest(lhs, places, first, norm_gain, in_weight, resident, xg, ring, d_model, taps):
@@ -344,8 +356,8 @@
         out_shape=[pltpu.VMEM((r, channels), BF16) for r in (taps, taps, taps, rest)]
         + [pltpu.VMEM(x.shape, BF16) for x in (xg, ring)],
         input_output_aliases={at: 4, at + 1: 5},
-        scratch_shapes=[pltpu.VMEM((rest, channels), BF16)] * 2 + [pltpu.SemaphoreType.DMA((SLOTS, 2 * n))],
-        compiler_params=pltpu.CompilerParams(vmem_limit_bytes=4 * rest * channels + 10 * MIB),
+        scratch_shapes=[pltpu.VMEM((rest, channels), BF16)] + [pltpu.SemaphoreType.DMA((SLOTS, 2 * n))],
+        compiler_params=pltpu.CompilerParams(vmem_limit_bytes=2 * rest * channels + 6 * MIB),
         cost_estimate=cost(rows, d_model // 2, 3 * channels),
         name="project_rest",
     )(
@@ -366,7 +378,7 @@
         in_specs=[SCALARS] + [RESIDENT] * len(resident) + [IN_PLACE] * len(waits),
         out_specs=[RESIDENT] * 2,
         out_shape=[pltpu.VMEM((taps, channels), BF16), pltpu.VMEM((n_far, taps, width), BF16)],
-        compiler_params=pltpu.CompilerParams(vmem_limit_bytes=12 * MIB),
+        compiler_params=pltpu.CompilerParams(vmem_limit_bytes=10 * MIB),
         cost_estimate=BRIEF,
         name="gate_first",
     )(places, *[in_vmem(x) for x in resident], *waits)
@@ -410,7 +422,7 @@
         in_specs=[SCALARS] + [RESIDENT] * (2 + len(add)) + [IN_PLACE] * len(waits),
         out_specs=[RESIDENT] * n_out,
         out_shape=[pltpu.VMEM((n_groups, rows, width // n_out), dtype)] * n_out,
-        compiler_params=pltpu.CompilerParams(vmem_limit_bytes=12 * MIB),
+        compiler_params=pltpu.CompilerParams(vmem_limit_bytes=10 * MIB),
         cost_estimate=BRIEF,
         name=name,
     )(places, *[in_vmem(x) for x in (part, out_weight, *add)], *waits)
@@ -482,8 +494,8 @@
     spectrum, ring = get_ready(places, 2, depth, 2 * n_far, filter_taps, conv_skip, of_filter, in_weight, ssq)
     far = [held_until(x, spectrum) for x in far]
     lhs = [other_core(x) for x in far]
-    xg, ssq = scale_far(far, places, 2, norm_gain, ssq)
-    resident = [acc, ssq, spectrum, forward, inverse]
+    xg, ssq, begun = scale_far(far, places, 2, norm_gain, ssq, ring)
+    resident = [acc, ssq, begun, spectrum, forward, inverse]
     tail, q_low, mixed_low, gated_rest = project_rest(
         lhs, places, 2, norm_gain, in_weight, resident, xg, ring, d_model, taps
     )

time: 83 us -> 82.5 us (level)
    pallas_call x1, Pallas kernels: 1.1 us -> 2.3 us  [scale_far(): pl.pallas_call(functools.partial(scaled_kernel, first, n), in_specs=[SCAL...]
    ppermute x8, waiting for transfers between devices: 1.37 us -> 0.49 us  [other_core(): return lax.ppermute(x, 'trow', [(0, 1), (1, 0)])]
  transfers between devices with their start and end apart: 12 -> 12, of which waited for: 4 -> 4; matrix products, arithmetic and copies ran while one was open for 0% -> 0% of each run, Pallas kernels for 44% -> 46%
where the time goes in v8:
time: 82.5 us; the launch traced here: 82.2 us
  Pallas kernels  58.9 us (71%)
  starting transfers between devices  10.9 us (13%)
  waiting for transfers between devices  9.69 us (12%)
  local copies, waits for them, and re-layouts  2.29 us (3%)
    pallas_call x1, Pallas kernels, project_rest(): pl.pallas_call(functools.partial(last_kernel, first, d_model, taps, n), i...  18 us
    pallas_call x1, Pallas kernels, project_local(): pl.pallas_call(functools.partial(local_kernel, first), in_specs=[SCALARS,...  17.7 us
    pallas_call x7, Pallas kernels, project_out(): pl.pallas_call(functools.partial(out_kernel, len(add), n_out, first), in_...  13.2 us
    ppermute x1, waiting for transfers between devices, on_device(): lax.ppermute(tail, 'seq', [(i, (i + 1) % n_seq) for i in range(n_seq)])  8.46 us
    ppermute x3, starting transfers between devices, chips_along(): return lax.ppermute(x, 'tcol', [(i, (i + s) % n_col) for i in range(n_col)])  6.23 us
    pallas_call x1, Pallas kernels, get_ready(): pl.pallas_call(functools.partial(ready_kernel, first, depth, count), in_s...  3.84 us
    ppermute x1, starting transfers between devices, on_device(): lax.ppermute(tail, 'seq', [(i, (i + 1) % n_seq) for i in range(n_seq)])  2.7 us
    pallas_call x1, Pallas kernels, scale_far(): pl.pallas_call(functools.partial(scaled_kernel, first, n), in_specs=[SCAL...  2.3 us
  transfers between devices with their start and end apart: 12, of which 4 were waited for; matrix products, arithmetic and copies ran while one was open for 0% of the time, Pallas kernels for 46%

profile of v8, /device:TPU:0, one launch (start us, length us, event | category | flops | bytes accessed | tf_op | source)
XLA Modules:
  0.0 82.2 jit_solution(3413274986349328614)
XLA Ops:
  0.5 2.5 %collective-permute-start = (bf16[512,1024]{1,0:T(8,128)(2,1)}, bf16[512,1024]{1,0:T(8,128)(2,1)}, u32[]{:S(2)}, u32[]{:S(2)}) collective-permute-start(bf16[512,1024]{1,0:T(8,128)(2,1)} %own_ref.1), channel_id=1, source_target_pairs={{0,1},{1,0},{2,3},{3,2},{4,5},{5,4},{6,7},{7,6},{8,9},{9,8},{10,11... | collective-permute-start | bytes 3145736 | tf_op jit(solution)/shard_map/ppermute | solution.py:474
  3.1 1.0 %copy-done = bf16[512,1024]{1,0:T(8,128)(2,1)} copy-done((bf16[512,1024]{1,0:T(8,128)(2,1)}, bf16[512,1024]{1,0:T(8,128)(2,1)S(1)}, u32[]{:S(2)}) %copy-start) | copy-done | bytes 1048600
  4.0 1.2 %copy-done.1 = bf16[512,1024]{1,0:T(8,128)(2,1)S(1)} copy-done((bf16[512,1024]{1,0:T(8,128)(2,1)S(1)}, bf16[512,1024]{1,0:T(8,128)(2,1)}, u32[]{:S(2)}) %copy-start.1) | copy-done | bytes 1048600
  5.3 17.7 %project_local.1 = (bf16[3,512,2048]{2,1,0:T(8,128)(2,1)S(1)}, f32[512,128]{1,0:T(8,128)S(1)}, bf16[2048,4096]{1,0:T(8,128)(2,1)S(1)}) custom-call(s32[9]{0:T(128)S(1)} %stack.33.places, bf16[512,1024]{1,0:T(8,128)(2,1)} %own_ref.1, bf16[512,1024]{1,0:T(8,128)(2,1)S(1)} %copy-done.1, f32[4,1,1024]{2,1,0:T(1,128)} %bitcast.14, ...), custom_call_target="tpu_custom_call" | custom-call | flops 12884901888 | bytes 27262976 | tf_op jit(solution)/shard_map/project_local/pallas_call | solution.py:289
  23.0 3.8 %get_ready.1 = (f32[384,2048]{1,0:T(8,128)S(1)}, bf16[3,3,2048,256]{3,2,1,0:T(8,128)(2,1)S(1)}) custom-call(s32[9]{0:T(128)S(1)} %stack.33.places, f32[128,2048]{1,0:T(8,128)} %taps_ref.1, f32[1,2048]{1,0:T(1,128)S(1)} %bitcast.13, bf16[384,256]{1,0:T(8,128)(2,1)S(1)} %copy-done.4, bf16[3,4096,2048]{2,1,0:T(8,128)(2,1)} %refs_2_.1, ...), custom_call_target="tpu_custom_call" | custom-call | flops 1 | bytes 1 | tf_op jit(solution)/shard_map/get_ready/pallas_call | solution.py:314
  27.2 2.3 %scale_far.1 = (bf16[512,2048]{1,0:T(8,128)(2,1)S(1)}, f32[512,128]{1,0:T(8,128)S(1)}, bf16[3,512,256]{2,1,0:T(8,128)(2,1)S(1)}) custom-call(s32[9]{0:T(128)S(1)} %stack.33.places, bf16[512,1024]{1,0:T(8,128)(2,1)} %held_until.1.refs_0_, f32[4,1,1024]{2,1,0:T(1,128)} %bitcast.15, f32[512,128]{1,0:T(8,128)S(1)} %get-tuple-element.23._.refs_2_, ...), custom_call_target="tpu_custom_call" | custom-call | flops 1 | bytes 1 | tf_op jit(solution)/shard_map/scale_far/pallas_call | solution.py:332
  30.0 18.0 %project_rest.1 = (bf16[128,2048]{1,0:T(8,128)(2,1)S(1)}, bf16[128,2048]{1,0:T(8,128)(2,1)S(1)}, bf16[128,2048]{1,0:T(8,128)(2,1)S(1)}, bf16[384,2048]{1,0:T(8,1...) custom-call(s32[9]{0:T(128)S(1)} %stack.33.places, ...), custom_call_target="tpu_custom_call", output_to_operand_aliasing={{4}: (10, {}), {5}: (11, {})} | custom-call | flops 12884901888 | bytes 27262976 | tf_op jit(solution)/shard_map/project_rest/pallas_call | solution.py:352
  48.0 2.3 %rest_theirs_far.1 = bf16[1,384,1024]{2,1,0:T(8,128)(2,1)S(1)} custom-call(s32[9]{0:T(128)S(1)} %stack.33.places, bf16[384,2048]{1,0:T(8,128)(2,1)S(1)} %get-tuple-element.34.refs_0_, bf16[2048,4096]{1,0:T(8,128)(2,1)S(1)} %get-tuple-element.33.refs_1_.w_ref), custom_call_target="tpu_custom_call" | custom-call | flops 1 | bytes 1 | tf_op jit(solution)/shard_map/rest_theirs_far/pallas_call | solution.py:420
  50.6 2.7 %collective-permute-start.3 = (bf16[128,2048]{1,0:T(8,128)(2,1)S(1)}, bf16[128,2048]{1,0:T(8,128)(2,1)S(1)}, u32[]{:S(2)}, u32[]{:S(2)}) collective-permute-start(bf16[128,2048]{1,0:T(8,128)(2,1)S(1)} %get-tuple-element.30), channel_id=1, source_target_pairs={{0,4},{4,8},{8,12},{12,16},{16,20},{20,24},{24,28},{28,0},{1,5},{5... | collective-permute-start | bytes 1572872 | tf_op jit(solution)/shard_map/ppermute | solution.py:502
  53.3 2.4 %rest_mine_far.1.refs_2_ = bf16[1,384,1024]{2,1,0:T(8,128)(2,1)S(1)} custom-call(s32[9]{0:T(128)S(1)} %stack.33.places, bf16[384,2048]{1,0:T(8,128)(2,1)S(1)} %get-tuple-element.34.refs_0_, bf16[2048,4096]{1,0:T(8,128)(2,1)S(1)} %get-tuple-element.33.refs_1_.w_ref, bf16[1,384,1024]{2,1,0:T(8,128)(2,1)S(1)} %collective-permute-done.4.refs_2_), custom_call_target="tpu_custom_call" | custom-call | flops 1 | bytes 1 | tf_op jit(solution)/shard_map/rest_mine_far/pallas_call | solution.py:420
  55.6 2.1 %collective-permute-start.11 = (bf16[384,1024]{1,0:T(8,128)(2,1)S(1)}, bf16[384,1024]{1,0:T(8,128)(2,1)S(1)}, u32[]{:S(2)}, u32[]{:S(2)}) collective-permute-start(bf16[384,1024]{1,0:T(8,128)(2,1)S(1)} %bitcast.11), channel_id=1, source_target_pairs={{0,1},{1,0},{2,3},{3,2},{4,5},{5,4},{6,7},{7,6},{8,9},{9,8},{10,11... | collective-permute-start | bytes 2359304 | tf_op jit(solution)/shard_map/ppermute | solution.py:474
  57.8 2.3 %rest_theirs_near.1 = (bf16[1,384,512]{2,1,0:T(8,128)(2,1)S(1)}, bf16[1,384,512]{2,1,0:T(8,128)(2,1)S(1)}) custom-call(s32[9]{0:T(128)S(1)} %stack.33.places, bf16[384,2048]{1,0:T(8,128)(2,1)S(1)} %get-tuple-element.34.refs_0_, bf16[2048,4096]{1,0:T(8,128)(2,1)S(1)} %get-tuple-element.33.refs_1_.w_ref, bf16[1,384,1024]{2,1,0:T(8,128)(2,1)S(1)} %rest_mine_far.1.refs_2_), custom_call_target="tpu_custom_call" | custom-call | flops 1 | bytes 1 | tf_op jit(solution)/shard_map/rest_theirs_near/pallas_call | solution.py:420
  60.2 8.5 %collective-permute-done.3.halo_ref = bf16[128,2048]{1,0:T(8,128)(2,1)S(1)} collective-permute-done((bf16[128,2048]{1,0:T(8,128)(2,1)S(1)}, bf16[128,2048]{1,0:T(8,128)(2,1)S(1)}, u32[]{:S(2)}, u32[]{:S(2)}) %collective-permute-start.3) | collective-permute-done | bytes 524320 | tf_op jit(solution)/shard_map/ppermute | solution.py:502
  68.7 2.0 %gate_first.1 = (bf16[128,2048]{1,0:T(8,128)(2,1)S(1)}, bf16[1,128,1024]{2,1,0:T(8,128)(2,1)S(1)}) custom-call(s32[9]{0:T(128)S(1)} %stack.33.places, bf16[128,2048]{1,0:T(8,128)(2,1)S(1)} %collective-permute-done.3.halo_ref, bf16[128,2048]{1,0:T(8,128)(2,1)S(1)} %get-tuple-element.31.mixed_ref, bf16[128,2048]{1,0:T(8,128)(2,1)S(1)} %get-tuple-element.32.q_ref, ...), custom_call_target="tpu_custom_call" | custom-call | flops 1 | bytes 1 | tf_op jit(solution)/shard_map/gate_first/pallas_call | solution.py:376
  70.8 0.5 collective-permute-start.10
  71.3 1.3 %first_mine_far.1.a_ref = f32[1,128,1024]{2,1,0:T(8,128)S(1)} custom-call(s32[9]{0:T(128)S(1)} %stack.33.places, bf16[128,2048]{1,0:T(8,128)(2,1)S(1)} %get-tuple-element.37.refs_0_, bf16[2048,4096]{1,0:T(8,128)(2,1)S(1)} %get-tuple-element.33.refs_1_.w_ref), custom_call_target="tpu_custom_call" | custom-call | flops 1 | bytes 1 | tf_op jit(solution)/shard_map/first_mine_far/pallas_call | solution.py:420
  72.6 1.6 %collective-permute-start.8 = (bf16[128,1024]{1,0:T(8,128)(2,1)S(1)}, bf16[128,1024]{1,0:T(8,128)(2,1)S(1)}, u32[]{:S(2)}, u32[]{:S(2)}) collective-permute-start(bf16[128,1024]{1,0:T(8,128)(2,1)S(1)} %bitcast.12), channel_id=1, source_target_pairs={{0,1},{1,0},{2,3},{3,2},{4,5},{5,4},{6,7},{7,6},{8,9},{9,8},{10,11... | collective-permute-start | bytes 786440 | tf_op jit(solution)/shard_map/ppermute | solution.py:474
  74.2 1.3 %first_theirs_near.1 = (bf16[1,128,512]{2,1,0:T(8,128)(2,1)S(1)}, bf16[1,128,512]{2,1,0:T(8,128)(2,1)S(1)}) custom-call(s32[9]{0:T(128)S(1)} %stack.33.places, bf16[128,2048]{1,0:T(8,128)(2,1)S(1)} %get-tuple-element.37.refs_0_, bf16[2048,4096]{1,0:T(8,128)(2,1)S(1)} %get-tuple-element.33.refs_1_.w_ref, bf16[1,128,1024]{2,1,0:T(8,128)(2,1)S(1)} %added.1.refs_2_), custom_call_target="tpu_custom_call" | custom-call | flops 1 | bytes 1 | tf_op jit(solution)/shard_map/first_theirs_near/pallas_call | solution.py:420
  75.6 0.5 collective-permute-start.7
  76.1 2.3 %rest_mine_near.1.refs_0_ = f32[1,384,1024]{2,1,0:T(8,128)S(1)} custom-call(s32[9]{0:T(128)S(1)} %stack.33.places, bf16[384,2048]{1,0:T(8,128)(2,1)S(1)} %get-tuple-element.34.refs_0_, bf16[2048,4096]{1,0:T(8,128)(2,1)S(1)} %get-tuple-element.33.refs_1_.w_ref, bf16[1,384,512]{2,1,0:T(8,128)(2,1)S(1)} %collective-permute-done.9.refs_2_, ...), custom_call_target="tpu_custom_call" | custom-call | flops 1 | bytes 1 | tf_op jit(solution)/shard_map/rest_mine_near/pallas_call | solution.py:420
  78.4 1.3 %first_mine_near.1.refs_0_ = f32[1,128,1024]{2,1,0:T(8,128)S(1)} custom-call(s32[9]{0:T(128)S(1)} %stack.33.places, bf16[128,2048]{1,0:T(8,128)(2,1)S(1)} %get-tuple-element.37.refs_0_, bf16[2048,4096]{1,0:T(8,128)(2,1)S(1)} %get-tuple-element.33.refs_1_.w_ref, bf16[1,128,512]{2,1,0:T(8,128)(2,1)S(1)} %collective-permute-done.6.refs_2_, ...), custom_call_target="tpu_custom_call" | custom-call | flops 1 | bytes 1 | tf_op jit(solution)/shard_map/first_mine_near/pallas_call | solution.py:420
  79.7 1.0 %total_rows.2.refs_2_ = bf16[512,1024]{1,0:T(8,128)(2,1)} custom-call(f32[1,384,1024]{2,1,0:T(8,128)S(1)} %rest_mine_near.1.refs_0_, bf16[384,1024]{1,0:T(8,128)(2,1)S(1)} %collective-permute-done.11.refs_1_), custom_call_target="tpu_custom_call" | custom-call | flops 1 | bytes 1 | tf_op jit(solution)/shard_map/total_rows/pallas_call | solution.py:448
  80.8 0.5 collective-permute-done.8.refs_1_
  81.2 0.8 total_rows.3
  (29 shorter events, 1.9 us)
Async XLA Ops:
  0.0 3.1 %collective-permute-start.1 = (bf16[512,1024]{1,0:T(8,128)(2,1)}, bf16[512,1024]{1,0:T(8,128)(2,1)S(1)}, u32[]{:S(2)}, u32[]{:S(2)}) collective-permute-start(bf16[512,1024]{1,0:T(8,128)(2,1)} %own_ref.1), channel_id=1, source_target_pairs={{0,2},{2,0},{1,3},{3,1},{4,6},{6,4},{5,7},{7,5},{8,10},{10,8},{9,1... | collective-permute-start | bytes 3145736 | tf_op jit(solution)/shard_map/ppermute | solution.py:471
  0.5 26.7 %collective-permute-start = (bf16[512,1024]{1,0:T(8,128)(2,1)}, bf16[512,1024]{1,0:T(8,128)(2,1)}, u32[]{:S(2)}, u32[]{:S(2)}) collective-permute-start(bf16[512,1024]{1,0:T(8,128)(2,1)} %own_ref.1), channel_id=1, source_target_pairs={{0,1},{1,0},{2,3},{3,2},{4,5},{5,4},{6,7},{7,6},{8,9},{9,8},{10,11... | collective-permute-start | bytes 3145736 | tf_op jit(solution)/shard_map/ppermute | solution.py:474
  3.1 1.0 %copy-start = (bf16[512,1024]{1,0:T(8,128)(2,1)}, bf16[512,1024]{1,0:T(8,128)(2,1)S(1)}, u32[]{:S(2)}) copy-start(bf16[512,1024]{1,0:T(8,128)(2,1)S(1)} %collective-permute-done.1.beside_ref) | copy-start | bytes 3145732
  4.0 1.2 %copy-start.1 = (bf16[512,1024]{1,0:T(8,128)(2,1)S(1)}, bf16[512,1024]{1,0:T(8,128)(2,1)}, u32[]{:S(2)}) copy-start(bf16[512,1024]{1,0:T(8,128)(2,1)} %copy-done) | copy-start | bytes 3145732
  5.3 17.7 %copy-start.4 = (bf16[384,256]{1,0:T(8,128)(2,1)S(1)}, bf16[384,256]{1,0:T(8,128)(2,1)}, u32[]{:S(2)}) copy-start(bf16[384,256]{1,0:T(8,128)(2,1)} %constant.35.clone.of_filter_ref) | copy-start | bytes 589828
  5.3 17.7 %copy-start.5 = (f32[2048]{0:T(1024)S(1)}, f32[2048]{0:T(1024)}, u32[]{:S(2)}) copy-start(f32[2048]{0:T(1024)} %param.13) | copy-start | bytes 24580
  27.1 2.9 %copy-start.2 = (bf16[256,256]{1,0:T(8,128)(2,1)S(1)}, bf16[256,256]{1,0:T(8,128)(2,1)}, u32[]{:S(2)}) copy-start(bf16[256,256]{1,0:T(8,128)(2,1)} %constant.33.clone.refs_7_.fwd_ref) | copy-start | bytes 393220
  27.1 2.9 %copy-start.3 = (bf16[128,256]{1,0:T(8,128)(2,1)S(1)}, bf16[128,256]{1,0:T(8,128)(2,1)}, u32[]{:S(2)}) copy-start(bf16[128,256]{1,0:T(8,128)(2,1)} %constant.34.clone.refs_8_.inv_ref) | copy-start | bytes 196612
  27.1 2.9 %collective-permute-start.2 = (bf16[512,1024]{1,0:T(8,128)(2,1)}, bf16[512,1024]{1,0:T(8,128)(2,1)S(1)}, u32[]{:S(2)}, u32[]{:S(2)}) collective-permute-start(bf16[512,1024]{1,0:T(8,128)(2,1)} %held_until.1.refs_0_), channel_id=1, source_target_pairs={{0,2},{2,0},{1,3},{3,1},{4,6},{6,4},{5,7},{7,5},{8,10},{10,8},{9,1... | collective-permute-start | bytes 3145736 | tf_op jit(solution)/shard_map/ppermute | solution.py:471
  50.4 2.9 %collective-permute-start.4 = (bf16[1,384,1024]{2,1,0:T(8,128)(2,1)S(1)}, bf16[1,384,1024]{2,1,0:T(8,128)(2,1)S(1)}, u32[]{:S(2)}, u32[]{:S(2)}) collective-permute-start(bf16[1,384,1024]{2,1,0:T(8,128)(2,1)S(1)} %rest_theirs_far.1), channel_id=1, source_target_pairs={{0,2},{2,0},{1,3},{3,1},{4,6},{6,4},{5,7},{7,5},{8,10},{10,8},{9,1... | collective-permute-start | bytes 2359304 | tf_op jit(solution)/shard_map/ppermute | solution.py:471
  50.6 18.1 %collective-permute-start.3 = (bf16[128,2048]{1,0:T(8,128)(2,1)S(1)}, bf16[128,2048]{1,0:T(8,128)(2,1)S(1)}, u32[]{:S(2)}, u32[]{:S(2)}) collective-permute-start(bf16[128,2048]{1,0:T(8,128)(2,1)S(1)} %get-tuple-element.30), channel_id=1, source_target_pairs={{0,4},{4,8},{8,12},{12,16},{16,20},{20,24},{24,28},{28,0},{1,5},{5... | collective-permute-start | bytes 1572872 | tf_op jit(solution)/shard_map/ppermute | solution.py:502
  55.6 24.1 %collective-permute-start.11 = (bf16[384,1024]{1,0:T(8,128)(2,1)S(1)}, bf16[384,1024]{1,0:T(8,128)(2,1)S(1)}, u32[]{:S(2)}, u32[]{:S(2)}) collective-permute-start(bf16[384,1024]{1,0:T(8,128)(2,1)S(1)} %bitcast.11), channel_id=1, source_target_pairs={{0,1},{1,0},{2,3},{3,2},{4,5},{5,4},{6,7},{7,6},{8,9},{9,8},{10,11... | collective-permute-start | bytes 2359304 | tf_op jit(solution)/shard_map/ppermute | solution.py:474
  60.1 15.4 %collective-permute-start.9 = (bf16[1,384,512]{2,1,0:T(8,128)(2,1)S(1)}, bf16[1,384,512]{2,1,0:T(8,128)(2,1)S(1)}, u32[]{:S(2)}, u32[]{:S(2)}) collective-permute-start(bf16[1,384,512]{2,1,0:T(8,128)(2,1)S(1)} %get-tuple-element.35.refs_0_), channel_id=1, source_target_pairs={{0,2},{2,0},{1,3},{3,1},{4,6},{6,4},{5,7},{7,5},{8,10},{10,8},{9,1... | collective-permute-start | bytes 1179656 | tf_op jit(solution)/shard_map/ppermute | solution.py:471
  70.7 1.9 %collective-permute-start.5 = (bf16[1,128,1024]{2,1,0:T(8,128)(2,1)S(1)}, bf16[1,128,1024]{2,1,0:T(8,128)(2,1)S(1)}, u32[]{:S(2)}, u32[]{:S(2)}) collective-permute-start(bf16[1,128,1024]{2,1,0:T(8,128)(2,1)S(1)} %get-tuple-element.38), channel_id=1, source_target_pairs={{0,2},{2,0},{1,3},{3,1},{4,6},{6,4},{5,7},{7,5},{8,10},{10,8},{9,1... | collective-permute-start | bytes 786440 | tf_op jit(solution)/shard_map/ppermute | solution.py:471
  70.8 5.3 %collective-permute-start.10 = (bf16[1,384,512]{2,1,0:T(8,128)(2,1)S(1)}, bf16[1,384,512]{2,1,0:T(8,128)(2,1)S(1)}, u32[]{:S(2)}, u32[]{:S(2)}) collective-permute-start(bf16[1,384,512]{2,1,0:T(8,128)(2,1)S(1)} %get-tuple-element.36.refs_1_), channel_id=1, source_target_pairs={{0,2},{2,0},{1,3},{3,1},{4,6},{6,4},{5,7},{7,5},{8,10},{10,8},{9,1... | collective-permute-start | bytes 1179656 | tf_op jit(solution)/shard_map/ppermute | solution.py:471
  72.6 8.6 %collective-permute-start.8 = (bf16[128,1024]{1,0:T(8,128)(2,1)S(1)}, bf16[128,1024]{1,0:T(8,128)(2,1)S(1)}, u32[]{:S(2)}, u32[]{:S(2)}) collective-permute-start(bf16[128,1024]{1,0:T(8,128)(2,1)S(1)} %bitcast.12), channel_id=1, source_target_pairs={{0,1},{1,0},{2,3},{3,2},{4,5},{5,4},{6,7},{7,6},{8,9},{9,8},{10,11... | collective-permute-start | bytes 786440 | tf_op jit(solution)/shard_map/ppermute | solution.py:474
  75.5 2.9 %collective-permute-start.6 = (bf16[1,128,512]{2,1,0:T(8,128)(2,1)S(1)}, bf16[1,128,512]{2,1,0:T(8,128)(2,1)S(1)}, u32[]{:S(2)}, u32[]{:S(2)}) collective-permute-start(bf16[1,128,512]{2,1,0:T(8,128)(2,1)S(1)} %get-tuple-element.39), channel_id=1, source_target_pairs={{0,2},{2,0},{1,3},{3,1},{4,6},{6,4},{5,7},{7,5},{8,10},{10,8},{9,1... | collective-permute-start | bytes 393224 | tf_op jit(solution)/shard_map/ppermute | solution.py:471
  75.6 2.9 %collective-permute-start.7 = (bf16[1,128,512]{2,1,0:T(8,128)(2,1)S(1)}, bf16[1,128,512]{2,1,0:T(8,128)(2,1)S(1)}, u32[]{:S(2)}, u32[]{:S(2)}) collective-permute-start(bf16[1,128,512]{2,1,0:T(8,128)(2,1)S(1)} %get-tuple-element.40), channel_id=1, source_target_pairs={{0,2},{2,0},{1,3},{3,1},{4,6},{6,4},{5,7},{7,5},{8,10},{10,8},{9,1... | collective-permute-start | bytes 393224 | tf_op jit(solution)/shard_map/ppermute | solution.py:471

commit v9 on v8

--- a/solution.py
+++ b/solution.py
@@ -216,7 +216,7 @@
     ct = column_tile(channels, 2048)
     for at in range(0, channels, ct):
         at = slice(at, at + ct)
-        before = jnp.where(places[has_before] > 0, halo_ref[:, at].astype(F32), 0.0).astype(BF16)
+        before = jnp.where(places[has_before] > 0, halo_ref[:, at], jnp.zeros_like(halo_ref[:, at]))
         gated_ref[:, at] = gate(before, mixed_ref[:, at], q_ref[:, at], at, spec_ref, fwd_ref, inv_ref)
     n_far, _, width = far_ref.shape
     for g in range(n_far):

time: 82.5 us -> 82.5 us (level)
  no operation moved by 1% of the time
where the time goes in v9:
time: 82.5 us; the launch traced here: 82.2 us
  Pallas kernels  59 us (72%)
  starting transfers between devices  10.9 us (13%)
  waiting for transfers between devices  9.69 us (12%)
  local copies, waits for them, and re-layouts  2.29 us (3%)
    pallas_call x1, Pallas kernels, project_rest(): pl.pallas_call(functools.partial(last_kernel, first, d_model, taps, n), i...  18 us
    pallas_call x1, Pallas kernels, project_local(): pl.pallas_call(functools.partial(local_kernel, first), in_specs=[SCALARS,...  17.7 us
    pallas_call x7, Pallas kernels, project_out(): pl.pallas_call(functools.partial(out_kernel, len(add), n_out, first), in_...  13.2 us
    ppermute x1, waiting for transfers between devices, on_device(): lax.ppermute(tail, 'seq', [(i, (i + 1) % n_seq) for i in range(n_seq)])  8.46 us
    ppermute x3, starting transfers between devices, chips_along(): return lax.ppermute(x, 'tcol', [(i, (i + s) % n_col) for i in range(n_col)])  6.23 us
    pallas_call x1, Pallas kernels, get_ready(): pl.pallas_call(functools.partial(ready_kernel, first, depth, count), in_s...  3.84 us
    ppermute x1, starting transfers between devices, on_device(): lax.ppermute(tail, 'seq', [(i, (i + 1) % n_seq) for i in range(n_seq)])  2.7 us
    pallas_call x1, Pallas kernels, scale_far(): pl.pallas_call(functools.partial(scaled_kernel, first, n), in_specs=[SCAL...  2.3 us
  transfers between devices with their start and end apart: 12, of which 4 were waited for; matrix products, arithmetic and copies ran while one was open for 0% of the time, Pallas kernels for 46%

profile of v9, /device:TPU:0, one launch (start us, length us, event | category | flops | bytes accessed | tf_op | source)
XLA Modules:
  0.0 82.2 jit_solution(5240604150550702632)
XLA Ops:
  0.5 2.5 %collective-permute-start = (bf16[512,1024]{1,0:T(8,128)(2,1)}, bf16[512,1024]{1,0:T(8,128)(2,1)}, u32[]{:S(2)}, u32[]{:S(2)}) collective-permute-start(bf16[512,1024]{1,0:T(8,128)(2,1)} %own_ref.1), channel_id=1, source_target_pairs={{0,1},{1,0},{2,3},{3,2},{4,5},{5,4},{6,7},{7,6},{8,9},{9,8},{10,11... | collective-permute-start | bytes 3145736 | tf_op jit(solution)/shard_map/ppermute | solution.py:474
  3.1 1.0 %copy-done = bf16[512,1024]{1,0:T(8,128)(2,1)} copy-done((bf16[512,1024]{1,0:T(8,128)(2,1)}, bf16[512,1024]{1,0:T(8,128)(2,1)S(1)}, u32[]{:S(2)}) %copy-start) | copy-done | bytes 1048600
  4.0 1.2 %copy-done.1 = bf16[512,1024]{1,0:T(8,128)(2,1)S(1)} copy-done((bf16[512,1024]{1,0:T(8,128)(2,1)S(1)}, bf16[512,1024]{1,0:T(8,128)(2,1)}, u32[]{:S(2)}) %copy-start.1) | copy-done | bytes 1048600
  5.3 17.7 %project_local.1 = (bf16[3,512,2048]{2,1,0:T(8,128)(2,1)S(1)}, f32[512,128]{1,0:T(8,128)S(1)}, bf16[2048,4096]{1,0:T(8,128)(2,1)S(1)}) custom-call(s32[9]{0:T(128)S(1)} %stack.33.places, bf16[512,1024]{1,0:T(8,128)(2,1)} %own_ref.1, bf16[512,1024]{1,0:T(8,128)(2,1)S(1)} %copy-done.1, f32[4,1,1024]{2,1,0:T(1,128)} %bitcast.14, ...), custom_call_target="tpu_custom_call" | custom-call | flops 12884901888 | bytes 27262976 | tf_op jit(solution)/shard_map/project_local/pallas_call | solution.py:289
  23.0 3.8 %get_ready.1 = (f32[384,2048]{1,0:T(8,128)S(1)}, bf16[3,3,2048,256]{3,2,1,0:T(8,128)(2,1)S(1)}) custom-call(s32[9]{0:T(128)S(1)} %stack.33.places, f32[128,2048]{1,0:T(8,128)} %taps_ref.1, f32[1,2048]{1,0:T(1,128)S(1)} %bitcast.13, bf16[384,256]{1,0:T(8,128)(2,1)S(1)} %copy-done.4, bf16[3,4096,2048]{2,1,0:T(8,128)(2,1)} %refs_2_.1, ...), custom_call_target="tpu_custom_call" | custom-call | flops 1 | bytes 1 | tf_op jit(solution)/shard_map/get_ready/pallas_call | solution.py:314
  27.2 2.3 %scale_far.1 = (bf16[512,2048]{1,0:T(8,128)(2,1)S(1)}, f32[512,128]{1,0:T(8,128)S(1)}, bf16[3,512,256]{2,1,0:T(8,128)(2,1)S(1)}) custom-call(s32[9]{0:T(128)S(1)} %stack.33.places, bf16[512,1024]{1,0:T(8,128)(2,1)} %held_until.1.refs_0_, f32[4,1,1024]{2,1,0:T(1,128)} %bitcast.15, f32[512,128]{1,0:T(8,128)S(1)} %get-tuple-element.23._.refs_2_, ...), custom_call_target="tpu_custom_call" | custom-call | flops 1 | bytes 1 | tf_op jit(solution)/shard_map/scale_far/pallas_call | solution.py:332
  29.5 0.5 collective-permute-done.2.refs_0_
  30.0 18.0 %project_rest.1 = (bf16[128,2048]{1,0:T(8,128)(2,1)S(1)}, bf16[128,2048]{1,0:T(8,128)(2,1)S(1)}, bf16[128,2048]{1,0:T(8,128)(2,1)S(1)}, bf16[384,2048]{1,0:T(8,1...) custom-call(s32[9]{0:T(128)S(1)} %stack.33.places, ...), custom_call_target="tpu_custom_call", output_to_operand_aliasing={{4}: (10, {}), {5}: (11, {})} | custom-call | flops 12884901888 | bytes 27262976 | tf_op jit(solution)/shard_map/project_rest/pallas_call | solution.py:352
  48.0 2.3 %rest_theirs_far.1 = bf16[1,384,1024]{2,1,0:T(8,128)(2,1)S(1)} custom-call(s32[9]{0:T(128)S(1)} %stack.33.places, bf16[384,2048]{1,0:T(8,128)(2,1)S(1)} %get-tuple-element.34.refs_0_, bf16[2048,4096]{1,0:T(8,128)(2,1)S(1)} %get-tuple-element.33.refs_1_.w_ref), custom_call_target="tpu_custom_call" | custom-call | flops 1 | bytes 1 | tf_op jit(solution)/shard_map/rest_theirs_far/pallas_call | solution.py:420
  50.6 2.7 %collective-permute-start.3 = (bf16[128,2048]{1,0:T(8,128)(2,1)S(1)}, bf16[128,2048]{1,0:T(8,128)(2,1)S(1)}, u32[]{:S(2)}, u32[]{:S(2)}) collective-permute-start(bf16[128,2048]{1,0:T(8,128)(2,1)S(1)} %get-tuple-element.30), channel_id=1, source_target_pairs={{0,4},{4,8},{8,12},{12,16},{16,20},{20,24},{24,28},{28,0},{1,5},{5... | collective-permute-start | bytes 1572872 | tf_op jit(solution)/shard_map/ppermute | solution.py:502
  53.3 2.4 %rest_mine_far.1.refs_2_ = bf16[1,384,1024]{2,1,0:T(8,128)(2,1)S(1)} custom-call(s32[9]{0:T(128)S(1)} %stack.33.places, bf16[384,2048]{1,0:T(8,128)(2,1)S(1)} %get-tuple-element.34.refs_0_, bf16[2048,4096]{1,0:T(8,128)(2,1)S(1)} %get-tuple-element.33.refs_1_.w_ref, bf16[1,384,1024]{2,1,0:T(8,128)(2,1)S(1)} %collective-permute-done.4.refs_2_), custom_call_target="tpu_custom_call" | custom-call | flops 1 | bytes 1 | tf_op jit(solution)/shard_map/rest_mine_far/pallas_call | solution.py:420
  55.6 2.1 %collective-permute-start.11 = (bf16[384,1024]{1,0:T(8,128)(2,1)S(1)}, bf16[384,1024]{1,0:T(8,128)(2,1)S(1)}, u32[]{:S(2)}, u32[]{:S(2)}) collective-permute-start(bf16[384,1024]{1,0:T(8,128)(2,1)S(1)} %bitcast.11), channel_id=1, source_target_pairs={{0,1},{1,0},{2,3},{3,2},{4,5},{5,4},{6,7},{7,6},{8,9},{9,8},{10,11... | collective-permute-start | bytes 2359304 | tf_op jit(solution)/shard_map/ppermute | solution.py:474
  57.8 2.3 %rest_theirs_near.1 = (bf16[1,384,512]{2,1,0:T(8,128)(2,1)S(1)}, bf16[1,384,512]{2,1,0:T(8,128)(2,1)S(1)}) custom-call(s32[9]{0:T(128)S(1)} %stack.33.places, bf16[384,2048]{1,0:T(8,128)(2,1)S(1)} %get-tuple-element.34.refs_0_, bf16[2048,4096]{1,0:T(8,128)(2,1)S(1)} %get-tuple-element.33.refs_1_.w_ref, bf16[1,384,1024]{2,1,0:T(8,128)(2,1)S(1)} %rest_mine_far.1.refs_2_), custom_call_target="tpu_custom_call" | custom-call | flops 1 | bytes 1 | tf_op jit(solution)/shard_map/rest_theirs_near/pallas_call | solution.py:420
  60.2 8.5 %collective-permute-done.3.halo_ref = bf16[128,2048]{1,0:T(8,128)(2,1)S(1)} collective-permute-done((bf16[128,2048]{1,0:T(8,128)(2,1)S(1)}, bf16[128,2048]{1,0:T(8,128)(2,1)S(1)}, u32[]{:S(2)}, u32[]{:S(2)}) %collective-permute-start.3) | collective-permute-done | bytes 524320 | tf_op jit(solution)/shard_map/ppermute | solution.py:502
  68.7 2.0 %gate_first.1 = (bf16[128,2048]{1,0:T(8,128)(2,1)S(1)}, bf16[1,128,1024]{2,1,0:T(8,128)(2,1)S(1)}) custom-call(s32[9]{0:T(128)S(1)} %stack.33.places, bf16[128,2048]{1,0:T(8,128)(2,1)S(1)} %collective-permute-done.3.halo_ref, bf16[128,2048]{1,0:T(8,128)(2,1)S(1)} %get-tuple-element.31.mixed_ref, bf16[128,2048]{1,0:T(8,128)(2,1)S(1)} %get-tuple-element.32.q_ref, ...), custom_call_target="tpu_custom_call" | custom-call | flops 1 | bytes 1 | tf_op jit(solution)/shard_map/gate_first/pallas_call | solution.py:376
  70.8 0.5 collective-permute-start.10
  71.3 1.3 %first_mine_far.1.a_ref = f32[1,128,1024]{2,1,0:T(8,128)S(1)} custom-call(s32[9]{0:T(128)S(1)} %stack.33.places, bf16[128,2048]{1,0:T(8,128)(2,1)S(1)} %get-tuple-element.37.refs_0_, bf16[2048,4096]{1,0:T(8,128)(2,1)S(1)} %get-tuple-element.33.refs_1_.w_ref), custom_call_target="tpu_custom_call" | custom-call | flops 1 | bytes 1 | tf_op jit(solution)/shard_map/first_mine_far/pallas_call | solution.py:420
  72.6 1.6 %collective-permute-start.8 = (bf16[128,1024]{1,0:T(8,128)(2,1)S(1)}, bf16[128,1024]{1,0:T(8,128)(2,1)S(1)}, u32[]{:S(2)}, u32[]{:S(2)}) collective-permute-start(bf16[128,1024]{1,0:T(8,128)(2,1)S(1)} %bitcast.12), channel_id=1, source_target_pairs={{0,1},{1,0},{2,3},{3,2},{4,5},{5,4},{6,7},{7,6},{8,9},{9,8},{10,11... | collective-permute-start | bytes 786440 | tf_op jit(solution)/shard_map/ppermute | solution.py:474
  74.2 1.3 %first_theirs_near.1 = (bf16[1,128,512]{2,1,0:T(8,128)(2,1)S(1)}, bf16[1,128,512]{2,1,0:T(8,128)(2,1)S(1)}) custom-call(s32[9]{0:T(128)S(1)} %stack.33.places, bf16[128,2048]{1,0:T(8,128)(2,1)S(1)} %get-tuple-element.37.refs_0_, bf16[2048,4096]{1,0:T(8,128)(2,1)S(1)} %get-tuple-element.33.refs_1_.w_ref, bf16[1,128,1024]{2,1,0:T(8,128)(2,1)S(1)} %added.1.refs_2_), custom_call_target="tpu_custom_call" | custom-call | flops 1 | bytes 1 | tf_op jit(solution)/shard_map/first_theirs_near/pallas_call | solution.py:420
  75.6 0.5 collective-permute-start.7
  76.1 2.3 %rest_mine_near.1.refs_0_ = f32[1,384,1024]{2,1,0:T(8,128)S(1)} custom-call(s32[9]{0:T(128)S(1)} %stack.33.places, bf16[384,2048]{1,0:T(8,128)(2,1)S(1)} %get-tuple-element.34.refs_0_, bf16[2048,4096]{1,0:T(8,128)(2,1)S(1)} %get-tuple-element.33.refs_1_.w_ref, bf16[1,384,512]{2,1,0:T(8,128)(2,1)S(1)} %collective-permute-done.9.refs_2_, ...), custom_call_target="tpu_custom_call" | custom-call | flops 1 | bytes 1 | tf_op jit(solution)/shard_map/rest_mine_near/pallas_call | solution.py:420
  78.4 1.3 %first_mine_near.1.refs_0_ = f32[1,128,1024]{2,1,0:T(8,128)S(1)} custom-call(s32[9]{0:T(128)S(1)} %stack.33.places, bf16[128,2048]{1,0:T(8,128)(2,1)S(1)} %get-tuple-element.37.refs_0_, bf16[2048,4096]{1,0:T(8,128)(2,1)S(1)} %get-tuple-element.33.refs_1_.w_ref, bf16[1,128,512]{2,1,0:T(8,128)(2,1)S(1)} %collective-permute-done.6.refs_2_, ...), custom_call_target="tpu_custom_call" | custom-call | flops 1 | bytes 1 | tf_op jit(solution)/shard_map/first_mine_near/pallas_call | solution.py:420
  79.8 1.0 %total_rows.2.refs_2_ = bf16[512,1024]{1,0:T(8,128)(2,1)} custom-call(f32[1,384,1024]{2,1,0:T(8,128)S(1)} %rest_mine_near.1.refs_0_, bf16[384,1024]{1,0:T(8,128)(2,1)S(1)} %collective-permute-done.11.refs_1_), custom_call_target="tpu_custom_call" | custom-call | flops 1 | bytes 1 | tf_op jit(solution)/shard_map/total_rows/pallas_call | solution.py:448
  81.2 0.8 total_rows.3
  (29 shorter events, 1.9 us)
Async XLA Ops:
  0.0 3.1 %collective-permute-start.1 = (bf16[512,1024]{1,0:T(8,128)(2,1)}, bf16[512,1024]{1,0:T(8,128)(2,1)S(1)}, u32[]{:S(2)}, u32[]{:S(2)}) collective-permute-start(bf16[512,1024]{1,0:T(8,128)(2,1)} %own_ref.1), channel_id=1, source_target_pairs={{0,2},{2,0},{1,3},{3,1},{4,6},{6,4},{5,7},{7,5},{8,10},{10,8},{9,1... | collective-permute-start | bytes 3145736 | tf_op jit(solution)/shard_map/ppermute | solution.py:471
  0.5 26.7 %collective-permute-start = (bf16[512,1024]{1,0:T(8,128)(2,1)}, bf16[512,1024]{1,0:T(8,128)(2,1)}, u32[]{:S(2)}, u32[]{:S(2)}) collective-permute-start(bf16[512,1024]{1,0:T(8,128)(2,1)} %own_ref.1), channel_id=1, source_target_pairs={{0,1},{1,0},{2,3},{3,2},{4,5},{5,4},{6,7},{7,6},{8,9},{9,8},{10,11... | collective-permute-start | bytes 3145736 | tf_op jit(solution)/shard_map/ppermute | solution.py:474
  3.1 1.0 %copy-start = (bf16[512,1024]{1,0:T(8,128)(2,1)}, bf16[512,1024]{1,0:T(8,128)(2,1)S(1)}, u32[]{:S(2)}) copy-start(bf16[512,1024]{1,0:T(8,128)(2,1)S(1)} %collective-permute-done.1.beside_ref) | copy-start | bytes 3145732
  4.0 1.2 %copy-start.1 = (bf16[512,1024]{1,0:T(8,128)(2,1)S(1)}, bf16[512,1024]{1,0:T(8,128)(2,1)}, u32[]{:S(2)}) copy-start(bf16[512,1024]{1,0:T(8,128)(2,1)} %copy-done) | copy-start | bytes 3145732
  5.3 17.7 %copy-start.4 = (bf16[384,256]{1,0:T(8,128)(2,1)S(1)}, bf16[384,256]{1,0:T(8,128)(2,1)}, u32[]{:S(2)}) copy-start(bf16[384,256]{1,0:T(8,128)(2,1)} %constant.35.clone.of_filter_ref) | copy-start | bytes 589828
  5.3 17.7 %copy-start.5 = (f32[2048]{0:T(1024)S(1)}, f32[2048]{0:T(1024)}, u32[]{:S(2)}) copy-start(f32[2048]{0:T(1024)} %param.13) | copy-start | bytes 24580
  27.1 2.9 %copy-start.2 = (bf16[256,256]{1,0:T(8,128)(2,1)S(1)}, bf16[256,256]{1,0:T(8,128)(2,1)}, u32[]{:S(2)}) copy-start(bf16[256,256]{1,0:T(8,128)(2,1)} %constant.33.clone.refs_7_.fwd_ref) | copy-start | bytes 393220
  27.1 2.9 %copy-start.3 = (bf16[128,256]{1,0:T(8,128)(2,1)S(1)}, bf16[128,256]{1,0:T(8,128)(2,1)}, u32[]{:S(2)}) copy-start(bf16[128,256]{1,0:T(8,128)(2,1)} %constant.34.clone.refs_8_.inv_ref) | copy-start | bytes 196612
  27.1 2.9 %collective-permute-start.2 = (bf16[512,1024]{1,0:T(8,128)(2,1)}, bf16[512,1024]{1,0:T(8,128)(2,1)S(1)}, u32[]{:S(2)}, u32[]{:S(2)}) collective-permute-start(bf16[512,1024]{1,0:T(8,128)(2,1)} %held_until.1.refs_0_), channel_id=1, source_target_pairs={{0,2},{2,0},{1,3},{3,1},{4,6},{6,4},{5,7},{7,5},{8,10},{10,8},{9,1... | collective-permute-start | bytes 3145736 | tf_op jit(solution)/shard_map/ppermute | solution.py:471
  50.4 2.9 %collective-permute-start.4 = (bf16[1,384,1024]{2,1,0:T(8,128)(2,1)S(1)}, bf16[1,384,1024]{2,1,0:T(8,128)(2,1)S(1)}, u32[]{:S(2)}, u32[]{:S(2)}) collective-permute-start(bf16[1,384,1024]{2,1,0:T(8,128)(2,1)S(1)} %rest_theirs_far.1), channel_id=1, source_target_pairs={{0,2},{2,0},{1,3},{3,1},{4,6},{6,4},{5,7},{7,5},{8,10},{10,8},{9,1... | collective-permute-start | bytes 2359304 | tf_op jit(solution)/shard_map/ppermute | solution.py:471
  50.6 18.1 %collective-permute-start.3 = (bf16[128,2048]{1,0:T(8,128)(2,1)S(1)}, bf16[128,2048]{1,0:T(8,128)(2,1)S(1)}, u32[]{:S(2)}, u32[]{:S(2)}) collective-permute-start(bf16[128,2048]{1,0:T(8,128)(2,1)S(1)} %get-tuple-element.30), channel_id=1, source_target_pairs={{0,4},{4,8},{8,12},{12,16},{16,20},{20,24},{24,28},{28,0},{1,5},{5... | collective-permute-start | bytes 1572872 | tf_op jit(solution)/shard_map/ppermute | solution.py:502
  55.6 24.1 %collective-permute-start.11 = (bf16[384,1024]{1,0:T(8,128)(2,1)S(1)}, bf16[384,1024]{1,0:T(8,128)(2,1)S(1)}, u32[]{:S(2)}, u32[]{:S(2)}) collective-permute-start(bf16[384,1024]{1,0:T(8,128)(2,1)S(1)} %bitcast.11), channel_id=1, source_target_pairs={{0,1},{1,0},{2,3},{3,2},{4,5},{5,4},{6,7},{7,6},{8,9},{9,8},{10,11... | collective-permute-start | bytes 2359304 | tf_op jit(solution)/shard_map/ppermute | solution.py:474
  60.1 15.4 %collective-permute-start.9 = (bf16[1,384,512]{2,1,0:T(8,128)(2,1)S(1)}, bf16[1,384,512]{2,1,0:T(8,128)(2,1)S(1)}, u32[]{:S(2)}, u32[]{:S(2)}) collective-permute-start(bf16[1,384,512]{2,1,0:T(8,128)(2,1)S(1)} %get-tuple-element.35.refs_0_), channel_id=1, source_target_pairs={{0,2},{2,0},{1,3},{3,1},{4,6},{6,4},{5,7},{7,5},{8,10},{10,8},{9,1... | collective-permute-start | bytes 1179656 | tf_op jit(solution)/shard_map/ppermute | solution.py:471
  70.7 1.9 %collective-permute-start.5 = (bf16[1,128,1024]{2,1,0:T(8,128)(2,1)S(1)}, bf16[1,128,1024]{2,1,0:T(8,128)(2,1)S(1)}, u32[]{:S(2)}, u32[]{:S(2)}) collective-permute-start(bf16[1,128,1024]{2,1,0:T(8,128)(2,1)S(1)} %get-tuple-element.38), channel_id=1, source_target_pairs={{0,2},{2,0},{1,3},{3,1},{4,6},{6,4},{5,7},{7,5},{8,10},{10,8},{9,1... | collective-permute-start | bytes 786440 | tf_op jit(solution)/shard_map/ppermute | solution.py:471
  70.8 5.3 %collective-permute-start.10 = (bf16[1,384,512]{2,1,0:T(8,128)(2,1)S(1)}, bf16[1,384,512]{2,1,0:T(8,128)(2,1)S(1)}, u32[]{:S(2)}, u32[]{:S(2)}) collective-permute-start(bf16[1,384,512]{2,1,0:T(8,128)(2,1)S(1)} %get-tuple-element.36.refs_1_), channel_id=1, source_target_pairs={{0,2},{2,0},{1,3},{3,1},{4,6},{6,4},{5,7},{7,5},{8,10},{10,8},{9,1... | collective-permute-start | bytes 1179656 | tf_op jit(solution)/shard_map/ppermute | solution.py:471
  72.6 8.6 %collective-permute-start.8 = (bf16[128,1024]{1,0:T(8,128)(2,1)S(1)}, bf16[128,1024]{1,0:T(8,128)(2,1)S(1)}, u32[]{:S(2)}, u32[]{:S(2)}) collective-permute-start(bf16[128,1024]{1,0:T(8,128)(2,1)S(1)} %bitcast.12), channel_id=1, source_target_pairs={{0,1},{1,0},{2,3},{3,2},{4,5},{5,4},{6,7},{7,6},{8,9},{9,8},{10,11... | collective-permute-start | bytes 786440 | tf_op jit(solution)/shard_map/ppermute | solution.py:474
  75.5 2.9 %collective-permute-start.6 = (bf16[1,128,512]{2,1,0:T(8,128)(2,1)S(1)}, bf16[1,128,512]{2,1,0:T(8,128)(2,1)S(1)}, u32[]{:S(2)}, u32[]{:S(2)}) collective-permute-start(bf16[1,128,512]{2,1,0:T(8,128)(2,1)S(1)} %get-tuple-element.39), channel_id=1, source_target_pairs={{0,2},{2,0},{1,3},{3,1},{4,6},{6,4},{5,7},{7,5},{8,10},{10,8},{9,1... | collective-permute-start | bytes 393224 | tf_op jit(solution)/shard_map/ppermute | solution.py:471
  75.6 2.9 %collective-permute-start.7 = (bf16[1,128,512]{2,1,0:T(8,128)(2,1)S(1)}, bf16[1,128,512]{2,1,0:T(8,128)(2,1)S(1)}, u32[]{:S(2)}, u32[]{:S(2)}) collective-permute-start(bf16[1,128,512]{2,1,0:T(8,128)(2,1)S(1)} %get-tuple-element.40), channel_id=1, source_target_pairs={{0,2},{2,0},{1,3},{3,1},{4,6},{6,4},{5,7},{7,5},{8,10},{10,8},{9,1... | collective-permute-start | bytes 393224 | tf_op jit(solution)/shard_map/ppermute | solution.py:471
